TPU v7x, 256 devices: a whole 4x4x8 slice. The times are simulated.
256 devices in a mesh: pool: 2 (over x_hi), group: 8 (over y, core), tp: 16 (over z, x_lo).
Axes of the slice: x: 4 (x_hi: 2, x_lo: 2; x = x_hi * 2 + x_lo), y: 4, z: 8, core: 2. Of those that a mesh axis runs over, the one named last changes fastest.
Arguments:
- cache: bfloat16 [2, 8, 64, 128, 16, 256], P('pool', 'group', None, None, 'tp'), may hold values from -6 to 6
- table: int32 [2, 8, 64], P('pool', 'group'), may hold values from 0 to 63, each once within a row
- lengths: int32 [2, 8, 16], P('pool', 'group'), may hold values from 1 to 512, 4096 in all within a row
- query: bfloat16 [2, 8, 16, 4096], P('pool', 'group', None, 'tp'), may hold values from -6 to 6
- step_kv: bfloat16 [2, 8, 16, 16, 256], P('pool', 'group', None, 'tp'), may hold values from -6 to 6
- resid: bfloat16 [2, 8, 16, 5120], P('pool', 'group'), may hold values from -3 to 3
- new_cache: bfloat16 [2, 8, 16, 256, 16, 256], P('pool', 'group', None, None, 'tp'), may hold values from -6 to 6
- new_lengths: int32 [2, 8, 16], P('pool', 'group'), may hold values from 1 to 255, 2048 in all within a row
- new_query: bfloat16 [2, 8, 16, 4096], P('pool', 'group', None, 'tp'), may hold values from -6 to 6
- new_step_kv: bfloat16 [2, 8, 16, 16, 256], P('pool', 'group', None, 'tp'), may hold values from -6 to 6
- new_resid: bfloat16 [2, 8, 16, 5120], P('pool', 'group'), may hold values from -3 to 3
- pairing: int32 [2, 8, 16, 1], P('pool', 'group'), may hold values from 0 to 15; in each aligned block of 16 rows (0 to 15, 16 to 31, ..., all dimensions but the last counted through in order) at most 2 rows name the same one
- o_weight: bfloat16 [4096, 5120], P('tp'), may hold values from -2 to 2
- norm_gain: bfloat16 [5120], replicated, may hold values from 0.099609375 to 1.8984375
Outputs:
- hidden: bfloat16 [2, 8, 48, 5120], P('pool', 'group')
- normed: bfloat16 [2, 8, 48, 5120], P('pool', 'group')
- slot_cache: bfloat16 [2, 8, 32, 256, 16, 256], P('pool', 'group', None, None, 'tp')
Inputs may be any that keep to these rules, and one draw needn't show every extreme that they name: `table`: each group's block ids, each once; request r owns entries r * 4 to r * 4 + 3. `lengths`: some request of each group fills all its 4 blocks. `new_lengths`: some request of each group has the longest prompt, leaving one free position. `pairing`: a group index pool * number of groups + group; no group sends more than 2 requests to one destination, and in some groups exactly 2.
All inputs are finite; a program needn't handle non-finite values.
Results may differ from a plain program's by a relative error of at most 0.0059.
Values may be sent and summed in bfloat16 or wider, within the bound.
No kernel may reach another device: no remote copies, remote signals or barrier semaphores. Data moves between devices by JAX's collectives and lax.ppermute only.
A program may use at most 64 MiB of HBM per device.

v0:
```python
import math

import jax
import jax.numpy as jnp
from jax import lax
from jax.sharding import PartitionSpec as P


def attend(query_rows, kv_rows, own_kv, length):
    row_count, tokens, kv_heads, pair_width = kv_rows.shape
    head_dim = pair_width // 2
    grouped = query_rows.reshape(row_count, kv_heads, -1, head_dim)
    key_part = kv_rows[..., :head_dim]
    value_part = kv_rows[..., head_dim:]
    scaling = 1.0 / math.sqrt(head_dim)
    scores = (
        jnp.einsum("rcgd,rtcd->rcgt", grouped, key_part, preferred_element_type=jnp.float32)
        * scaling
    )
    own_score = (
        jnp.einsum(
            "rcgd,rcd->rcg", grouped, own_kv[..., :head_dim], preferred_element_type=jnp.float32
        )
        * scaling
    )
    position = jnp.arange(tokens, dtype=jnp.int32)
    visible = (position[None, :] < length[:, None])[:, None, None, :]
    highest = jnp.maximum(jnp.max(jnp.where(visible, scores, -1e30), axis=-1), own_score)
    exponent = jnp.where(visible, jnp.exp(scores - highest[..., None]), 0.0)
    own_exponent = jnp.exp(own_score - highest)
    denominator = jnp.sum(exponent, axis=-1) + own_exponent
    weights = (exponent / denominator[..., None]).astype(jnp.bfloat16)
    own_weight = (own_exponent / denominator).astype(jnp.bfloat16)
    blended = jnp.einsum("rcgt,rtcd->rcgd", weights, value_part, preferred_element_type=jnp.float32)
    own_value = own_kv[..., head_dim:].astype(jnp.float32)
    blended = blended + own_weight.astype(jnp.float32)[..., None] * own_value[:, :, None, :]
    return blended.astype(jnp.bfloat16).reshape(row_count, -1)


def append_token(kv_rows, own_kv, length):
    position = jnp.arange(kv_rows.shape[1], dtype=jnp.int32)
    place_here = (position[None, :] == length[:, None])[:, :, None, None]
    return jnp.where(place_here, own_kv[:, None], kv_rows)


def finish(resid_rows, projected, norm_gain):
    hidden = (resid_rows.astype(jnp.float32) + projected).astype(jnp.bfloat16)
    widened = lax.optimization_barrier(hidden).astype(jnp.float32)
    inverse = lax.rsqrt(jnp.mean(widened * widened, axis=-1, keepdims=True) + 1e-06)
    normed = (widened * inverse * norm_gain.astype(jnp.float32)).astype(jnp.bfloat16)
    return (hidden, normed)


def serve_slots(incoming):
    kv_in, query_in, own_in, resid_in, length_in = incoming
    sources = length_in.shape[0]
    items = length_in.shape[1]

    def flatten_items(array):
        return array.reshape((sources * items,) + array.shape[2:])

    kv_flat = flatten_items(kv_in)
    own_flat = flatten_items(own_in)
    length_flat = flatten_items(length_in)
    attended = attend(flatten_items(query_in), kv_flat, own_flat, length_flat)
    appended = append_token(kv_flat, own_flat, length_flat)
    return (
        attended.reshape((sources, items) + attended.shape[1:]),
        appended.reshape((sources, items) + appended.shape[1:]),
        resid_in,
    )


def body(
    cache,
    table,
    lengths,
    query,
    step_kv,
    resid,
    new_cache,
    new_lengths,
    new_query,
    new_step_kv,
    new_resid,
    pairing,
    o_weight,
    norm_gain,
):
    requests = lengths.shape[2]
    gathered = cache[0, 0][table[0, 0]]
    gathered = gathered.reshape(requests, -1, gathered.shape[2], gathered.shape[3])
    resident = attend(query[0, 0], gathered, step_kv[0, 0], lengths[0, 0])
    pools = lax.axis_size("pool")
    groups = pools * lax.axis_size("group")
    fresh_count = new_lengths.shape[2]
    capacity = max(2, 2 * fresh_count // groups)
    target_group = pairing[0, 0, :, 0]
    position = jnp.arange(fresh_count, dtype=jnp.int32)
    matches = (target_group[:, None] == target_group[None, :]) & (
        position[None, :] < position[:, None]
    )
    target = target_group * capacity + jnp.sum(matches.astype(jnp.int32), axis=1)

    def to_slots(payload):
        blank_slots = jnp.zeros((groups * capacity,) + payload.shape[1:], payload.dtype)
        return blank_slots.at[target].set(payload).reshape((groups, capacity) + payload.shape[1:])

    send_cache = to_slots(new_cache[0, 0])
    send_query = to_slots(new_query[0, 0])
    send_own = to_slots(new_step_kv[0, 0])
    send_resid = to_slots(new_resid[0, 0])
    send_length = to_slots(new_lengths[0, 0])
    slot_results = serve_slots(
        (
            lax.all_to_all(send_cache, ("pool", "group"), split_axis=0, concat_axis=0, tiled=True),
            lax.all_to_all(send_query, ("pool", "group"), split_axis=0, concat_axis=0, tiled=True),
            lax.all_to_all(send_own, ("pool", "group"), split_axis=0, concat_axis=0, tiled=True),
            lax.all_to_all(send_resid, ("pool", "group"), split_axis=0, concat_axis=0, tiled=True),
            lax.all_to_all(send_length, ("pool", "group"), split_axis=0, concat_axis=0, tiled=True),
        )
    )
    attended_new, appended, resid_new = slot_results
    attended_all = jnp.concatenate(
        [resident, attended_new.reshape(-1, attended_new.shape[-1])], axis=0
    )
    resid_all = jnp.concatenate([resid[0, 0], resid_new.reshape(-1, resid_new.shape[-1])], axis=0)
    slot_cache = appended.reshape((-1,) + appended.shape[2:])
    partial_terms = jnp.dot(attended_all, o_weight, preferred_element_type=jnp.float32)
    projected = lax.psum(partial_terms, "tp")
    hidden, normed = finish(resid_all, projected, norm_gain)
    return (hidden[None, None], normed[None, None], slot_cache[None, None])


def solution(mesh):
    placed = (
        P("pool", "group", None, None, "tp", None),
        P("pool", "group", None),
        P("pool", "group", None),
        P("pool", "group", None, "tp"),
        P("pool", "group", None, "tp", None),
        P("pool", "group", None, None),
        P("pool", "group", None, None, "tp", None),
        P("pool", "group", None),
        P("pool", "group", None, "tp"),
        P("pool", "group", None, "tp", None),
        P("pool", "group", None, None),
        P("pool", "group", None, None),
        P("tp", None),
        P(),
    )
    return jax.shard_map(
        body,
        mesh=mesh,
        in_specs=placed,
        out_specs=(
            P("pool", "group", None, None),
            P("pool", "group", None, None),
            P("pool", "group", None, None, "tp", None),
        ),
        check_vma=False,
    )
```

profile of v0, /device:TPU:8, one launch (start us, length us, event | category | flops | bytes accessed | tf_op | source)
XLA Modules:
  0.0 274.2 jit_solution(17321620596721001410)
XLA Ops:
  7.2 0.0 copy-start
  7.2 1.0 convert_reduce_fusion
  8.2 0.7 fusion.43
  8.8 0.8 scatter_custom_fusion.1
  9.6 0.7 all_to_all.19
  10.3 7.4 %all-to-all-start.1 = ((s32[16,1,2]{2,1,0:T(1,128)}), s32[16,1,2]{2,1,0:T(1,128)S(1)}, u32[]{:S(2)}, u32[]{:S(2)}) async-start(s32[16,1,2]{2,1,0:T(1,128)} %bitcast.21), calls=%async_computation.1 | async-start | bytes 16384 | tf_op jit(solution)/shard_map/all_to_all | solution.py:120
  17.7 0.8 scatter_custom_fusion.4
  18.5 0.6 reshape.327
  19.1 4.7 %all-to-all-done.1 = s32[16,1,2]{2,1,0:T(1,128)S(1)} async-done(((s32[16,1,2]{2,1,0:T(1,128)}), s32[16,1,2]{2,1,0:T(1,128)S(1)}, u32[]{:S(2)}, u32[]{:S(2)}) %all-to-all-start.1) | async-done | bytes 160 | tf_op jit(solution)/shard_map/all_to_all | solution.py:120
  23.8 4.8 %all-to-all-start.4 = ((bf16[16,2,1,256]{3,1,2,0:T(2,128)(2,1)}), bf16[16,2,1,256]{3,1,2,0:T(2,128)(2,1)S(1)}, u32[]{:S(2)}, u32[]{:S(2)}) async-start(bf16[16,2,1,256]{3,1,2,0:T(2,128)(2,1)} %reshape.327), calls=%async_computation.4 | async-start | bytes 32768 | tf_op jit(solution)/shard_map/all_to_all | solution.py:118
  28.6 0.8 scatter_custom_fusion.2
  29.4 0.6 reshape.322
  30.0 4.9 %all-to-all-done.4 = bf16[16,2,1,256]{3,1,2,0:T(2,128)(2,1)S(1)} async-done(((bf16[16,2,1,256]{3,1,2,0:T(2,128)(2,1)}), bf16[16,2,1,256]{3,1,2,0:T(2,128)(2,1)S(1)}, u32[]{:S(2)}, u32[]{:S(2)}) %all-to-all-start.4) | async-done | bytes 16416 | tf_op jit(solution)/shard_map/all_to_all | solution.py:118
  34.9 4.7 %all-to-all-start.2 = ((bf16[16,2,256]{2,1,0:T(2,128)(2,1)}), bf16[16,2,256]{2,1,0:T(2,128)(2,1)S(1)}, u32[]{:S(2)}, u32[]{:S(2)}) async-start(bf16[16,2,256]{2,1,0:T(2,128)(2,1)} %reshape.322), calls=%async_computation.2 | async-start | bytes 32768 | tf_op jit(solution)/shard_map/all_to_all | solution.py:117
  39.6 2.5 broadcast.155
  42.1 5.9 %scatter_fusion = bf16[32,256,256]{2,1,0:T(8,128)(2,1)} fusion(bf16[32,256,256]{2,1,0:T(8,128)(2,1)} %broadcast.155, s32[16]{0:T(128)S(1)} %fusion.43, bf16[16,256,256]{2,1,0:T(8,128)(2,1)} %bitcast.121), kind=kCustom, calls=%fused_computation.4 | custom fusion | bytes 6291520 | tf_op jit(solution)/shard_map/scatter | solution.py:107
  48.0 0.0 all-to-all-done.2
  48.0 0.0 copy-start.5
  48.0 0.0 copy-start.8
  48.0 7.4 %all-to-all-start.3 = ((bf16[16,2,256,1,256]{4,2,1,3,0:T(8,128)(2,1)}), bf16[16,2,256,1,256]{4,2,1,3,0:T(8,128)(2,1)}, u32[]{:S(2)}, u32[]{:S(2)}) async-start(bf16[16,2,256,1,256]{4,2,1,3,0:T(8,128)(2,1)} %bitcast.116), calls=%async_computation.3 | async-start | bytes 8388608 | tf_op jit(solution)/shard_map/all_to_all | solution.py:116
  55.4 0.0 all-reduce.2.cloned.1.call-start
  55.5 0.0 copy-done.5
  55.5 0.0 copy-done.8
  55.5 0.0 copy-start.7
  55.5 0.0 copy-start.6
  55.5 5.0 %gather_fusion = bf16[64,128,256]{2,1,0:T(8,128)(2,1)} fusion(bf16[64,128,256]{2,1,0:T(8,128)(2,1)} %bitcast.118, s32[1024]{0:T(1024)S(1)} %pad_clamp_fusion), kind=kCustom, calls=%fused_computation | custom fusion | bytes 8388864 | tf_op jit(solution)/shard_map/gather | solution.py:91
  60.5 0.0 copy-done.7
  60.5 0.1 iota_compare_fusion.2
  60.6 0.0 copy-done.6
  60.6 0.1 fusion.36
  60.7 2.3 select_reduce_fusion.1
  63.1 0.2 bitcast_reduce_fusion
  63.3 2.0 fusion.9
  65.4 0.5 broadcast.169
  65.9 0.7 reduce.12
  66.6 0.1 lt.91
  66.7 0.1 iota_compare_fusion
  66.8 0.1 fusion.25
  67.0 48.2 %all-to-all-done.3 = bf16[16,2,256,1,256]{4,2,1,3,0:T(8,128)(2,1)} async-done(((bf16[16,2,256,1,256]{4,2,1,3,0:T(8,128)(2,1)}), bf16[16,2,256,1,256]{4,2,1,3,0:T(8,128)(2,1)}, u32[]{:S(2)}, u32[]{:S(2)}) %all-to-all-start.3) | async-done | bytes 4194336 | tf_op jit(solution)/shard_map/all_to_all | solution.py:116
  115.1 2.3 select_reduce_fusion
  117.4 0.0 copy-start.2
  117.4 0.2 fusion.38
  117.7 0.0 copy-start.4
  117.7 2.0 fusion.7
  119.7 0.0 copy-done
  119.8 1.5 fusion.21
  121.3 0.0 all-reduce.2.cloned.1.call-update
  121.3 0.0 copy-done.2
  121.3 0.9 scatter_custom_fusion
  122.3 0.8 reshape.314
  123.1 8.5 %all-to-all-start = ((bf16[16,2,5120]{2,1,0:T(2,128)(2,1)}), bf16[16,2,5120]{2,1,0:T(2,128)(2,1)S(1)}, u32[]{:S(2)}, u32[]{:S(2)}) async-start(bf16[16,2,5120]{2,1,0:T(2,128)(2,1)} %reshape.314), calls=%async_computation | async-start | bytes 655360 | tf_op jit(solution)/shard_map/all_to_all | solution.py:119
  131.7 0.0 copy-done.4
  131.7 7.4 %all-to-all-done = bf16[16,2,5120]{2,1,0:T(2,128)(2,1)S(1)} async-done(((bf16[16,2,5120]{2,1,0:T(2,128)(2,1)}), bf16[16,2,5120]{2,1,0:T(2,128)(2,1)S(1)}, u32[]{:S(2)}, u32[]{:S(2)}) %all-to-all-start) | async-done | bytes 327712 | tf_op jit(solution)/shard_map/all_to_all | solution.py:119
  139.0 0.1 reshape.315
  139.2 0.0 copy-start.3
  139.2 5.3 %broadcast_select_fusion = bf16[1,1,32,256,1,256]{5,3,4,2,1,0:T(8,128)(2,1)} fusion(bf16[1,1,32,256,1,256]{5,3,4,2,1,0:T(8,128)(2,1)} %bitcast.37, pred[32,256]{1,0:T(8,128)(4,1)S(1)} %get-tuple-element.11, bf16[32,256]{1,0:T(8,128)(2,1)S(1)} %broadcast_in_dim.113), kind=kLoop, calls=%fused_computation.6 | loop fusion | flops 2097152 | bytes 8413184 | tf_op jit(solution)/shard_map/jit(_where)/select_n | solution.py:43
  144.5 120.4 %all-reduce.2.cloned.1.call-done = f32[48,5120]{1,0:T(8,128)} async-done(((f32[48,5120]{1,0:T(8,128)}), f32[48,5120]{1,0:T(8,128)}) %all-reduce.2.cloned.1.call-update) | async-done | bytes 983056 | tf_op jit(solution)/shard_map/psum | solution.py:130
  264.9 0.0 copy-done.3
  264.9 1.3 add_convert_fusion
  266.2 0.0 copy-start.1
  266.2 0.2 fusion.10
  266.4 1.0 fusion.13
  267.4 0.0 copy-done.1
  (16 shorter events, 0.1 us)
Async XLA Ops:
  7.2 112.6 %copy-start = (bf16[256,5120]{1,0:T(8,128)(2,1)S(1)}, bf16[256,5120]{1,0:T(8,128)(2,1)}, u32[]{:S(2)}) copy-start(bf16[256,5120]{1,0:T(8,128)(2,1)} %param.26) | copy-start | bytes 7864324
  10.3 13.5 %all-to-all-start.1 = ((s32[16,1,2]{2,1,0:T(1,128)}), s32[16,1,2]{2,1,0:T(1,128)S(1)}, u32[]{:S(2)}, u32[]{:S(2)}) async-start(s32[16,1,2]{2,1,0:T(1,128)} %bitcast.21), calls=%async_computation.1 | async-start | bytes 16384 | tf_op jit(solution)/shard_map/all_to_all | solution.py:120
  23.8 11.1 %all-to-all-start.4 = ((bf16[16,2,1,256]{3,1,2,0:T(2,128)(2,1)}), bf16[16,2,1,256]{3,1,2,0:T(2,128)(2,1)S(1)}, u32[]{:S(2)}, u32[]{:S(2)}) async-start(bf16[16,2,1,256]{3,1,2,0:T(2,128)(2,1)} %reshape.327), calls=%async_computation.4 | async-start | bytes 32768 | tf_op jit(solution)/shard_map/all_to_all | solution.py:118
  34.9 13.1 %all-to-all-start.2 = ((bf16[16,2,256]{2,1,0:T(2,128)(2,1)}), bf16[16,2,256]{2,1,0:T(2,128)(2,1)S(1)}, u32[]{:S(2)}, u32[]{:S(2)}) async-start(bf16[16,2,256]{2,1,0:T(2,128)(2,1)} %reshape.322), calls=%async_computation.2 | async-start | bytes 32768 | tf_op jit(solution)/shard_map/all_to_all | solution.py:117
  48.0 7.5 %copy-start.5 = (bf16[1,1,16,256]{3,2,1,0:T(8,128)(2,1)S(1)}, bf16[1,1,16,256]{3,2,1,0:T(8,128)(2,1)}, u32[]{:S(2)}) copy-start(bf16[1,1,16,256]{3,2,1,0:T(8,128)(2,1)} %param.17) | copy-start | bytes 24580
  48.0 7.5 %copy-start.8 = (s32[1,1,64]{2,1,0:T(1,128)S(1)}, s32[1,1,64]{2,1,0:T(1,128)}, u32[]{:S(2)}) copy-start(s32[1,1,64]{2,1,0:T(1,128)} %param.15) | copy-start | bytes 772
  48.0 67.1 %all-to-all-start.3 = ((bf16[16,2,256,1,256]{4,2,1,3,0:T(8,128)(2,1)}), bf16[16,2,256,1,256]{4,2,1,3,0:T(8,128)(2,1)}, u32[]{:S(2)}, u32[]{:S(2)}) async-start(bf16[16,2,256,1,256]{4,2,1,3,0:T(8,128)(2,1)} %bitcast.116), calls=%async_computation.3 | async-start | bytes 8388608 | tf_op jit(solution)/shard_map/all_to_all | solution.py:116
  55.4 209.5 %all-reduce.2.cloned.1.call-start = ((), (), s32[]{:S(2)}) async-start(), calls=%async_computation.5 | async-start | bytes 1966080 | tf_op jit(solution)/shard_map/psum | solution.py:130
  55.5 5.0 %copy-start.7 = (s32[1,1,16]{2,1,0:T(1,128)S(1)}, s32[1,1,16]{2,1,0:T(1,128)}, u32[]{:S(2)}) copy-start(s32[1,1,16]{2,1,0:T(1,128)} %param.16) | copy-start | bytes 196
  55.5 5.1 %copy-start.6 = (bf16[1,1,16,1,256]{4,2,3,1,0:T(8,128)(2,1)S(1)}, bf16[1,1,16,1,256]{4,2,3,1,0:T(8,128)(2,1)}, u32[]{:S(2)}) copy-start(bf16[1,1,16,1,256]{4,2,3,1,0:T(8,128)(2,1)} %param.18) | copy-start | bytes 24580
  117.4 3.9 %copy-start.2 = (bf16[1,1,16,5120]{3,2,1,0:T(8,128)(2,1)S(1)}, bf16[1,1,16,5120]{3,2,1,0:T(8,128)(2,1)}, u32[]{:S(2)}) copy-start(bf16[1,1,16,5120]{3,2,1,0:T(8,128)(2,1)} %param.24) | copy-start | bytes 491524
  117.7 14.0 %copy-start.4 = (bf16[5120]{0:T(1024)(128)(2,1)S(1)}, bf16[5120]{0:T(1024)(128)(2,1)}, u32[]{:S(2)}) copy-start(bf16[5120]{0:T(1024)(128)(2,1)} %param.27) | copy-start | bytes 30724
  123.1 15.9 %all-to-all-start = ((bf16[16,2,5120]{2,1,0:T(2,128)(2,1)}), bf16[16,2,5120]{2,1,0:T(2,128)(2,1)S(1)}, u32[]{:S(2)}, u32[]{:S(2)}) async-start(bf16[16,2,5120]{2,1,0:T(2,128)(2,1)} %reshape.314), calls=%async_computation | async-start | bytes 655360 | tf_op jit(solution)/shard_map/all_to_all | solution.py:119
  139.2 125.7 %copy-start.3 = (bf16[1,1,16,5120]{3,2,1,0:T(8,128)(2,1)S(1)}, bf16[1,1,16,5120]{3,2,1,0:T(8,128)(2,1)}, u32[]{:S(2)}) copy-start(bf16[1,1,16,5120]{3,2,1,0:T(8,128)(2,1)} %param.19) | copy-start | bytes 491524
  266.2 1.2 copy-start.1
Sparse Core Ops, SparseCore 0:
  121.4 143.3 all-reduce.1
where the time goes:
time: 275 us; the launch traced here: 274 us
  waiting for transfers between devices  185 us (67%)
  starting transfers between devices  32.9 us (12%)
  local copies, waits for them, and re-layouts  20.3 us (7%)
  between operations  14.3 us (5%)
  other arithmetic  10.7 us (4%)
  matrix products  10.5 us (4%)
    psum x1, waiting for transfers between devices, body(): projected = lax.psum(partial_terms, 'tp')  120 us
    all_to_all x1, waiting for transfers between devices, body(): lax.all_to_all(send_cache, ('pool', 'group'), split_axis=0, concat_axis=0...  48.2 us
    scatter x5, local copies, waits for them, and re-layouts, to_slots(): blank_slots.at[target].set(payload)  9.2 us
    all_to_all x1, starting transfers between devices, body(): lax.all_to_all(send_resid, ('pool', 'group'), split_axis=0, concat_axis=0...  8.54 us
    all_to_all x1, starting transfers between devices, body(): lax.all_to_all(send_cache, ('pool', 'group'), split_axis=0, concat_axis=0...  7.43 us
    all_to_all x1, starting transfers between devices, body(): lax.all_to_all(send_length, ('pool', 'group'), split_axis=0, concat_axis=...  7.39 us
    all_to_all x1, waiting for transfers between devices, body(): lax.all_to_all(send_resid, ('pool', 'group'), split_axis=0, concat_axis=0...  7.36 us
  transfers between devices with their start and end apart: 6, of which 5 were waited for; matrix products, arithmetic and copies ran while one was open for 11% of the time, Pallas kernels for 0%

commit v1 on v0

v1 whole, which is shorter than its diff:
```python
import functools
import math

import jax
import jax.numpy as jnp
from jax import lax
from jax.experimental import pallas as pl
from jax.experimental.pallas import tpu as pltpu
from jax.sharding import PartitionSpec as P

REQ = 16
HD = 128
NZ = 8
SMEM = pltpu.SMEM
VMEM = pltpu.VMEM
VMEM_LIMIT = 48 * 1024 * 1024


def softmax_parts(scores, own_score, lengths):
    position = lax.broadcasted_iota(jnp.int32, scores.shape, 1)
    visible = position < lengths
    top = jnp.max(jnp.where(visible, scores, -1e30), axis=-1, keepdims=True)
    top = jnp.maximum(top, own_score)
    exponent = jnp.where(visible, jnp.exp(scores - top), 0.0)
    own_exponent = jnp.exp(own_score - top)
    denominator = jnp.sum(exponent, axis=-1, keepdims=True) + own_exponent
    weights = (exponent / denominator).astype(jnp.bfloat16).astype(jnp.float32)
    own_weight = (own_exponent / denominator).astype(jnp.bfloat16).astype(jnp.float32)
    return weights, own_weight


def heads_as_rows(wide):
    return jnp.concatenate([wide[:, :HD], wide[:, HD:]], axis=0)


def attend(query, own, kv_of, ready, length_of, tokens):
    rows = 2 * REQ
    scale = 1.0 / math.sqrt(HD)
    heads = heads_as_rows(query)
    own_key = own[:, :HD].astype(jnp.float32)
    own_value = own[:, HD:].astype(jnp.float32)
    own_key = jnp.concatenate([own_key, own_key], axis=0)
    own_value = jnp.concatenate([own_value, own_value], axis=0)
    own_score = jnp.sum(heads.astype(jnp.float32) * own_key, axis=-1, keepdims=True) * scale
    request = lax.broadcasted_iota(jnp.int32, (rows, 1), 0) % REQ
    lengths = jnp.zeros((rows, 1), jnp.int32)
    scores = jnp.zeros((rows, tokens), jnp.float32)
    for r in range(REQ):
        ready(r)
        lengths = jnp.where(request == r, length_of(r), lengths)
        one = lax.dot_general(
            heads, kv_of(r)[:, :HD], (((1,), (1,)), ((), ())), preferred_element_type=jnp.float32
        )
        scores = jnp.where(request == r, one, scores)
    weights, own_weight = softmax_parts(scores * scale, own_score, lengths)
    total = own_weight * own_value
    for r in range(REQ):
        mine = jnp.where(request == r, weights, 0.0).astype(jnp.bfloat16)
        total = total + jnp.dot(mine, kv_of(r)[:, HD:], preferred_element_type=jnp.float32)
    attended = total.astype(jnp.bfloat16)
    return jnp.concatenate([attended[:REQ], attended[REQ:]], axis=1)


def front_kernel(
    place,
    pairing,
    new_lengths,
    lengths,
    table,
    query,
    own,
    new_query,
    new_own,
    resid,
    new_resid,
    new_cache,
    cache,
    weight,
    send,
    first,
    *rest,
):
    others = rest[: NZ - 1]
    new_buf, kv_buf, w_buf, taken, count, new_sem, kv_sem, w_sem, send_sem = rest[NZ - 1 :]
    z, x_lo = place[0], place[1]
    width = w_buf.shape[1] // NZ

    new_copies = [
        pltpu.make_async_copy(new_cache.at[i], new_buf.at[i], new_sem.at[i]) for i in range(REQ)
    ]
    for copy in new_copies:
        copy.start()
    kv_copies = [
        pltpu.make_async_copy(
            cache.at[table[e]], kv_buf.at[e // 4, pl.ds(e % 4 * 128, 128)], kv_sem.at[e]
        )
        for e in range(4 * REQ)
    ]
    for copy in kv_copies:
        copy.start()
    w_copy = pltpu.make_async_copy(weight, w_buf, w_sem)
    w_copy.start()

    new_buf[REQ] = jnp.zeros(new_buf.shape[1:], new_buf.dtype)
    for j in range(2 * REQ):
        taken[j] = REQ
    for j in range(REQ):
        count[j] = 0
    for i in range(REQ):
        target = pairing[i]
        k = count[target]
        count[target] = k + 1
        taken[2 * target + k] = i

    for i in range(REQ):
        new_copies[i].wait()
        base = pl.multiple_of(new_lengths[i] // 16 * 16, 16)
        window = new_buf[i, pl.ds(base, 16), :].astype(jnp.float32)
        row = lax.broadcasted_iota(jnp.int32, (16, 1), 0)
        token = new_own[i : i + 1, :].astype(jnp.float32)
        window = jnp.where(row == new_lengths[i] - base, token, window)
        new_buf[i, pl.ds(base, 16), :] = window.astype(new_buf.dtype)
    send_copies = [
        pltpu.make_async_copy(new_buf.at[taken[j]], send.at[j], send_sem.at[j])
        for j in range(2 * REQ)
    ]
    for copy in send_copies:
        copy.start()

    new_rows = attend(
        new_query[...],
        new_own[...],
        lambda r: new_buf.at[r],
        lambda r: None,
        lambda r: new_lengths[r],
        new_buf.shape[1],
    )

    def kv_ready(r):
        for b in range(4):
            kv_copies[4 * r + b].wait()

    rows = attend(
        query[...],
        own[...],
        lambda r: kv_buf.at[r],
        kv_ready,
        lambda r: lengths[r],
        kv_buf.shape[1],
    )
    attended = jnp.concatenate([rows, new_rows], axis=0)
    w_copy.wait()
    for k in range(NZ):
        columns = pl.ds(pl.multiple_of((z ^ k) * width, 128), width)
        part = jnp.dot(attended, w_buf[:, columns], preferred_element_type=jnp.float32)
        if k:
            others[k - 1][...] = part.astype(jnp.bfloat16)
        else:
            block = jnp.concatenate([resid[:, columns], new_resid[:, columns]], axis=0)
            first[...] = part + jnp.where(x_lo == 0, block.astype(jnp.float32), 0.0)
    for copy in send_copies:
        copy.wait()


def front(place, pairing, new_lengths, lengths, table, query, own, new_query, new_own, resid, new_resid, new_cache, cache, weight):
    tokens = new_cache.shape[1]
    width = weight.shape[1] // NZ
    any_space = pl.BlockSpec(memory_space=pl.ANY)
    smem = pl.BlockSpec(memory_space=SMEM)
    vmem = pl.BlockSpec(memory_space=VMEM)
    return pl.pallas_call(
        front_kernel,
        out_shape=[
            jax.ShapeDtypeStruct((2 * REQ, tokens, 2 * HD), jnp.bfloat16),
            jax.ShapeDtypeStruct((2 * REQ, width), jnp.float32),
        ]
        + [jax.ShapeDtypeStruct((2 * REQ, width), jnp.bfloat16)] * (NZ - 1),
        in_specs=[smem] * 5 + [vmem] * 6 + [any_space] * 3,
        out_specs=[any_space] + [vmem] * NZ,
        scratch_shapes=[
            VMEM((REQ + 1, tokens, 2 * HD), jnp.bfloat16),
            VMEM((REQ, 4 * cache.shape[1], 2 * HD), jnp.bfloat16),
            VMEM(weight.shape, jnp.bfloat16),
            SMEM((2 * REQ,), jnp.int32),
            SMEM((REQ,), jnp.int32),
            pltpu.SemaphoreType.DMA((REQ,)),
            pltpu.SemaphoreType.DMA((4 * REQ,)),
            pltpu.SemaphoreType.DMA,
            pltpu.SemaphoreType.DMA((2 * REQ,)),
        ],
        compiler_params=pltpu.CompilerParams(vmem_limit_bytes=VMEM_LIMIT),
        cost_estimate=pl.CostEstimate(flops=400_000_000, bytes_accessed=14_000_000, transcendentals=30_000),
        name="front",
    )(place, pairing, new_lengths, lengths, table, query, own, new_query, new_own, resid, new_resid, new_cache, cache, weight)


def add_kernel(first, *refs):
    total = first[...]
    for part in refs[:-1]:
        total = total + part[...].astype(jnp.float32)
    refs[-1][...] = total.astype(jnp.bfloat16)


def route_kernel(place, pairing, left, right, resident, *refs):
    outs, count = refs[:4], refs[4]
    me = place[2]
    hidden = (left[...].astype(jnp.float32) + right[...].astype(jnp.float32)).astype(jnp.bfloat16)
    resident[...] = hidden[:REQ]
    for j in range(REQ):
        count[j] = 0
    row = lax.broadcasted_iota(jnp.int32, (2 * REQ, REQ), 0)
    column = lax.broadcasted_iota(jnp.int32, (2 * REQ, REQ), 1)
    target_row = jnp.zeros((2 * REQ, REQ), jnp.int32)
    for i in range(REQ):
        target = pairing[i]
        k = count[target]
        count[target] = k + 1
        offset = me ^ target
        at = ((offset >> 3) * 2 + (offset & 1)) * 8 + ((offset >> 1) & 3) * 2 + k
        target_row = jnp.where(column == i, at, target_row)
    chosen = jnp.where(row == target_row, 1.0, 0.0).astype(jnp.bfloat16)
    placed = jnp.dot(chosen, hidden[REQ:], preferred_element_type=jnp.float32)
    for g in range(4):
        outs[g][...] = placed[8 * g : 8 * g + 8].astype(jnp.bfloat16)


def finish_kernel(place, gain, *refs):
    blocks, (hidden, normed) = refs[:NZ], refs[NZ:]
    z, me = place[0], place[2]
    rows, width = blocks[0].shape
    slots = rows - REQ
    slot = lax.broadcasted_iota(jnp.int32, (slots, slots), 0)
    column = lax.broadcasted_iota(jnp.int32, (slots, slots), 1)
    offset = (slot >> 1) ^ me
    at = ((offset >> 1) & 3) * 8 + ((offset >> 3) * 2 + (offset & 1)) * 2 + (slot & 1)
    order = jnp.where(column == at, 1.0, 0.0).astype(jnp.bfloat16)
    square = jnp.zeros((rows, 1), jnp.float32)
    for k in range(NZ):
        columns = pl.ds(pl.multiple_of((z ^ k) * width, 128), width)
        block = blocks[k][...]
        placed = jnp.dot(order, block[REQ:], preferred_element_type=jnp.float32)
        wide = jnp.concatenate([block[:REQ].astype(jnp.float32), placed], axis=0)
        hidden[:, columns] = wide.astype(jnp.bfloat16)
        square = square + jnp.sum(wide * wide, axis=-1, keepdims=True)
    inverse = lax.rsqrt(square / (width * NZ) + 1e-06)
    for k in range(NZ):
        columns = slice(k * width, (k + 1) * width)
        wide = hidden[:, columns].astype(jnp.float32)
        normed[:, columns] = (wide * inverse * gain[:, columns].astype(jnp.float32)).astype(
            jnp.bfloat16
        )


def body(
    cache,
    table,
    lengths,
    query,
    step_kv,
    resid,
    new_cache,
    new_lengths,
    new_query,
    new_step_kv,
    new_resid,
    pairing,
    o_weight,
    norm_gain,
):
    pool, group, tp = lax.axis_index("pool"), lax.axis_index("group"), lax.axis_index("tp")
    groups = lax.axis_size("pool") * lax.axis_size("group")
    ranks = lax.axis_size("tp")
    place = jnp.stack([tp // 2, tp % 2, pool * lax.axis_size("group") + group]).astype(jnp.int32)
    pair = pairing[0, 0, :, 0]
    smem = pl.BlockSpec(memory_space=SMEM)
    vmem = pl.BlockSpec(memory_space=VMEM)

    send, first, *others = front(
        place,
        pair,
        new_lengths[0, 0],
        lengths[0, 0],
        table[0, 0],
        query[0, 0],
        step_kv[0, 0, :, 0],
        new_query[0, 0],
        new_step_kv[0, 0, :, 0],
        resid[0, 0],
        new_resid[0, 0],
        new_cache[0, 0, :, :, 0],
        cache[0, 0, :, :, 0],
        o_weight,
    )
    both = ("pool", "group")
    slot_cache = lax.all_to_all(
        send.reshape((groups, 2) + send.shape[1:]), both, split_axis=0, concat_axis=0, tiled=True
    )
    slot_cache = slot_cache.reshape(send.shape)[None, None, :, :, None, :]

    def over_tp(array, flip):
        return lax.ppermute(array, "tp", [(t, t ^ flip) for t in range(ranks)])

    def over_groups(array, flip):
        return lax.ppermute(array, both, [(s, s ^ flip) for s in range(groups)])

    parts = [over_tp(others[k - 1], 2 * k) for k in range(1, NZ)]
    width = first.shape[1]
    half = pl.pallas_call(
        add_kernel,
        out_shape=jax.ShapeDtypeStruct(first.shape, jnp.bfloat16),
        in_specs=[vmem] * NZ,
        out_specs=vmem,
        name="add",
    )(first, *parts)
    other_half = over_tp(half, 1)
    resident, *toward = pl.pallas_call(
        route_kernel,
        out_shape=[jax.ShapeDtypeStruct((REQ, width), jnp.bfloat16)]
        + [jax.ShapeDtypeStruct((8, width), jnp.bfloat16)] * 4,
        in_specs=[smem] * 2 + [vmem] * 2,
        out_specs=[vmem] * 5,
        scratch_shapes=[SMEM((REQ,), jnp.int32)],
        name="route",
    )(place, pair, half, other_half)
    crossed = [toward[0]] + [
        over_groups(toward[g], (g >> 1) * 8 + (g & 1)) for g in range(1, 4)
    ]
    crossed = jnp.stack(crossed).reshape(4, 4, 2, width)
    turned = crossed.transpose(1, 0, 2, 3).reshape(4, 8, width)
    slots = [turned[0]] + [over_groups(turned[y], 2 * y) for y in range(1, 4)]
    block = jnp.concatenate([resident] + slots, axis=0)
    blocks = [block] + [over_tp(block, 2 * k) for k in range(1, NZ)]
    hidden, normed = pl.pallas_call(
        finish_kernel,
        out_shape=[jax.ShapeDtypeStruct((block.shape[0], width * NZ), jnp.bfloat16)] * 2,
        in_specs=[smem] + [vmem] * (NZ + 1),
        out_specs=[vmem] * 2,
        name="finish",
    )(place, norm_gain.reshape(1, -1), *blocks)
    return (hidden[None, None], normed[None, None], slot_cache)


def solution(mesh):
    placed = (
        P("pool", "group", None, None, "tp", None),
        P("pool", "group", None),
        P("pool", "group", None),
        P("pool", "group", None, "tp"),
        P("pool", "group", None, "tp", None),
        P("pool", "group", None, None),
        P("pool", "group", None, None, "tp", None),
        P("pool", "group", None),
        P("pool", "group", None, "tp"),
        P("pool", "group", None, "tp", None),
        P("pool", "group", None, None),
        P("pool", "group", None, None),
        P("tp", None),
        P(),
    )
    return jax.shard_map(
        body,
        mesh=mesh,
        in_specs=placed,
        out_specs=(
            P("pool", "group", None, None),
            P("pool", "group", None, None),
            P("pool", "group", None, None, "tp", None),
        ),
        check_vma=False,
    )
```

time: 275 us -> 137 us (0.50)
  the two profiles are of different devices: /device:TPU:8 before, /device:TPU:1 now
where the time goes in v1:
time: 137 us; the launch traced here: 136 us
  starting transfers between devices  50.3 us (37%)
  waiting for transfers between devices  50 us (36%)
  local copies, waits for them, and re-layouts  19.9 us (15%)
  Pallas kernels  14.8 us (11%)
    ppermute x15, waiting for transfers between devices, over_tp(): return lax.ppermute(array, 'tp', [(t, t ^ flip) for t in range(ranks)])  45.2 us
    ppermute x15, starting transfers between devices, over_tp(): return lax.ppermute(array, 'tp', [(t, t ^ flip) for t in range(ranks)])  29.5 us
    unnamed x67, local copies, waits for them, and re-layouts  18.5 us
    ppermute x6, starting transfers between devices, over_groups(): return lax.ppermute(array, both, [(s, s ^ flip) for s in range(groups)])  12.2 us
    pallas_call x1, Pallas kernels, front(): pl.pallas_call(front_kernel, out_shape=[jax.ShapeDtypeStruct((2 * REQ, to...  9.33 us
    all_to_all x1, starting transfers between devices, body(): lax.all_to_all(send.reshape((groups, 2) + send.shape[1:]), both, split_ax...  8.58 us
    ppermute x6, waiting for transfers between devices, over_groups(): return lax.ppermute(array, both, [(s, s ^ flip) for s in range(groups)])  4.76 us
  transfers between devices with their start and end apart: 22, of which 8 were waited for; matrix products, arithmetic and copies ran while one was open for 2% of the time, Pallas kernels for 4%

profile of v1, /device:TPU:1, one launch (start us, length us, event | category | flops | bytes accessed | tf_op | source)
XLA Modules:
  0.0 136.1 jit_solution(7895927507365521807)
XLA Ops:
  0.7 0.1 pad_add_fusion.place
  0.7 1.7 %copy-done = bf16[256,5120]{1,0:T(8,128)(2,1)S(1)} copy-done((bf16[256,5120]{1,0:T(8,128)(2,1)S(1)}, bf16[256,5120]{1,0:T(8,128)(2,1)}, u32[]{:S(2)}) %copy-start) | copy-done | bytes 2621464
  2.5 1.6 %copy-done.1 = bf16[1,1,16,256,1,256]{5,3,4,2,1,0:T(8,128)(2,1)S(1)} copy-done((bf16[1,1,16,256,1,256]{5,3,4,2,1,0:T(8,128)(2,1)S(1)}, bf16[1,1,16,256,1,256]{5,3,4,2,1,0:T(8,128)(2,1)}, u32[]{:S(2)}) %copy-start.1) | copy-done | bytes 2097176
  4.1 0.9 copy-done.2
  5.0 0.9 copy-done.3
  5.9 0.7 copy-done.5
  6.6 0.7 copy-done.6
  7.3 0.7 copy-done.7
  8.0 0.7 copy-done.8
  8.7 0.7 copy-done.10
  9.3 0.7 copy-done.11
  10.0 0.7 copy-done.12
  10.7 0.7 copy-done.13
  11.3 9.3 %front.1 = (bf16[32,256,256]{2,1,0:T(8,128)(2,1)}, f32[32,640]{1,0:T(8,128)S(1)}, bf16[32,640]{1,0:T(8,128)(2,1)S(1)}, bf16[32,640]{1,0:T(8,128)(2,1)S(1)}, bf16...) custom-call(s32[3]{0:T(128)S(1)} %pad_add_fusion.place, ...), custom_call_target="tpu_custom_call" | custom-call | flops 400000000 | bytes 14000000 | tf_op jit(solution)/shard_map/front/pallas_call | solution.py:171
  20.7 0.0 copy-start.4
  20.7 0.6 copy-done.4
  21.3 8.6 %all-to-all-start = ((bf16[16,2,256,256]{3,2,1,0:T(8,128)(2,1)}), bf16[16,2,256,256]{3,2,1,0:T(8,128)(2,1)}, u32[]{:S(2)}, u32[]{:S(2)}) async-start(bf16[16,2,256,256]{3,2,1,0:T(8,128)(2,1)} %bitcast.37), calls=%async_computation | async-start | bytes 8388608 | tf_op jit(solution)/shard_map/all_to_all | solution.py:295
  29.9 1.7 %collective-permute-start = (bf16[32,640]{1,0:T(8,128)(2,1)S(1)}, bf16[32,640]{1,0:T(8,128)(2,1)S(1)}, u32[]{:S(2)}, u32[]{:S(2)}) collective-permute-start(bf16[32,640]{1,0:T(8,128)(2,1)S(1)} %get-tuple-element.20), channel_id=1, source_target_pairs={{0,2},{1,3},{2,0},{3,1},{4,6},{5,7},{6,4},{7,5},{8,10},{9,11},{10,... | collective-permute-start | bytes 122888 | tf_op jit(solution)/shard_map/ppermute | solution.py:301
  31.5 3.0 %collective-permute-start.1 = (bf16[32,640]{1,0:T(8,128)(2,1)S(1)}, bf16[32,640]{1,0:T(8,128)(2,1)S(1)}, u32[]{:S(2)}, u32[]{:S(2)}) collective-permute-start(bf16[32,640]{1,0:T(8,128)(2,1)S(1)} %get-tuple-element.21), channel_id=1, source_target_pairs={{0,4},{1,5},{2,6},{3,7},{4,0},{5,1},{6,2},{7,3},{8,12},{9,13},{10,... | collective-permute-start | bytes 122888 | tf_op jit(solution)/shard_map/ppermute | solution.py:301
  34.5 5.8 %collective-permute-start.3 = (bf16[32,640]{1,0:T(8,128)(2,1)S(1)}, bf16[32,640]{1,0:T(8,128)(2,1)S(1)}, u32[]{:S(2)}, u32[]{:S(2)}) collective-permute-start(bf16[32,640]{1,0:T(8,128)(2,1)S(1)} %get-tuple-element.23), channel_id=1, source_target_pairs={{0,8},{1,9},{2,10},{3,11},{4,12},{5,13},{6,14},{7,15},{8,0},{9,1},... | collective-permute-start | bytes 122888 | tf_op jit(solution)/shard_map/ppermute | solution.py:301
  40.3 0.0 collective-permute-start.4
  40.3 0.0 collective-permute-done.refs_0_
  40.3 4.1 %collective-permute-start.5 = (bf16[32,640]{1,0:T(8,128)(2,1)S(1)}, bf16[32,640]{1,0:T(8,128)(2,1)S(1)}, u32[]{:S(2)}, u32[]{:S(2)}) collective-permute-start(bf16[32,640]{1,0:T(8,128)(2,1)S(1)} %get-tuple-element.25), channel_id=1, source_target_pairs={{0,12},{1,13},{2,14},{3,15},{4,8},{5,9},{6,10},{7,11},{8,4},{9,5},... | collective-permute-start | bytes 122888 | tf_op jit(solution)/shard_map/ppermute | solution.py:301
  44.4 0.0 collective-permute-done.1.refs_1_
  44.4 0.0 collective-permute-start.6
  44.4 0.0 collective-permute-done.3.refs_3_
  44.5 1.8 %collective-permute-done.4.refs_4_ = bf16[32,640]{1,0:T(8,128)(2,1)S(1)} collective-permute-done((bf16[32,640]{1,0:T(8,128)(2,1)S(1)}, bf16[32,640]{1,0:T(8,128)(2,1)S(1)}, u32[]{:S(2)}, u32[]{:S(2)}) %collective-permute-start.4) | collective-permute-done | bytes 40992 | tf_op jit(solution)/shard_map/ppermute | solution.py:301
  46.3 0.0 collective-permute-done.5.refs_5_
  46.3 3.2 %collective-permute-done.6.refs_6_ = bf16[32,640]{1,0:T(8,128)(2,1)S(1)} collective-permute-done((bf16[32,640]{1,0:T(8,128)(2,1)S(1)}, bf16[32,640]{1,0:T(8,128)(2,1)S(1)}, u32[]{:S(2)}, u32[]{:S(2)}) %collective-permute-start.6) | collective-permute-done | bytes 40992 | tf_op jit(solution)/shard_map/ppermute | solution.py:301
  49.6 0.6 copy-done.28
  50.1 1.6 %add.15.left = bf16[32,640]{1,0:T(8,128)(2,1)} custom-call(f32[32,640]{1,0:T(8,128)} %copy-done.4, bf16[32,640]{1,0:T(8,128)(2,1)} %copy-done.22, bf16[32,640]{1,0:T(8,128)(2,1)} %copy-done.23, bf16[32,640]{1,0:T(8,128)(2,1)} %copy-done.24, bf16[32,640]{1,0:T(8,128)(2,1)} %copy-done.25, bf16[32,640]{1,0:T(8,128)(2,1)} %copy-done.26, ...), custom_call_target="tpu_custom_call" | custom-call | tf_op jit(solution)/shard_map/add/pallas_call | solution.py:308
  51.8 0.3 collective-permute-start.7
  52.1 33.7 %collective-permute-done.7.right = bf16[32,640]{1,0:T(8,128)(2,1)S(1)} collective-permute-done((bf16[32,640]{1,0:T(8,128)(2,1)}, bf16[32,640]{1,0:T(8,128)(2,1)S(1)}, u32[]{:S(2)}, u32[]{:S(2)}) %collective-permute-start.7) | collective-permute-done | bytes 40992 | tf_op jit(solution)/shard_map/ppermute | solution.py:301
  85.8 0.6 copy-done.29
  86.4 1.6 %route.1 = (bf16[16,640]{1,0:T(8,128)(2,1)}, bf16[8,640]{1,0:T(8,128)(2,1)}, bf16[8,640]{1,0:T(8,128)(2,1)}, bf16[8,640]{1,0:T(8,128)(2,1)}, bf16[8,640]{1,0:T(8,128)(2,1)}) custom-call(s32[3]{0:T(128)} %copy-done.9, s32[16]{0:T(128)} %bitcast.32, bf16[32,640]{1,0:T(8,128)(2,1)} %add.15.left, bf16[32,640]{1,0:T(8,128)(2,1)} %copy-done.29), custom_call_target="tpu_custom_call" | custom-call | tf_op jit(solution)/shard_map/route/pallas_call | solution.py:316
  88.1 0.6 collective-permute-start.8
  88.6 3.1 %collective-permute-start.9 = (bf16[8,640]{1,0:T(8,128)(2,1)}, bf16[8,640]{1,0:T(8,128)(2,1)S(1)}, u32[]{:S(2)}, u32[]{:S(2)}) collective-permute-start(bf16[8,640]{1,0:T(8,128)(2,1)} %get-tuple-element.30), channel_id=1, source_target_pairs={{0,128},{16,144},{32,160},{48,176},{64,192},{80,208},{96,224},{112... | collective-permute-start | bytes 30728 | tf_op jit(solution)/shard_map/ppermute | solution.py:304
  91.8 0.1 collective-permute-start.10
  91.9 0.7 constant_dynamic-update-slice_fusion.4
  92.6 0.7 stack.31
  93.3 0.0 collective-permute-done.8
  93.3 0.0 collective-permute-done.9
  93.3 3.3 %collective-permute-done.10 = bf16[8,640]{1,0:T(8,128)(2,1)S(1)} collective-permute-done((bf16[8,640]{1,0:T(8,128)(2,1)}, bf16[8,640]{1,0:T(8,128)(2,1)S(1)}, u32[]{:S(2)}, u32[]{:S(2)}) %collective-permute-start.10) | collective-permute-done | bytes 10272 | tf_op jit(solution)/shard_map/ppermute | solution.py:304
  96.6 0.1 maximum_bitcast_fusion
  96.8 5.9 %collective-permute-start.11 = (bf16[8,640]{1,0:T(8,128)(2,1)S(1)}, bf16[8,640]{1,0:T(8,128)(2,1)S(1)}, u32[]{:S(2)}, u32[]{:S(2)}) collective-permute-start(bf16[8,640]{1,0:T(8,128)(2,1)S(1)} %squeeze.61), channel_id=1, source_target_pairs={{0,32},{16,48},{32,0},{48,16},{64,96},{80,112},{96,64},{112,80},{1... | collective-permute-start | bytes 30728 | tf_op jit(solution)/shard_map/ppermute | solution.py:304
  102.6 0.1 collective-permute-start.12
  102.8 2.5 %collective-permute-start.13 = (bf16[8,640]{1,0:T(8,128)(2,1)S(1)}, bf16[8,640]{1,0:T(8,128)(2,1)S(1)}, u32[]{:S(2)}, u32[]{:S(2)}) collective-permute-start(bf16[8,640]{1,0:T(8,128)(2,1)S(1)} %squeeze.63), channel_id=1, source_target_pairs={{0,96},{16,112},{32,64},{48,80},{64,32},{80,48},{96,0},{112,16},{1... | collective-permute-start | bytes 30728 | tf_op jit(solution)/shard_map/ppermute | solution.py:304
  105.3 0.0 collective-permute-done.11
  105.3 1.5 %collective-permute-done.12 = bf16[8,640]{1,0:T(8,128)(2,1)S(1)} collective-permute-done((bf16[8,640]{1,0:T(8,128)(2,1)S(1)}, bf16[8,640]{1,0:T(8,128)(2,1)S(1)}, u32[]{:S(2)}, u32[]{:S(2)}) %collective-permute-start.12) | collective-permute-done | bytes 10272 | tf_op jit(solution)/shard_map/ppermute | solution.py:304
  106.8 0.0 collective-permute-done.13
  106.8 1.8 %collective-permute-start.14 = (bf16[48,640]{1,0:T(8,128)(2,1)S(1)}, bf16[48,640]{1,0:T(8,128)(2,1)S(1)}, u32[]{:S(2)}, u32[]{:S(2)}) collective-permute-start(bf16[48,640]{1,0:T(8,128)(2,1)S(1)} %constant_dynamic-update-slice_fusion.refs_0_), channel_id=1, source_target_pairs={{0,2},{1,3},{2,0},{3,1},{4,6},{5,7},{6,4},{7,5},{8,10},{9,11},{10,... | collective-permute-start | bytes 184328 | tf_op jit(solution)/shard_map/ppermute | solution.py:301
  108.5 3.0 %collective-permute-start.15 = (bf16[48,640]{1,0:T(8,128)(2,1)S(1)}, bf16[48,640]{1,0:T(8,128)(2,1)S(1)}, u32[]{:S(2)}, u32[]{:S(2)}) collective-permute-start(bf16[48,640]{1,0:T(8,128)(2,1)S(1)} %constant_dynamic-update-slice_fusion.refs_0_), channel_id=1, source_target_pairs={{0,4},{1,5},{2,6},{3,7},{4,0},{5,1},{6,2},{7,3},{8,12},{9,13},{10,... | collective-permute-start | bytes 184328 | tf_op jit(solution)/shard_map/ppermute | solution.py:301
  111.5 0.1 collective-permute-start.16
  111.6 5.7 %collective-permute-start.17 = (bf16[48,640]{1,0:T(8,128)(2,1)S(1)}, bf16[48,640]{1,0:T(8,128)(2,1)S(1)}, u32[]{:S(2)}, u32[]{:S(2)}) collective-permute-start(bf16[48,640]{1,0:T(8,128)(2,1)S(1)} %constant_dynamic-update-slice_fusion.refs_0_), channel_id=1, source_target_pairs={{0,8},{1,9},{2,10},{3,11},{4,12},{5,13},{6,14},{7,15},{8,0},{9,1},... | collective-permute-start | bytes 184328 | tf_op jit(solution)/shard_map/ppermute | solution.py:301
  117.3 0.0 collective-permute-start.18
  117.3 0.0 collective-permute-done.14.refs_1_
  117.3 4.1 %collective-permute-start.19 = (bf16[48,640]{1,0:T(8,128)(2,1)S(1)}, bf16[48,640]{1,0:T(8,128)(2,1)S(1)}, u32[]{:S(2)}, u32[]{:S(2)}) collective-permute-start(bf16[48,640]{1,0:T(8,128)(2,1)S(1)} %constant_dynamic-update-slice_fusion.refs_0_), channel_id=1, source_target_pairs={{0,12},{1,13},{2,14},{3,15},{4,8},{5,9},{6,10},{7,11},{8,4},{9,5},... | collective-permute-start | bytes 184328 | tf_op jit(solution)/shard_map/ppermute | solution.py:301
  121.4 0.6 reshape.30.gain
  122.1 3.9 %collective-permute-done.18.refs_5_ = bf16[48,640]{1,0:T(8,128)(2,1)S(1)} collective-permute-done((bf16[48,640]{1,0:T(8,128)(2,1)S(1)}, bf16[48,640]{1,0:T(8,128)(2,1)S(1)}, u32[]{:S(2)}, u32[]{:S(2)}) %collective-permute-start.18) | collective-permute-done | bytes 61472 | tf_op jit(solution)/shard_map/ppermute | solution.py:301
  126.0 0.2 collective-permute-done.19.refs_6_
  126.2 2.3 %collective-permute-done.20.refs_7_ = bf16[48,640]{1,0:T(8,128)(2,1)S(1)} collective-permute-done((bf16[48,640]{1,0:T(8,128)(2,1)S(1)}, bf16[48,640]{1,0:T(8,128)(2,1)S(1)}, u32[]{:S(2)}, u32[]{:S(2)}) %collective-permute-start.20) | collective-permute-done | bytes 61472 | tf_op jit(solution)/shard_map/ppermute | solution.py:301
  128.5 0.6 copy-done.21
  129.2 2.2 %finish.1 = (bf16[48,5120]{1,0:T(8,128)(2,1)}, bf16[48,5120]{1,0:T(8,128)(2,1)}) custom-call(s32[3]{0:T(128)} %copy-done.9, bf16[1,5120]{1,0:T(2,128)(2,1)} %reshape.30.gain, bf16[48,640]{1,0:T(8,128)(2,1)} %copy-done.14, bf16[48,640]{1,0:T(8,128)(2,1)} %copy-done.15, bf16[48,640]{1,0:T(8,128)(2,1)} %copy-done.16, bf16[48,640]{1,0:T(8,128)(2,1)} %copy-done.17, ...), custom_call_target="tpu_custom_call" | custom-call | tf_op jit(solution)/shard_map/finish/pallas_call | solution.py:333
  131.4 4.6 %copy.26 = bf16[1,1,32,256,1,256]{5,3,4,2,1,0:T(8,128)(2,1)} copy(bf16[1,1,32,256,1,256]{5,3,4,2,1,0:T(8,128)(2,1)} %bitcast.23) | data formatting | bytes 8388608
  (64 shorter events, 0.3 us)
Async XLA Ops:
  0.7 19.9 %copy-start.9 = (s32[3]{0:T(128)}, s32[3]{0:T(128)S(1)}, u32[]{:S(2)}) copy-start(s32[3]{0:T(128)S(1)} %pad_add_fusion.place) | copy-start | bytes 40
  0.7 1.7 %copy-start = (bf16[256,5120]{1,0:T(8,128)(2,1)S(1)}, bf16[256,5120]{1,0:T(8,128)(2,1)}, u32[]{:S(2)}) copy-start(bf16[256,5120]{1,0:T(8,128)(2,1)} %weight.1) | copy-start | bytes 7864324
  2.5 1.6 %copy-start.1 = (bf16[1,1,16,256,1,256]{5,3,4,2,1,0:T(8,128)(2,1)S(1)}, bf16[1,1,16,256,1,256]{5,3,4,2,1,0:T(8,128)(2,1)}, u32[]{:S(2)}) copy-start(bf16[1,1,16,256,1,256]{5,3,4,2,1,0:T(8,128)(2,1)} %param.20) | copy-start | bytes 6291460
  4.1 0.9 copy-start.2
  5.0 0.9 copy-start.3
  5.9 0.7 copy-start.5
  6.6 0.7 copy-start.6
  7.3 0.7 copy-start.7
  8.0 0.7 copy-start.8
  8.7 0.7 copy-start.10
  9.3 0.7 copy-start.11
  10.0 0.7 copy-start.12
  10.7 0.7 copy-start.13
  20.7 0.6 copy-start.4
  21.3 100.1 %copy-start.30 = (bf16[5120]{0:T(1024)(128)(2,1)S(1)}, bf16[5120]{0:T(1024)(128)(2,1)}, u32[]{:S(2)}) copy-start(bf16[5120]{0:T(1024)(128)(2,1)} %param.27) | copy-start | bytes 30724
  21.3 110.1 %all-to-all-start = ((bf16[16,2,256,256]{3,2,1,0:T(8,128)(2,1)}), bf16[16,2,256,256]{3,2,1,0:T(8,128)(2,1)}, u32[]{:S(2)}, u32[]{:S(2)}) async-start(bf16[16,2,256,256]{3,2,1,0:T(8,128)(2,1)} %bitcast.37), calls=%async_computation | async-start | bytes 8388608 | tf_op jit(solution)/shard_map/all_to_all | solution.py:295
  29.9 10.5 %collective-permute-start = (bf16[32,640]{1,0:T(8,128)(2,1)S(1)}, bf16[32,640]{1,0:T(8,128)(2,1)S(1)}, u32[]{:S(2)}, u32[]{:S(2)}) collective-permute-start(bf16[32,640]{1,0:T(8,128)(2,1)S(1)} %get-tuple-element.20), channel_id=1, source_target_pairs={{0,2},{1,3},{2,0},{3,1},{4,6},{5,7},{6,4},{7,5},{8,10},{9,11},{10,... | collective-permute-start | bytes 122888 | tf_op jit(solution)/shard_map/ppermute | solution.py:301
  31.5 12.9 %collective-permute-start.1 = (bf16[32,640]{1,0:T(8,128)(2,1)S(1)}, bf16[32,640]{1,0:T(8,128)(2,1)S(1)}, u32[]{:S(2)}, u32[]{:S(2)}) collective-permute-start(bf16[32,640]{1,0:T(8,128)(2,1)S(1)} %get-tuple-element.21), channel_id=1, source_target_pairs={{0,4},{1,5},{2,6},{3,7},{4,0},{5,1},{6,2},{7,3},{8,12},{9,13},{10,... | collective-permute-start | bytes 122888 | tf_op jit(solution)/shard_map/ppermute | solution.py:301
  34.5 9.9 %collective-permute-start.2 = (bf16[32,640]{1,0:T(8,128)(2,1)S(1)}, bf16[32,640]{1,0:T(8,128)(2,1)S(1)}, u32[]{:S(2)}, u32[]{:S(2)}) collective-permute-start(bf16[32,640]{1,0:T(8,128)(2,1)S(1)} %get-tuple-element.22), channel_id=1, source_target_pairs={{0,6},{1,7},{2,4},{3,5},{4,2},{5,3},{6,0},{7,1},{8,14},{9,15},{10,... | collective-permute-start | bytes 122888 | tf_op jit(solution)/shard_map/ppermute | solution.py:301
  34.5 9.9 %collective-permute-start.3 = (bf16[32,640]{1,0:T(8,128)(2,1)S(1)}, bf16[32,640]{1,0:T(8,128)(2,1)S(1)}, u32[]{:S(2)}, u32[]{:S(2)}) collective-permute-start(bf16[32,640]{1,0:T(8,128)(2,1)S(1)} %get-tuple-element.23), channel_id=1, source_target_pairs={{0,8},{1,9},{2,10},{3,11},{4,12},{5,13},{6,14},{7,15},{8,0},{9,1},... | collective-permute-start | bytes 122888 | tf_op jit(solution)/shard_map/ppermute | solution.py:301
  40.3 6.0 %collective-permute-start.4 = (bf16[32,640]{1,0:T(8,128)(2,1)S(1)}, bf16[32,640]{1,0:T(8,128)(2,1)S(1)}, u32[]{:S(2)}, u32[]{:S(2)}) collective-permute-start(bf16[32,640]{1,0:T(8,128)(2,1)S(1)} %get-tuple-element.24), channel_id=1, source_target_pairs={{0,10},{1,11},{2,8},{3,9},{4,14},{5,15},{6,12},{7,13},{8,2},{9,3},... | collective-permute-start | bytes 122888 | tf_op jit(solution)/shard_map/ppermute | solution.py:301
  40.3 9.2 %copy-start.22 = (bf16[32,640]{1,0:T(8,128)(2,1)}, bf16[32,640]{1,0:T(8,128)(2,1)S(1)}, u32[]{:S(2)}) copy-start(bf16[32,640]{1,0:T(8,128)(2,1)S(1)} %collective-permute-done.refs_0_) | copy-start | bytes 122884
  40.3 5.9 %collective-permute-start.5 = (bf16[32,640]{1,0:T(8,128)(2,1)S(1)}, bf16[32,640]{1,0:T(8,128)(2,1)S(1)}, u32[]{:S(2)}, u32[]{:S(2)}) collective-permute-start(bf16[32,640]{1,0:T(8,128)(2,1)S(1)} %get-tuple-element.25), channel_id=1, source_target_pairs={{0,12},{1,13},{2,14},{3,15},{4,8},{5,9},{6,10},{7,11},{8,4},{9,5},... | collective-permute-start | bytes 122888 | tf_op jit(solution)/shard_map/ppermute | solution.py:301
  44.4 5.1 %copy-start.23 = (bf16[32,640]{1,0:T(8,128)(2,1)}, bf16[32,640]{1,0:T(8,128)(2,1)S(1)}, u32[]{:S(2)}) copy-start(bf16[32,640]{1,0:T(8,128)(2,1)S(1)} %collective-permute-done.1.refs_1_) | copy-start | bytes 122884
  44.4 5.1 %collective-permute-start.6 = (bf16[32,640]{1,0:T(8,128)(2,1)S(1)}, bf16[32,640]{1,0:T(8,128)(2,1)S(1)}, u32[]{:S(2)}, u32[]{:S(2)}) collective-permute-start(bf16[32,640]{1,0:T(8,128)(2,1)S(1)} %get-tuple-element.26), channel_id=1, source_target_pairs={{0,14},{1,15},{2,12},{3,13},{4,10},{5,11},{6,8},{7,9},{8,6},{9,7},... | collective-permute-start | bytes 122888 | tf_op jit(solution)/shard_map/ppermute | solution.py:301
  44.4 5.1 %copy-start.24 = (bf16[32,640]{1,0:T(8,128)(2,1)}, bf16[32,640]{1,0:T(8,128)(2,1)S(1)}, u32[]{:S(2)}) copy-start(bf16[32,640]{1,0:T(8,128)(2,1)S(1)} %collective-permute-done.2.refs_2_) | copy-start | bytes 122884
  44.5 5.1 %copy-start.25 = (bf16[32,640]{1,0:T(8,128)(2,1)}, bf16[32,640]{1,0:T(8,128)(2,1)S(1)}, u32[]{:S(2)}) copy-start(bf16[32,640]{1,0:T(8,128)(2,1)S(1)} %collective-permute-done.3.refs_3_) | copy-start | bytes 122884
  46.3 3.3 %copy-start.26 = (bf16[32,640]{1,0:T(8,128)(2,1)}, bf16[32,640]{1,0:T(8,128)(2,1)S(1)}, u32[]{:S(2)}) copy-start(bf16[32,640]{1,0:T(8,128)(2,1)S(1)} %collective-permute-done.4.refs_4_) | copy-start | bytes 122884
  46.3 3.3 %copy-start.27 = (bf16[32,640]{1,0:T(8,128)(2,1)}, bf16[32,640]{1,0:T(8,128)(2,1)S(1)}, u32[]{:S(2)}) copy-start(bf16[32,640]{1,0:T(8,128)(2,1)S(1)} %collective-permute-done.5.refs_5_) | copy-start | bytes 122884
  49.5 0.6 copy-start.28
  51.8 34.1 %collective-permute-start.7 = (bf16[32,640]{1,0:T(8,128)(2,1)}, bf16[32,640]{1,0:T(8,128)(2,1)S(1)}, u32[]{:S(2)}, u32[]{:S(2)}) collective-permute-start(bf16[32,640]{1,0:T(8,128)(2,1)} %add.15.left), channel_id=1, source_target_pairs={{0,1},{1,0},{2,3},{3,2},{4,5},{5,4},{6,7},{7,6},{8,9},{9,8},{10,11... | collective-permute-start | bytes 122888 | tf_op jit(solution)/shard_map/ppermute | solution.py:301
  85.8 0.6 copy-start.29
  88.1 5.2 %collective-permute-start.8 = (bf16[8,640]{1,0:T(8,128)(2,1)}, bf16[8,640]{1,0:T(8,128)(2,1)S(1)}, u32[]{:S(2)}, u32[]{:S(2)}) collective-permute-start(bf16[8,640]{1,0:T(8,128)(2,1)} %get-tuple-element.29), channel_id=1, source_target_pairs={{0,16},{16,0},{32,48},{48,32},{64,80},{80,64},{96,112},{112,96},{1... | collective-permute-start | bytes 30728 | tf_op jit(solution)/shard_map/ppermute | solution.py:304
  88.6 4.7 %collective-permute-start.9 = (bf16[8,640]{1,0:T(8,128)(2,1)}, bf16[8,640]{1,0:T(8,128)(2,1)S(1)}, u32[]{:S(2)}, u32[]{:S(2)}) collective-permute-start(bf16[8,640]{1,0:T(8,128)(2,1)} %get-tuple-element.30), channel_id=1, source_target_pairs={{0,128},{16,144},{32,160},{48,176},{64,192},{80,208},{96,224},{112... | collective-permute-start | bytes 30728 | tf_op jit(solution)/shard_map/ppermute | solution.py:304
  91.8 4.8 %collective-permute-start.10 = (bf16[8,640]{1,0:T(8,128)(2,1)}, bf16[8,640]{1,0:T(8,128)(2,1)S(1)}, u32[]{:S(2)}, u32[]{:S(2)}) collective-permute-start(bf16[8,640]{1,0:T(8,128)(2,1)} %get-tuple-element.31), channel_id=1, source_target_pairs={{0,144},{16,128},{32,176},{48,160},{64,208},{80,192},{96,240},{112... | collective-permute-start | bytes 30728 | tf_op jit(solution)/shard_map/ppermute | solution.py:304
  96.8 8.5 %collective-permute-start.11 = (bf16[8,640]{1,0:T(8,128)(2,1)S(1)}, bf16[8,640]{1,0:T(8,128)(2,1)S(1)}, u32[]{:S(2)}, u32[]{:S(2)}) collective-permute-start(bf16[8,640]{1,0:T(8,128)(2,1)S(1)} %squeeze.61), channel_id=1, source_target_pairs={{0,32},{16,48},{32,0},{48,16},{64,96},{80,112},{96,64},{112,80},{1... | collective-permute-start | bytes 30728 | tf_op jit(solution)/shard_map/ppermute | solution.py:304
  102.6 4.1 %collective-permute-start.12 = (bf16[8,640]{1,0:T(8,128)(2,1)S(1)}, bf16[8,640]{1,0:T(8,128)(2,1)S(1)}, u32[]{:S(2)}, u32[]{:S(2)}) collective-permute-start(bf16[8,640]{1,0:T(8,128)(2,1)S(1)} %squeeze.62), channel_id=1, source_target_pairs={{0,64},{16,80},{32,96},{48,112},{64,0},{80,16},{96,32},{112,48},{1... | collective-permute-start | bytes 30728 | tf_op jit(solution)/shard_map/ppermute | solution.py:304
  102.8 4.0 %collective-permute-start.13 = (bf16[8,640]{1,0:T(8,128)(2,1)S(1)}, bf16[8,640]{1,0:T(8,128)(2,1)S(1)}, u32[]{:S(2)}, u32[]{:S(2)}) collective-permute-start(bf16[8,640]{1,0:T(8,128)(2,1)S(1)} %squeeze.63), channel_id=1, source_target_pairs={{0,96},{16,112},{32,64},{48,80},{64,32},{80,48},{96,0},{112,16},{1... | collective-permute-start | bytes 30728 | tf_op jit(solution)/shard_map/ppermute | solution.py:304
  106.8 21.7 %copy-start.14 = (bf16[48,640]{1,0:T(8,128)(2,1)}, bf16[48,640]{1,0:T(8,128)(2,1)S(1)}, u32[]{:S(2)}) copy-start(bf16[48,640]{1,0:T(8,128)(2,1)S(1)} %constant_dynamic-update-slice_fusion.refs_0_) | copy-start | bytes 184324
  106.8 10.6 %collective-permute-start.14 = (bf16[48,640]{1,0:T(8,128)(2,1)S(1)}, bf16[48,640]{1,0:T(8,128)(2,1)S(1)}, u32[]{:S(2)}, u32[]{:S(2)}) collective-permute-start(bf16[48,640]{1,0:T(8,128)(2,1)S(1)} %constant_dynamic-update-slice_fusion.refs_0_), channel_id=1, source_target_pairs={{0,2},{1,3},{2,0},{3,1},{4,6},{5,7},{6,4},{7,5},{8,10},{9,11},{10,... | collective-permute-start | bytes 184328 | tf_op jit(solution)/shard_map/ppermute | solution.py:301
  108.5 12.9 %collective-permute-start.15 = (bf16[48,640]{1,0:T(8,128)(2,1)S(1)}, bf16[48,640]{1,0:T(8,128)(2,1)S(1)}, u32[]{:S(2)}, u32[]{:S(2)}) collective-permute-start(bf16[48,640]{1,0:T(8,128)(2,1)S(1)} %constant_dynamic-update-slice_fusion.refs_0_), channel_id=1, source_target_pairs={{0,4},{1,5},{2,6},{3,7},{4,0},{5,1},{6,2},{7,3},{8,12},{9,13},{10,... | collective-permute-start | bytes 184328 | tf_op jit(solution)/shard_map/ppermute | solution.py:301
  111.5 10.5 %collective-permute-start.16 = (bf16[48,640]{1,0:T(8,128)(2,1)S(1)}, bf16[48,640]{1,0:T(8,128)(2,1)S(1)}, u32[]{:S(2)}, u32[]{:S(2)}) collective-permute-start(bf16[48,640]{1,0:T(8,128)(2,1)S(1)} %constant_dynamic-update-slice_fusion.refs_0_), channel_id=1, source_target_pairs={{0,6},{1,7},{2,4},{3,5},{4,2},{5,3},{6,0},{7,1},{8,14},{9,15},{10,... | collective-permute-start | bytes 184328 | tf_op jit(solution)/shard_map/ppermute | solution.py:301
  111.6 10.4 %collective-permute-start.17 = (bf16[48,640]{1,0:T(8,128)(2,1)S(1)}, bf16[48,640]{1,0:T(8,128)(2,1)S(1)}, u32[]{:S(2)}, u32[]{:S(2)}) collective-permute-start(bf16[48,640]{1,0:T(8,128)(2,1)S(1)} %constant_dynamic-update-slice_fusion.refs_0_), channel_id=1, source_target_pairs={{0,8},{1,9},{2,10},{3,11},{4,12},{5,13},{6,14},{7,15},{8,0},{9,1},... | collective-permute-start | bytes 184328 | tf_op jit(solution)/shard_map/ppermute | solution.py:301
  117.3 8.6 %collective-permute-start.18 = (bf16[48,640]{1,0:T(8,128)(2,1)S(1)}, bf16[48,640]{1,0:T(8,128)(2,1)S(1)}, u32[]{:S(2)}, u32[]{:S(2)}) collective-permute-start(bf16[48,640]{1,0:T(8,128)(2,1)S(1)} %constant_dynamic-update-slice_fusion.refs_0_), channel_id=1, source_target_pairs={{0,10},{1,11},{2,8},{3,9},{4,14},{5,15},{6,12},{7,13},{8,2},{9,3},... | collective-permute-start | bytes 184328 | tf_op jit(solution)/shard_map/ppermute | solution.py:301
  117.3 11.1 %copy-start.15 = (bf16[48,640]{1,0:T(8,128)(2,1)}, bf16[48,640]{1,0:T(8,128)(2,1)S(1)}, u32[]{:S(2)}) copy-start(bf16[48,640]{1,0:T(8,128)(2,1)S(1)} %collective-permute-done.14.refs_1_) | copy-start | bytes 184324
  117.3 8.8 %collective-permute-start.19 = (bf16[48,640]{1,0:T(8,128)(2,1)S(1)}, bf16[48,640]{1,0:T(8,128)(2,1)S(1)}, u32[]{:S(2)}, u32[]{:S(2)}) collective-permute-start(bf16[48,640]{1,0:T(8,128)(2,1)S(1)} %constant_dynamic-update-slice_fusion.refs_0_), channel_id=1, source_target_pairs={{0,12},{1,13},{2,14},{3,15},{4,8},{5,9},{6,10},{7,11},{8,4},{9,5},... | collective-permute-start | bytes 184328 | tf_op jit(solution)/shard_map/ppermute | solution.py:301
  121.4 7.1 %copy-start.16 = (bf16[48,640]{1,0:T(8,128)(2,1)}, bf16[48,640]{1,0:T(8,128)(2,1)S(1)}, u32[]{:S(2)}) copy-start(bf16[48,640]{1,0:T(8,128)(2,1)S(1)} %collective-permute-done.15.refs_2_) | copy-start | bytes 184324
  121.4 7.1 %collective-permute-start.20 = (bf16[48,640]{1,0:T(8,128)(2,1)S(1)}, bf16[48,640]{1,0:T(8,128)(2,1)S(1)}, u32[]{:S(2)}, u32[]{:S(2)}) collective-permute-start(bf16[48,640]{1,0:T(8,128)(2,1)S(1)} %constant_dynamic-update-slice_fusion.refs_0_), channel_id=1, source_target_pairs={{0,14},{1,15},{2,12},{3,13},{4,10},{5,11},{6,8},{7,9},{8,6},{9,7},... | collective-permute-start | bytes 184328 | tf_op jit(solution)/shard_map/ppermute | solution.py:301
  122.1 6.4 %copy-start.17 = (bf16[48,640]{1,0:T(8,128)(2,1)}, bf16[48,640]{1,0:T(8,128)(2,1)S(1)}, u32[]{:S(2)}) copy-start(bf16[48,640]{1,0:T(8,128)(2,1)S(1)} %collective-permute-done.16.refs_3_) | copy-start | bytes 184324
  122.1 6.4 %copy-start.18 = (bf16[48,640]{1,0:T(8,128)(2,1)}, bf16[48,640]{1,0:T(8,128)(2,1)S(1)}, u32[]{:S(2)}) copy-start(bf16[48,640]{1,0:T(8,128)(2,1)S(1)} %collective-permute-done.17.refs_4_) | copy-start | bytes 184324
  125.9 2.6 %copy-start.19 = (bf16[48,640]{1,0:T(8,128)(2,1)}, bf16[48,640]{1,0:T(8,128)(2,1)S(1)}, u32[]{:S(2)}) copy-start(bf16[48,640]{1,0:T(8,128)(2,1)S(1)} %collective-permute-done.18.refs_5_) | copy-start | bytes 184324
  126.2 2.3 %copy-start.20 = (bf16[48,640]{1,0:T(8,128)(2,1)}, bf16[48,640]{1,0:T(8,128)(2,1)S(1)}, u32[]{:S(2)}) copy-start(bf16[48,640]{1,0:T(8,128)(2,1)S(1)} %collective-permute-done.19.refs_6_) | copy-start | bytes 184324
  128.5 0.6 copy-start.21

commit v2 on v1

v2 whole, which is shorter than its diff:
```python
import functools
import math

import jax
import jax.numpy as jnp
from jax import lax
from jax.experimental import pallas as pl
from jax.experimental.pallas import tpu as pltpu
from jax.sharding import PartitionSpec as P

REQ = 16
HD = 128
NZ = 8
CUT = 176
SMEM = pltpu.SMEM
VMEM = pltpu.VMEM
VMEM_LIMIT = 63 * 1024 * 1024
SMALL_LIMIT = 8 * 1024 * 1024


def softmax_parts(scores, own_score, lengths):
    position = lax.broadcasted_iota(jnp.int32, scores.shape, 1)
    visible = position < lengths
    top = jnp.max(jnp.where(visible, scores, -1e30), axis=-1, keepdims=True)
    top = jnp.maximum(top, own_score)
    exponent = jnp.where(visible, jnp.exp(scores - top), 0.0)
    own_exponent = jnp.exp(own_score - top)
    denominator = jnp.sum(exponent, axis=-1, keepdims=True) + own_exponent
    weights = (exponent / denominator).astype(jnp.bfloat16).astype(jnp.float32)
    own_weight = (own_exponent / denominator).astype(jnp.bfloat16).astype(jnp.float32)
    return weights, own_weight


def heads_as_rows(wide):
    return jnp.concatenate([wide[:, :HD], wide[:, HD:]], axis=0)


def attend(query, own, kv_of, length_of, tokens):
    rows = 2 * REQ
    scale = 1.0 / math.sqrt(HD)
    heads = heads_as_rows(query)
    own_key = own[:, :HD].astype(jnp.float32)
    own_value = own[:, HD:].astype(jnp.float32)
    own_key = jnp.concatenate([own_key, own_key], axis=0)
    own_value = jnp.concatenate([own_value, own_value], axis=0)
    own_score = jnp.sum(heads.astype(jnp.float32) * own_key, axis=-1, keepdims=True) * scale
    request = lax.broadcasted_iota(jnp.int32, (rows, 1), 0) % REQ
    lengths = jnp.zeros((rows, 1), jnp.int32)
    scores = jnp.zeros((rows, tokens), jnp.float32)
    for r in range(REQ):
        lengths = jnp.where(request == r, length_of(r), lengths)
        one = lax.dot_general(
            heads, kv_of(r)[:, :HD], (((1,), (1,)), ((), ())), preferred_element_type=jnp.float32
        )
        scores = jnp.where(request == r, one, scores)
    weights, own_weight = softmax_parts(scores * scale, own_score, lengths)
    total = own_weight * own_value
    for r in range(REQ):
        mine = jnp.where(request == r, weights, 0.0).astype(jnp.bfloat16)
        total = total + jnp.dot(mine, kv_of(r)[:, HD:], preferred_element_type=jnp.float32)
    attended = total.astype(jnp.bfloat16)
    return jnp.concatenate([attended[:REQ], attended[REQ:]], axis=1)


def group_index():
    return lax.axis_index("pool") * lax.axis_size("group") + lax.axis_index("group")


def pack_kernel(pairing_in, lengths_in, own_in, new_cache, early, late, buf, own, pairing, lengths, taken, count, small_sem, in_sem, early_sem, late_sem):
    small = [
        pltpu.make_async_copy(pairing_in, pairing, small_sem.at[0]),
        pltpu.make_async_copy(lengths_in, lengths, small_sem.at[1]),
        pltpu.make_async_copy(own_in, own, small_sem.at[2]),
    ]
    for copy in small:
        copy.start()
    load = pltpu.make_async_copy(new_cache, buf.at[pl.ds(0, REQ)], in_sem)
    load.start()
    buf[REQ] = jnp.zeros(buf.shape[1:], buf.dtype)
    for j in range(2 * REQ):
        taken[j] = REQ
    for j in range(REQ):
        count[j] = 0
    for copy in small:
        copy.wait()
    for i in range(REQ):
        target = pairing[i]
        k = count[target]
        count[target] = k + 1
        taken[2 * target + k] = i
    row = lax.broadcasted_iota(jnp.int32, (16, 1), 0)
    load.wait()
    for i in range(REQ):
        base = pl.multiple_of(lengths[i] // 16 * 16, 16)
        window = buf[i, pl.ds(base, 16), :].astype(jnp.float32)
        token = own[i : i + 1, :].astype(jnp.float32)
        window = jnp.where(row == lengths[i] - base, token, window)
        buf[i, pl.ds(base, 16), :] = window.astype(buf.dtype)
    cut = early.shape[1]
    for j in range(2 * REQ):
        request = buf.at[taken[j]]
        pltpu.make_async_copy(request.at[pl.ds(0, cut)], early.at[j], early_sem).start()
    for j in range(2 * REQ):
        request = buf.at[taken[j]]
        pltpu.make_async_copy(request.at[pl.ds(cut, late.shape[1])], late.at[j], late_sem).start()
    pltpu.make_async_copy(early, early, early_sem).wait()
    pltpu.make_async_copy(late, late, late_sem).wait()


def pack(pairing, new_lengths, new_own, new_cache):
    tokens = new_cache.shape[1]
    any_space = pl.BlockSpec(memory_space=pltpu.HBM)
    return pl.pallas_call(
        pack_kernel,
        out_shape=[
            jax.ShapeDtypeStruct((2 * REQ, CUT, 2 * HD), jnp.bfloat16),
            jax.ShapeDtypeStruct((2 * REQ, tokens - CUT, 2 * HD), jnp.bfloat16),
        ],
        in_specs=[any_space] * 4,
        out_specs=[any_space] * 2,
        scratch_shapes=[
            VMEM((REQ + 1, tokens, 2 * HD), jnp.bfloat16),
            VMEM(new_own.shape, jnp.bfloat16),
            SMEM((REQ,), jnp.int32),
            SMEM((REQ,), jnp.int32),
            SMEM((2 * REQ,), jnp.int32),
            SMEM((REQ,), jnp.int32),
            pltpu.SemaphoreType.DMA((3,)),
            pltpu.SemaphoreType.DMA,
            pltpu.SemaphoreType.DMA,
            pltpu.SemaphoreType.DMA,
        ],
        compiler_params=pltpu.CompilerParams(vmem_limit_bytes=VMEM_LIMIT),
        cost_estimate=pl.CostEstimate(flops=1_000_000, bytes_accessed=6_400_000, transcendentals=0),
        name="pack",
    )(pairing, new_lengths, new_own, new_cache)


def front_kernel(*refs):
    ins, refs = refs[:13], refs[13:]
    first, one_up, one_down, two_up, two_down, opposite, chosen = refs[:7]
    refs = refs[7:]
    bufs, (count, table_sem, small_sem, new_sem, kv_sem, weight_sem) = refs[:13], refs[13:]
    pairing, lengths, table, new_lengths, query, own, new_query, new_own, resid, new_resid, weight, new_buf, kv_buf = bufs
    new_cache, cache = ins[11], ins[12]
    z, x_lo = lax.axis_index("tp") // 2, lax.axis_index("tp") % 2
    width = weight.shape[1] // NZ

    table_copy = pltpu.make_async_copy(ins[2], table, table_sem)
    table_copy.start()
    small = [pltpu.make_async_copy(ins[n], bufs[n], small_sem.at[n]) for n in range(10) if n != 2]
    new_copy = pltpu.make_async_copy(new_cache, new_buf, new_sem)
    weight_copy = pltpu.make_async_copy(ins[10], weight, weight_sem)
    for copy in small:
        copy.start()
    new_copy.start()
    table_copy.wait()
    for e in range(4 * REQ):
        pltpu.make_async_copy(cache.at[table[e]], kv_buf.at[e], kv_sem).start()
    weight_copy.start()
    for copy in small:
        copy.wait()
    new_copy.wait()

    new_rows = attend(
        new_query[...],
        new_own[...],
        lambda r: new_buf[r],
        lambda r: new_lengths[r],
        new_buf.shape[1],
    )

    pltpu.make_async_copy(cache, kv_buf, kv_sem).wait()
    rows = attend(
        query[...],
        own[...],
        lambda r: kv_buf[4 * r : 4 * r + 4].reshape(4 * kv_buf.shape[1], 2 * HD),
        lambda r: lengths[r],
        4 * kv_buf.shape[1],
    )
    attended = jnp.concatenate([rows, new_rows], axis=0)
    weight_copy.wait()

    def block_of(shift):
        return pl.ds(pl.multiple_of((z + shift + NZ) % NZ * width, 128), width)

    def part(shift):
        return jnp.dot(attended, weight[:, block_of(shift)], preferred_element_type=jnp.float32)

    two_up[: 2 * REQ] = part(2).astype(jnp.bfloat16)
    two_up[2 * REQ :] = part(3).astype(jnp.bfloat16)
    two_down[: 2 * REQ] = part(-2).astype(jnp.bfloat16)
    two_down[2 * REQ :] = part(-3).astype(jnp.bfloat16)
    opposite[...] = part(4).astype(jnp.bfloat16)
    one_up[...] = part(1)
    one_down[...] = part(-1)
    columns = block_of(0)
    block = jnp.concatenate([resid[:, columns], new_resid[:, columns]], axis=0)
    first[...] = part(0) + jnp.where(x_lo == 0, block.astype(jnp.float32), 0.0)

    me = group_index()
    for j in range(REQ):
        count[j] = 0
    row = lax.broadcasted_iota(jnp.int32, (2 * REQ, REQ), 0)
    column = lax.broadcasted_iota(jnp.int32, (2 * REQ, REQ), 1)
    target_row = jnp.zeros((2 * REQ, REQ), jnp.int32)
    for i in range(REQ):
        target = pairing[i]
        k = count[target]
        count[target] = k + 1
        target_row = jnp.where(column == i, (me ^ target) * 2 + k, target_row)
    chosen[...] = jnp.where(row == target_row, 1.0, 0.0).astype(jnp.bfloat16)


def front(*args):
    pairing, lengths, table, new_lengths, query, own, new_query, new_own, resid, new_resid, weight, new_cache, cache = args
    width = weight.shape[1] // NZ
    any_space = pl.BlockSpec(memory_space=pltpu.HBM)
    vmem = pl.BlockSpec(memory_space=VMEM)
    return pl.pallas_call(
        front_kernel,
        out_shape=[jax.ShapeDtypeStruct((2 * REQ, width), jnp.float32)] * 3
        + [jax.ShapeDtypeStruct((4 * REQ, width), jnp.bfloat16)] * 2
        + [jax.ShapeDtypeStruct((2 * REQ, width), jnp.bfloat16)]
        + [jax.ShapeDtypeStruct((2 * REQ, REQ), jnp.bfloat16)],
        in_specs=[any_space] * 13,
        out_specs=[vmem] * 7,
        scratch_shapes=[SMEM(array.shape, array.dtype) for array in args[:4]]
        + [VMEM(array.shape, array.dtype) for array in args[4:12]]
        + [
            VMEM(cache.shape, jnp.bfloat16),
            SMEM((REQ,), jnp.int32),
            pltpu.SemaphoreType.DMA,
            pltpu.SemaphoreType.DMA((10,)),
            pltpu.SemaphoreType.DMA,
            pltpu.SemaphoreType.DMA,
            pltpu.SemaphoreType.DMA,
        ],
        compiler_params=pltpu.CompilerParams(vmem_limit_bytes=VMEM_LIMIT - 2560 * 1024),
        cost_estimate=pl.CostEstimate(
            flops=400_000_000, bytes_accessed=9_500_000, transcendentals=30_000
        ),
        name="front",
    )(*args)


def spread_kernel(first, *refs):
    *parts, chosen, near, far = refs
    total = first[...]
    for part in parts:
        total = total + part[: 2 * REQ].astype(jnp.float32)
    half = total.astype(jnp.bfloat16)
    placed = jnp.dot(chosen[...], half[REQ:], preferred_element_type=jnp.float32)
    placed = placed.astype(jnp.bfloat16)
    near[:REQ] = half[:REQ]
    near[REQ:] = placed[:REQ]
    far[...] = placed[REQ:]


def finish_kernel(gain, *refs):
    *blocks, hidden, normed = refs
    z, me = lax.axis_index("tp") // 2, group_index()
    rows, width = blocks[0].shape
    slots = rows - REQ
    slot = lax.broadcasted_iota(jnp.int32, (slots, slots), 0)
    column = lax.broadcasted_iota(jnp.int32, (slots, slots), 1)
    offset = (slot >> 1) ^ me
    at = (offset & 1) * 16 + ((offset >> 1) & 3) * 4 + (offset >> 3) * 2 + (slot & 1)
    order = jnp.where(column == at, 1.0, 0.0).astype(jnp.bfloat16)
    square = jnp.zeros((rows, 1), jnp.float32)
    places = [(0, 0, 0), (1, 0, -1), (2, 0, 1), (3, 0, 4), (4, 0, -2), (4, 1, -3), (5, 0, 2), (5, 1, 3)]
    for n, part, shift in places:
        columns = pl.ds(pl.multiple_of((z + shift + NZ) % NZ * width, 128), width)
        block = blocks[n][rows * part : rows * (part + 1)]
        placed = jnp.dot(order, block[REQ:], preferred_element_type=jnp.float32)
        wide = jnp.concatenate([block[:REQ].astype(jnp.float32), placed], axis=0)
        hidden[:, columns] = wide.astype(jnp.bfloat16)
        square = square + jnp.sum(wide * wide, axis=-1, keepdims=True)
    inverse = lax.rsqrt(square / (width * NZ) + 1e-06)
    for k in range(NZ):
        columns = slice(k * width, (k + 1) * width)
        wide = hidden[:, columns].astype(jnp.float32)
        normed[:, columns] = (wide * inverse * gain[:, columns].astype(jnp.float32)).astype(
            jnp.bfloat16
        )


def place_kernel(start, part, *refs):
    whole, buf, in_sem, out_sem = refs[-4:]
    size = part.shape[0] // 4
    for n in range(4):
        rows = pl.ds(n * size, size)
        pltpu.make_async_copy(part.at[rows], buf.at[rows], in_sem.at[n]).start()
    for n in range(4):
        rows = pl.ds(n * size, size)
        pltpu.make_async_copy(part.at[rows], buf.at[rows], in_sem.at[n]).wait()
        target = whole.at[rows, pl.ds(start, part.shape[1])]
        pltpu.make_async_copy(buf.at[rows], target, out_sem.at[n]).start()
    for n in range(4):
        rows = pl.ds(n * size, size)
        target = whole.at[rows, pl.ds(start, part.shape[1])]
        pltpu.make_async_copy(buf.at[rows], target, out_sem.at[n]).wait()


def place(part, start, whole):
    given = [part] if isinstance(whole, tuple) else [part, whole]
    shape = whole if isinstance(whole, tuple) else whole.shape
    any_space = pl.BlockSpec(memory_space=pltpu.HBM)
    return pl.pallas_call(
        functools.partial(place_kernel, start),
        out_shape=jax.ShapeDtypeStruct(shape, part.dtype),
        in_specs=[any_space] * len(given),
        out_specs=any_space,
        scratch_shapes=[
            VMEM(part.shape, part.dtype),
            pltpu.SemaphoreType.DMA((4,)),
            pltpu.SemaphoreType.DMA((4,)),
        ],
        compiler_params=pltpu.CompilerParams(vmem_limit_bytes=SMALL_LIMIT),
        input_output_aliases={} if len(given) == 1 else {1: 0},
        cost_estimate=pl.CostEstimate(flops=0, bytes_accessed=2 * part.size * 2, transcendentals=0),
        name="place",
    )(*given)


def body(
    cache,
    table,
    lengths,
    query,
    step_kv,
    resid,
    new_cache,
    new_lengths,
    new_query,
    new_step_kv,
    new_resid,
    pairing,
    o_weight,
    norm_gain,
):
    pools, groups = lax.axis_size("pool"), lax.axis_size("pool") * lax.axis_size("group")
    ranks = lax.axis_size("tp")
    pair = pairing[0, 0, :, 0]
    prompts = new_cache[0, 0, :, :, 0]
    vmem = pl.BlockSpec(memory_space=VMEM)
    both = ("pool", "group")

    def over_tp(array, flip):
        return lax.ppermute(array, "tp", [(t, t ^ flip) for t in range(ranks)])

    def round_z(array, shift):
        return lax.ppermute(array, "tp", [(t, (t + 2 * shift) % ranks) for t in range(ranks)])

    def over_groups(array, flip):
        return lax.ppermute(array, both, [(s, s ^ flip) for s in range(groups)])

    def deliver(array):
        blocks = array.reshape((groups, 2) + array.shape[1:])
        return lax.all_to_all(blocks, both, split_axis=0, concat_axis=0, tiled=True).reshape(array.shape)

    early, late = pack(pair, new_lengths[0, 0], new_step_kv[0, 0, :, 0], prompts)
    early = deliver(early)

    first, one_up, one_down, two_up, two_down, opposite, chosen = front(
        pair,
        lengths[0, 0],
        table[0, 0],
        new_lengths[0, 0],
        query[0, 0],
        step_kv[0, 0, :, 0],
        new_query[0, 0],
        new_step_kv[0, 0, :, 0],
        resid[0, 0],
        new_resid[0, 0],
        o_weight,
        prompts,
        cache[0, 0, :, :, 0],
    )
    from_below, from_above = round_z(two_up, 2), round_z(two_down, -2)
    opposite = round_z(opposite, 4)
    gain = norm_gain.reshape(1, -1)
    from_below, from_above, opposite, gain = lax.optimization_barrier(
        (from_below, from_above, opposite, gain)
    )
    one_up = (one_up + from_below[2 * REQ :].astype(jnp.float32)).astype(jnp.bfloat16)
    one_down = (one_down + from_above[2 * REQ :].astype(jnp.float32)).astype(jnp.bfloat16)
    parts = [from_below, from_above, opposite, round_z(one_up, 1), round_z(one_down, -1)]
    width = first.shape[1]
    near, far = pl.pallas_call(
        spread_kernel,
        out_shape=[
            jax.ShapeDtypeStruct((2 * REQ, width), jnp.bfloat16),
            jax.ShapeDtypeStruct((REQ, width), jnp.bfloat16),
        ],
        in_specs=[vmem] * (len(parts) + 2),
        out_specs=[vmem] * 2,
        compiler_params=pltpu.CompilerParams(vmem_limit_bytes=SMALL_LIMIT),
        name="spread",
    )(first, *parts, chosen)

    across = [(n, n ^ (ranks + 1)) for n in range(pools * ranks)]
    far_here = over_groups(far, groups // 2)
    far_there = lax.ppermute(far, ("pool", "tp"), across)
    near_there = over_tp(near, 1)
    near = (near.astype(jnp.float32) + near_there.astype(jnp.float32)).astype(jnp.bfloat16)
    far = (far_here.astype(jnp.float32) + far_there.astype(jnp.float32)).astype(jnp.bfloat16)
    toward = [
        jnp.concatenate([near[REQ + 4 * y : REQ + 4 * y + 4], far[4 * y : 4 * y + 4]], axis=0)
        for y in range(4)
    ]
    slots = [toward[0]] + [over_groups(toward[y], 2 * y) for y in range(1, 4)]
    late, *slots = lax.optimization_barrier((late, *slots))
    late = deliver(late)
    slots = jnp.stack(slots).reshape(4, 2, 2, 2, width)
    kept, given = (slots[:, :, c].reshape(REQ, width) for c in range(2))
    block = jnp.concatenate([near[:REQ], kept, over_groups(given, 1)], axis=0)

    slot_cache = place(early, 0, (2 * REQ,) + prompts.shape[1:])
    below, above, opposite, slot_cache = lax.optimization_barrier(
        (round_z(block, 1), round_z(block, -1), round_z(block, 4), slot_cache)
    )
    two_below = round_z(jnp.concatenate([block, below], axis=0), 2)
    two_above = round_z(jnp.concatenate([block, above], axis=0), -2)
    blocks = [block, below, above, opposite, two_below, two_above]
    hidden, normed = pl.pallas_call(
        finish_kernel,
        out_shape=[jax.ShapeDtypeStruct((block.shape[0], width * NZ), jnp.bfloat16)] * 2,
        in_specs=[vmem] * (len(blocks) + 1),
        out_specs=[vmem] * 2,
        compiler_params=pltpu.CompilerParams(vmem_limit_bytes=SMALL_LIMIT),
        name="finish",
    )(gain, *blocks)

    slot_cache = place(late, CUT, slot_cache)
    return (hidden[None, None], normed[None, None], slot_cache[None, None, :, :, None, :])


def solution(mesh):
    placed = (
        P("pool", "group", None, None, "tp", None),
        P("pool", "group", None),
        P("pool", "group", None),
        P("pool", "group", None, "tp"),
        P("pool", "group", None, "tp", None),
        P("pool", "group", None, None),
        P("pool", "group", None, None, "tp", None),
        P("pool", "group", None),
        P("pool", "group", None, "tp"),
        P("pool", "group", None, "tp", None),
        P("pool", "group", None, None),
        P("pool", "group", None, None),
        P("tp", None),
        P(),
    )
    return jax.shard_map(
        body,
        mesh=mesh,
        in_specs=placed,
        out_specs=(
            P("pool", "group", None, None),
            P("pool", "group", None, None),
            P("pool", "group", None, None, "tp", None),
        ),
        check_vma=False,
    )
```

time: 137 us -> 94.6 us (0.69)
  waiting for transfers between devices: 50 us -> 19.2 us
  local copies, waits for them, and re-layouts: 19.9 us -> 1.8 us
  starting transfers between devices: 50.3 us -> 54 us
  other arithmetic: 0.14 us -> 1.9 us
    ppermute x15 -> x1, waiting for transfers between devices: 45.2 us -> 0.04 us  [over_tp(): return lax.ppermute(array, 'tp', [(t, t ^ flip) for t in range(ranks)])]
    ppermute x15 -> x1, starting transfers between devices: 29.5 us -> 0.3 us  [over_tp(): return lax.ppermute(array, 'tp', [(t, t ^ flip) for t in range(ranks)])]
    ppermute x0 -> x11, starting transfers between devices: none -> 27.2 us  [the longest x10 27.2 us: round_z(): lax.ppermute(array, 'tp', [(t, (t + 2 * shift) % ranks) for t in range(ra...]
    unnamed x67 -> x10, local copies, waits for them, and re-layouts: 18.5 us -> 1.66 us
    ppermute x0 -> x11, waiting for transfers between devices: none -> 9.65 us  [the longest x10 8.89 us: round_z(): lax.ppermute(array, 'tp', [(t, (t + 2 * shift) % ranks) for t in range(ra...]
    all_to_all x1 -> x2, starting transfers between devices: 8.58 us -> 16.4 us  [deliver(): lax.all_to_all(blocks, both, split_axis=0, concat_axis=0, tiled=True)]
    ppermute x6 -> x5, waiting for transfers between devices: 4.76 us -> 7.62 us  [over_groups(): return lax.ppermute(array, both, [(s, s ^ flip) for s in range(groups)])]
    ppermute x6 -> x5, starting transfers between devices: 12.2 us -> 10 us  [over_groups(): return lax.ppermute(array, both, [(s, s ^ flip) for s in range(groups)])]
  transfers between devices with their start and end apart: 22 -> 19, of which waited for: 8 -> 11; matrix products, arithmetic and copies ran while one was open for 2% -> 2% of each run, Pallas kernels for 4% -> 11%
where the time goes in v2:
time: 94.6 us; the launch traced here: 93.2 us
  starting transfers between devices  54 us (57%)
  waiting for transfers between devices  19.2 us (20%)
  Pallas kernels  15.6 us (16%)
  other arithmetic  1.9 us (2%)
  local copies, waits for them, and re-layouts  1.8 us (2%)
    ppermute x10, starting transfers between devices, round_z(): lax.ppermute(array, 'tp', [(t, (t + 2 * shift) % ranks) for t in range(ra...  27.2 us
    all_to_all x2, starting transfers between devices, deliver(): lax.all_to_all(blocks, both, split_axis=0, concat_axis=0, tiled=True)  16.4 us
    ppermute x5, starting transfers between devices, over_groups(): return lax.ppermute(array, both, [(s, s ^ flip) for s in range(groups)])  10 us
    ppermute x10, waiting for transfers between devices, round_z(): lax.ppermute(array, 'tp', [(t, (t + 2 * shift) % ranks) for t in range(ra...  8.89 us
    ppermute x5, waiting for transfers between devices, over_groups(): return lax.ppermute(array, both, [(s, s ^ flip) for s in range(groups)])  7.62 us
    pallas_call x1, Pallas kernels, front(): pl.pallas_call(front_kernel, out_shape=[jax.ShapeDtypeStruct((2 * REQ, wi...  5.66 us
    pallas_call x2, Pallas kernels, place(): pl.pallas_call(functools.partial(place_kernel, start), out_shape=jax.Shap...  4.88 us
    pallas_call x1, Pallas kernels, pack(): pl.pallas_call(pack_kernel, out_shape=[jax.ShapeDtypeStruct((2 * REQ, CUT...  3.71 us
  transfers between devices with their start and end apart: 19, of which 11 were waited for; matrix products, arithmetic and copies ran while one was open for 2% of the time, Pallas kernels for 11%

profile of v2, /device:TPU:1, one launch (start us, length us, event | category | flops | bytes accessed | tf_op | source)
XLA Modules:
  0.0 93.2 jit_solution(17143471863445882497)
XLA Ops:
  0.6 3.7 %pack.1 = (bf16[32,176,256]{2,1,0:T(8,128)(2,1)}, bf16[32,80,256]{2,1,0:T(8,128)(2,1)}) custom-call(s32[16]{0:T(128)} %bitcast.43, s32[16]{0:T(128)} %bitcast.45, bf16[16,256]{1,0:T(8,128)(2,1)} %bitcast.38, bf16[16,256,256]{2,1,0:T(8,128)(2,1)} %bitcast.31), custom_call_target="tpu_custom_call" | custom-call | flops 1000000 | bytes 6400000 | tf_op jit(solution)/shard_map/pack/pallas_call | solution.py:113
  4.3 8.5 %all-to-all-start = ((bf16[16,2,176,256]{3,2,1,0:T(8,128)(2,1)}), bf16[16,2,176,256]{3,2,1,0:T(8,128)(2,1)S(1)}, u32[]{:S(2)}, u32[]{:S(2)}) async-start(bf16[16,2,176,256]{3,2,1,0:T(8,128)(2,1)} %bitcast.34), calls=%async_computation | async-start | bytes 5767168 | tf_op jit(solution)/shard_map/all_to_all | solution.py:360
  12.8 0.0 copy-start.2
  12.8 5.7 %front.1 = (f32[32,640]{1,0:T(8,128)}, f32[32,640]{1,0:T(8,128)}, f32[32,640]{1,0:T(8,128)}, bf16[64,640]{1,0:T(8,128)(2,1)}, bf16[64,640]{1,0:T(8,128)(2,1)}, /...) custom-call(s32[16]{0:T(128)} %bitcast.44, s32[16]{0:T(128)} %bitcast.47, s32[64]{0:T(128)} %bitcast.48, s32[16]{0:T(128)} %bitcast.46, ...), custom_call_target="tpu_custom_call" | custom-call | flops 400000000 | bytes 9500000 | tf_op jit(solution)/shard_map/front/pallas_call | solution.py:220
  18.5 3.1 %collective-permute-start = (bf16[64,640]{1,0:T(8,128)(2,1)}, bf16[64,640]{1,0:T(8,128)(2,1)S(1)}, u32[]{:S(2)}, u32[]{:S(2)}) collective-permute-start(bf16[64,640]{1,0:T(8,128)(2,1)} %get-tuple-element.29), channel_id=1, source_target_pairs={{0,4},{1,5},{2,6},{3,7},{4,8},{5,9},{6,10},{7,11},{8,12},{9,13},{1... | collective-permute-start | bytes 245768 | tf_op jit(solution)/shard_map/ppermute | solution.py:353
  21.6 3.1 %collective-permute-start.1 = (bf16[64,640]{1,0:T(8,128)(2,1)}, bf16[64,640]{1,0:T(8,128)(2,1)S(1)}, u32[]{:S(2)}, u32[]{:S(2)}) collective-permute-start(bf16[64,640]{1,0:T(8,128)(2,1)} %get-tuple-element.30), channel_id=1, source_target_pairs={{0,12},{1,13},{2,14},{3,15},{4,0},{5,1},{6,2},{7,3},{8,4},{9,5},{1... | collective-permute-start | bytes 245768 | tf_op jit(solution)/shard_map/ppermute | solution.py:353
  24.7 4.4 %collective-permute-start.2 = (bf16[32,640]{1,0:T(8,128)(2,1)}, bf16[32,640]{1,0:T(8,128)(2,1)S(1)}, u32[]{:S(2)}, u32[]{:S(2)}) collective-permute-start(bf16[32,640]{1,0:T(8,128)(2,1)} %get-tuple-element.31), channel_id=1, source_target_pairs={{0,8},{1,9},{2,10},{3,11},{4,12},{5,13},{6,14},{7,15},{8,0},{9,1},... | collective-permute-start | bytes 122888 | tf_op jit(solution)/shard_map/ppermute | solution.py:353
  29.1 0.0 copy-done.2
  29.1 3.0 %collective-permute-done.2.refs_2_ = bf16[32,640]{1,0:T(8,128)(2,1)S(1)} collective-permute-done((bf16[32,640]{1,0:T(8,128)(2,1)}, bf16[32,640]{1,0:T(8,128)(2,1)S(1)}, u32[]{:S(2)}, u32[]{:S(2)}) %collective-permute-start.2) | collective-permute-done | bytes 40992 | tf_op jit(solution)/shard_map/ppermute | solution.py:353
  32.1 0.0 collective-permute-done.refs_0_
  32.1 0.0 collective-permute-done.1.refs_1_
  32.1 0.9 add_convert_fusion.2
  33.0 3.2 %collective-permute-start.3 = (bf16[32,640]{1,0:T(8,128)(2,1)S(1)}, bf16[32,640]{1,0:T(8,128)(2,1)S(1)}, u32[]{:S(2)}, u32[]{:S(2)}) collective-permute-start(bf16[32,640]{1,0:T(8,128)(2,1)S(1)} %add_convert_fusion.2), channel_id=1, source_target_pairs={{0,2},{1,3},{2,4},{3,5},{4,6},{5,7},{6,8},{7,9},{8,10},{9,11},{10,... | collective-permute-start | bytes 122888 | tf_op jit(solution)/shard_map/ppermute | solution.py:353
  36.2 0.9 add_convert_fusion.1
  37.1 0.1 collective-permute-start.4
  37.2 0.3 collective-permute-done.3.refs_3_
  37.5 2.9 %collective-permute-done.4.refs_4_ = bf16[32,640]{1,0:T(8,128)(2,1)S(1)} collective-permute-done((bf16[32,640]{1,0:T(8,128)(2,1)S(1)}, bf16[32,640]{1,0:T(8,128)(2,1)S(1)}, u32[]{:S(2)}, u32[]{:S(2)}) %collective-permute-start.4) | collective-permute-done | bytes 40992 | tf_op jit(solution)/shard_map/ppermute | solution.py:353
  40.3 0.0 copy-start
  40.3 0.9 copy-done
  41.2 0.0 copy-start.1
  41.2 0.7 copy-done.1
  41.9 0.1 spread.1
  42.1 2.9 %collective-permute-start.6 = (bf16[16,640]{1,0:T(8,128)(2,1)S(1)}, bf16[16,640]{1,0:T(8,128)(2,1)S(1)}, u32[]{:S(2)}, u32[]{:S(2)}) collective-permute-start(bf16[16,640]{1,0:T(8,128)(2,1)S(1)} %get-tuple-element.42), channel_id=1, source_target_pairs={{0,128},{16,144},{32,160},{48,176},{64,192},{80,208},{96,224},{112... | collective-permute-start | bytes 61448 | tf_op jit(solution)/shard_map/ppermute | solution.py:356
  45.0 0.0 collective-permute-start.7
  45.0 0.3 collective-permute-start.5
  45.3 3.8 %collective-permute-done.6 = bf16[16,640]{1,0:T(8,128)(2,1)S(1)} collective-permute-done((bf16[16,640]{1,0:T(8,128)(2,1)S(1)}, bf16[16,640]{1,0:T(8,128)(2,1)S(1)}, u32[]{:S(2)}, u32[]{:S(2)}) %collective-permute-start.6) | collective-permute-done | bytes 20512 | tf_op jit(solution)/shard_map/ppermute | solution.py:356
  49.1 0.8 collective-permute-done.7
  49.9 0.0 collective-permute-done.5
  50.0 2.2 %collective-permute-start.10 = (bf16[8,640]{1,0:T(8,128)(2,1)S(1)}, bf16[8,640]{1,0:T(8,128)(2,1)S(1)}, u32[]{:S(2)}, u32[]{:S(2)}) collective-permute-start(bf16[8,640]{1,0:T(8,128)(2,1)S(1)} %pad_maximum_fusion.7), channel_id=1, source_target_pairs={{0,96},{16,112},{32,64},{48,80},{64,32},{80,48},{96,0},{112,16},{1... | collective-permute-start | bytes 30728 | tf_op jit(solution)/shard_map/ppermute | solution.py:356
  52.2 4.6 %collective-permute-start.9 = (bf16[8,640]{1,0:T(8,128)(2,1)S(1)}, bf16[8,640]{1,0:T(8,128)(2,1)S(1)}, u32[]{:S(2)}, u32[]{:S(2)}) collective-permute-start(bf16[8,640]{1,0:T(8,128)(2,1)S(1)} %pad_maximum_fusion.6), channel_id=1, source_target_pairs={{0,64},{16,80},{32,96},{48,112},{64,0},{80,16},{96,32},{112,48},{1... | collective-permute-start | bytes 30728 | tf_op jit(solution)/shard_map/ppermute | solution.py:356
  56.8 0.1 collective-permute-start.8
  56.9 0.0 collective-permute-done.10
  56.9 0.9 collective-permute-done.9
  57.9 1.9 %collective-permute-done.8 = bf16[8,640]{1,0:T(8,128)(2,1)S(1)} collective-permute-done((bf16[8,640]{1,0:T(8,128)(2,1)S(1)}, bf16[8,640]{1,0:T(8,128)(2,1)S(1)}, u32[]{:S(2)}, u32[]{:S(2)}) %collective-permute-start.8) | collective-permute-done | bytes 10272 | tf_op jit(solution)/shard_map/ppermute | solution.py:356
  59.7 0.0 all-to-all-done
  59.7 8.0 %all-to-all-start.1 = ((bf16[16,2,80,256]{3,2,1,0:T(8,128)(2,1)}), bf16[16,2,80,256]{3,2,1,0:T(8,128)(2,1)}, u32[]{:S(2)}, u32[]{:S(2)}) async-start(bf16[16,2,80,256]{3,2,1,0:T(8,128)(2,1)} %bitcast.35), calls=%async_computation.1 | async-start | bytes 2621440 | tf_op jit(solution)/shard_map/all_to_all | solution.py:360
  67.9 0.2 collective-permute-start.11
  68.2 1.0 %collective-permute-done.11 = bf16[16,640]{1,0:T(8,128)(2,1)S(1)} collective-permute-done((bf16[16,640]{1,0:T(8,128)(2,1)S(1)}, bf16[16,640]{1,0:T(8,128)(2,1)S(1)}, u32[]{:S(2)}, u32[]{:S(2)}) %collective-permute-start.11) | collective-permute-done | bytes 20512 | tf_op jit(solution)/shard_map/ppermute | solution.py:356
  69.2 1.6 %collective-permute-start.12 = (bf16[48,640]{1,0:T(8,128)(2,1)S(1)}, bf16[48,640]{1,0:T(8,128)(2,1)S(1)}, u32[]{:S(2)}, u32[]{:S(2)}) collective-permute-start(bf16[48,640]{1,0:T(8,128)(2,1)S(1)} %pad_maximum_fusion.3.refs_0_), channel_id=1, source_target_pairs={{0,2},{1,3},{2,4},{3,5},{4,6},{5,7},{6,8},{7,9},{8,10},{9,11},{10,... | collective-permute-start | bytes 184328 | tf_op jit(solution)/shard_map/ppermute | solution.py:353
  70.8 4.1 %collective-permute-start.13 = (bf16[48,640]{1,0:T(8,128)(2,1)S(1)}, bf16[48,640]{1,0:T(8,128)(2,1)S(1)}, u32[]{:S(2)}, u32[]{:S(2)}) collective-permute-start(bf16[48,640]{1,0:T(8,128)(2,1)S(1)} %pad_maximum_fusion.3.refs_0_), channel_id=1, source_target_pairs={{0,14},{1,15},{2,0},{3,1},{4,2},{5,3},{6,4},{7,5},{8,6},{9,7},{10,... | collective-permute-start | bytes 184328 | tf_op jit(solution)/shard_map/ppermute | solution.py:353
  74.9 3.9 %collective-permute-start.14 = (bf16[48,640]{1,0:T(8,128)(2,1)S(1)}, bf16[48,640]{1,0:T(8,128)(2,1)S(1)}, u32[]{:S(2)}, u32[]{:S(2)}) collective-permute-start(bf16[48,640]{1,0:T(8,128)(2,1)S(1)} %pad_maximum_fusion.3.refs_0_), channel_id=1, source_target_pairs={{0,8},{1,9},{2,10},{3,11},{4,12},{5,13},{6,14},{7,15},{8,0},{9,1},... | collective-permute-start | bytes 184328 | tf_op jit(solution)/shard_map/ppermute | solution.py:353
  78.9 2.8 %place.2.refs_0_ = bf16[32,256,256]{2,1,0:T(8,128)(2,1)} custom-call(bf16[32,176,256]{2,1,0:T(8,128)(2,1)S(1)} %bitcast.29), custom_call_target="tpu_custom_call" | custom-call | bytes 5767168 | tf_op jit(solution)/shard_map/place/pallas_call | solution.py:309
  81.7 0.0 collective-permute-done.12.refs_1_
  81.7 0.0 collective-permute-done.13.refs_2_
  81.7 0.6 collective-permute-done.14.refs_3_
  82.3 0.1 collective-permute-start.15
  82.4 3.6 %collective-permute-start.16 = (bf16[96,640]{1,0:T(8,128)(2,1)S(1)}, bf16[96,640]{1,0:T(8,128)(2,1)S(1)}, u32[]{:S(2)}, u32[]{:S(2)}) collective-permute-start(bf16[96,640]{1,0:T(8,128)(2,1)S(1)} %get-tuple-element.58), channel_id=1, source_target_pairs={{0,12},{1,13},{2,14},{3,15},{4,0},{5,1},{6,2},{7,3},{8,4},{9,5},{1... | collective-permute-start | bytes 368648 | tf_op jit(solution)/shard_map/ppermute | solution.py:353
  86.0 1.9 %all-to-all-done.1 = bf16[16,2,80,256]{3,2,1,0:T(8,128)(2,1)} async-done(((bf16[16,2,80,256]{3,2,1,0:T(8,128)(2,1)}), bf16[16,2,80,256]{3,2,1,0:T(8,128)(2,1)}, u32[]{:S(2)}, u32[]{:S(2)}) %all-to-all-start.1) | async-done | bytes 1310752 | tf_op jit(solution)/shard_map/all_to_all | solution.py:360
  87.9 2.1 %place.3 = bf16[32,256,256]{2,1,0:T(8,128)(2,1)} custom-call(bf16[32,80,256]{2,1,0:T(8,128)(2,1)} %bitcast.17.part, bf16[32,256,256]{2,1,0:T(8,128)(2,1)} %place.2.refs_0_), custom_call_target="tpu_custom_call", output_to_operand_aliasing={{}: (1, {})} | custom-call | bytes 2621440 | tf_op jit(solution)/shard_map/place/pallas_call | solution.py:309
  89.9 0.0 collective-permute-done.15.refs_4_
  90.0 2.1 %collective-permute-done.16.refs_5_ = bf16[96,640]{1,0:T(8,128)(2,1)S(1)} collective-permute-done((bf16[96,640]{1,0:T(8,128)(2,1)S(1)}, bf16[96,640]{1,0:T(8,128)(2,1)S(1)}, u32[]{:S(2)}, u32[]{:S(2)}) %collective-permute-start.16) | collective-permute-done | bytes 122912 | tf_op jit(solution)/shard_map/ppermute | solution.py:353
  92.0 1.2 %finish.1 = (bf16[48,5120]{1,0:T(8,128)(2,1)}, bf16[48,5120]{1,0:T(8,128)(2,1)}) custom-call(bf16[1,5120]{1,0:T(2,128)(2,1)S(1)} %reshape.30.gain, bf16[48,640]{1,0:T(8,128)(2,1)S(1)} %pad_maximum_fusion.3.refs_0_, bf16[48,640]{1,0:T(8,128)(2,1)S(1)} %collective-permute-done.12.refs_1_, bf16[48,640]{1,0:T(8,128)(2,1)S(1)} %collective-permute-done.13.refs_2_, ...), custom_call_target="tpu_custom_call" | custom-call | tf_op jit(solution)/shard_map/finish/pallas_call | solution.py:426
  (23 shorter events, 0.3 us)
Async XLA Ops:
  4.3 55.4 %all-to-all-start = ((bf16[16,2,176,256]{3,2,1,0:T(8,128)(2,1)}), bf16[16,2,176,256]{3,2,1,0:T(8,128)(2,1)S(1)}, u32[]{:S(2)}, u32[]{:S(2)}) async-start(bf16[16,2,176,256]{3,2,1,0:T(8,128)(2,1)} %bitcast.34), calls=%async_computation | async-start | bytes 5767168 | tf_op jit(solution)/shard_map/all_to_all | solution.py:360
  12.8 16.3 %copy-start.2 = (bf16[5120]{0:T(1024)(128)(2,1)S(1)}, bf16[5120]{0:T(1024)(128)(2,1)}, u32[]{:S(2)}) copy-start(bf16[5120]{0:T(1024)(128)(2,1)} %param.27) | copy-start | bytes 30724
  18.5 13.7 %collective-permute-start = (bf16[64,640]{1,0:T(8,128)(2,1)}, bf16[64,640]{1,0:T(8,128)(2,1)S(1)}, u32[]{:S(2)}, u32[]{:S(2)}) collective-permute-start(bf16[64,640]{1,0:T(8,128)(2,1)} %get-tuple-element.29), channel_id=1, source_target_pairs={{0,4},{1,5},{2,6},{3,7},{4,8},{5,9},{6,10},{7,11},{8,12},{9,13},{1... | collective-permute-start | bytes 245768 | tf_op jit(solution)/shard_map/ppermute | solution.py:353
  21.6 10.6 %collective-permute-start.1 = (bf16[64,640]{1,0:T(8,128)(2,1)}, bf16[64,640]{1,0:T(8,128)(2,1)S(1)}, u32[]{:S(2)}, u32[]{:S(2)}) collective-permute-start(bf16[64,640]{1,0:T(8,128)(2,1)} %get-tuple-element.30), channel_id=1, source_target_pairs={{0,12},{1,13},{2,14},{3,15},{4,0},{5,1},{6,2},{7,3},{8,4},{9,5},{1... | collective-permute-start | bytes 245768 | tf_op jit(solution)/shard_map/ppermute | solution.py:353
  24.7 7.4 %collective-permute-start.2 = (bf16[32,640]{1,0:T(8,128)(2,1)}, bf16[32,640]{1,0:T(8,128)(2,1)S(1)}, u32[]{:S(2)}, u32[]{:S(2)}) collective-permute-start(bf16[32,640]{1,0:T(8,128)(2,1)} %get-tuple-element.31), channel_id=1, source_target_pairs={{0,8},{1,9},{2,10},{3,11},{4,12},{5,13},{6,14},{7,15},{8,0},{9,1},... | collective-permute-start | bytes 122888 | tf_op jit(solution)/shard_map/ppermute | solution.py:353
  33.0 4.4 %collective-permute-start.3 = (bf16[32,640]{1,0:T(8,128)(2,1)S(1)}, bf16[32,640]{1,0:T(8,128)(2,1)S(1)}, u32[]{:S(2)}, u32[]{:S(2)}) collective-permute-start(bf16[32,640]{1,0:T(8,128)(2,1)S(1)} %add_convert_fusion.2), channel_id=1, source_target_pairs={{0,2},{1,3},{2,4},{3,5},{4,6},{5,7},{6,8},{7,9},{8,10},{9,11},{10,... | collective-permute-start | bytes 122888 | tf_op jit(solution)/shard_map/ppermute | solution.py:353
  37.1 3.2 %collective-permute-start.4 = (bf16[32,640]{1,0:T(8,128)(2,1)S(1)}, bf16[32,640]{1,0:T(8,128)(2,1)S(1)}, u32[]{:S(2)}, u32[]{:S(2)}) collective-permute-start(bf16[32,640]{1,0:T(8,128)(2,1)S(1)} %add_convert_fusion.1), channel_id=1, source_target_pairs={{0,14},{1,15},{2,0},{3,1},{4,2},{5,3},{6,4},{7,5},{8,6},{9,7},{10,... | collective-permute-start | bytes 122888 | tf_op jit(solution)/shard_map/ppermute | solution.py:353
  40.3 0.9 copy-start
  41.2 0.7 copy-start.1
  42.1 7.1 %collective-permute-start.6 = (bf16[16,640]{1,0:T(8,128)(2,1)S(1)}, bf16[16,640]{1,0:T(8,128)(2,1)S(1)}, u32[]{:S(2)}, u32[]{:S(2)}) collective-permute-start(bf16[16,640]{1,0:T(8,128)(2,1)S(1)} %get-tuple-element.42), channel_id=1, source_target_pairs={{0,128},{16,144},{32,160},{48,176},{64,192},{80,208},{96,224},{112... | collective-permute-start | bytes 61448 | tf_op jit(solution)/shard_map/ppermute | solution.py:356
  45.0 4.9 %collective-permute-start.7 = (bf16[16,640]{1,0:T(8,128)(2,1)S(1)}, bf16[16,640]{1,0:T(8,128)(2,1)S(1)}, u32[]{:S(2)}, u32[]{:S(2)}) collective-permute-start(bf16[16,640]{1,0:T(8,128)(2,1)S(1)} %get-tuple-element.42), channel_id=1, source_target_pairs={{0,129},{1,128},{2,131},{3,130},{4,133},{5,132},{6,135},{7,134},{8... | collective-permute-start | bytes 61448 | tf_op jit(solution)/shard_map/ppermute | solution.py:404
  45.0 4.9 %collective-permute-start.5 = (bf16[32,640]{1,0:T(8,128)(2,1)S(1)}, bf16[32,640]{1,0:T(8,128)(2,1)S(1)}, u32[]{:S(2)}, u32[]{:S(2)}) collective-permute-start(bf16[32,640]{1,0:T(8,128)(2,1)S(1)} %get-tuple-element.40), channel_id=1, source_target_pairs={{0,1},{1,0},{2,3},{3,2},{4,5},{5,4},{6,7},{7,6},{8,9},{9,8},{10,11... | collective-permute-start | bytes 122888 | tf_op jit(solution)/shard_map/ppermute | solution.py:350
  50.0 6.9 %collective-permute-start.10 = (bf16[8,640]{1,0:T(8,128)(2,1)S(1)}, bf16[8,640]{1,0:T(8,128)(2,1)S(1)}, u32[]{:S(2)}, u32[]{:S(2)}) collective-permute-start(bf16[8,640]{1,0:T(8,128)(2,1)S(1)} %pad_maximum_fusion.7), channel_id=1, source_target_pairs={{0,96},{16,112},{32,64},{48,80},{64,32},{80,48},{96,0},{112,16},{1... | collective-permute-start | bytes 30728 | tf_op jit(solution)/shard_map/ppermute | solution.py:356
  52.2 5.6 %collective-permute-start.9 = (bf16[8,640]{1,0:T(8,128)(2,1)S(1)}, bf16[8,640]{1,0:T(8,128)(2,1)S(1)}, u32[]{:S(2)}, u32[]{:S(2)}) collective-permute-start(bf16[8,640]{1,0:T(8,128)(2,1)S(1)} %pad_maximum_fusion.6), channel_id=1, source_target_pairs={{0,64},{16,80},{32,96},{48,112},{64,0},{80,16},{96,32},{112,48},{1... | collective-permute-start | bytes 30728 | tf_op jit(solution)/shard_map/ppermute | solution.py:356
  56.8 2.9 %collective-permute-start.8 = (bf16[8,640]{1,0:T(8,128)(2,1)S(1)}, bf16[8,640]{1,0:T(8,128)(2,1)S(1)}, u32[]{:S(2)}, u32[]{:S(2)}) collective-permute-start(bf16[8,640]{1,0:T(8,128)(2,1)S(1)} %pad_maximum_fusion.5), channel_id=1, source_target_pairs={{0,32},{16,48},{32,0},{48,16},{64,96},{80,112},{96,64},{112,80},{1... | collective-permute-start | bytes 30728 | tf_op jit(solution)/shard_map/ppermute | solution.py:356
  59.7 28.1 %all-to-all-start.1 = ((bf16[16,2,80,256]{3,2,1,0:T(8,128)(2,1)}), bf16[16,2,80,256]{3,2,1,0:T(8,128)(2,1)}, u32[]{:S(2)}, u32[]{:S(2)}) async-start(bf16[16,2,80,256]{3,2,1,0:T(8,128)(2,1)} %bitcast.35), calls=%async_computation.1 | async-start | bytes 2621440 | tf_op jit(solution)/shard_map/all_to_all | solution.py:360
  67.9 1.3 %collective-permute-start.11 = (bf16[16,640]{1,0:T(8,128)(2,1)S(1)}, bf16[16,640]{1,0:T(8,128)(2,1)S(1)}, u32[]{:S(2)}, u32[]{:S(2)}) collective-permute-start(bf16[16,640]{1,0:T(8,128)(2,1)S(1)} %reshape_squeeze.7), channel_id=1, source_target_pairs={{0,16},{16,0},{32,48},{48,32},{64,80},{80,64},{96,112},{112,96},{1... | collective-permute-start | bytes 61448 | tf_op jit(solution)/shard_map/ppermute | solution.py:356
  69.2 12.5 %collective-permute-start.12 = (bf16[48,640]{1,0:T(8,128)(2,1)S(1)}, bf16[48,640]{1,0:T(8,128)(2,1)S(1)}, u32[]{:S(2)}, u32[]{:S(2)}) collective-permute-start(bf16[48,640]{1,0:T(8,128)(2,1)S(1)} %pad_maximum_fusion.3.refs_0_), channel_id=1, source_target_pairs={{0,2},{1,3},{2,4},{3,5},{4,6},{5,7},{6,8},{7,9},{8,10},{9,11},{10,... | collective-permute-start | bytes 184328 | tf_op jit(solution)/shard_map/ppermute | solution.py:353
  70.8 10.9 %collective-permute-start.13 = (bf16[48,640]{1,0:T(8,128)(2,1)S(1)}, bf16[48,640]{1,0:T(8,128)(2,1)S(1)}, u32[]{:S(2)}, u32[]{:S(2)}) collective-permute-start(bf16[48,640]{1,0:T(8,128)(2,1)S(1)} %pad_maximum_fusion.3.refs_0_), channel_id=1, source_target_pairs={{0,14},{1,15},{2,0},{3,1},{4,2},{5,3},{6,4},{7,5},{8,6},{9,7},{10,... | collective-permute-start | bytes 184328 | tf_op jit(solution)/shard_map/ppermute | solution.py:353
  74.9 7.4 %collective-permute-start.14 = (bf16[48,640]{1,0:T(8,128)(2,1)S(1)}, bf16[48,640]{1,0:T(8,128)(2,1)S(1)}, u32[]{:S(2)}, u32[]{:S(2)}) collective-permute-start(bf16[48,640]{1,0:T(8,128)(2,1)S(1)} %pad_maximum_fusion.3.refs_0_), channel_id=1, source_target_pairs={{0,8},{1,9},{2,10},{3,11},{4,12},{5,13},{6,14},{7,15},{8,0},{9,1},... | collective-permute-start | bytes 184328 | tf_op jit(solution)/shard_map/ppermute | solution.py:353
  82.3 7.6 %collective-permute-start.15 = (bf16[96,640]{1,0:T(8,128)(2,1)S(1)}, bf16[96,640]{1,0:T(8,128)(2,1)S(1)}, u32[]{:S(2)}, u32[]{:S(2)}) collective-permute-start(bf16[96,640]{1,0:T(8,128)(2,1)S(1)} %get-tuple-element.59), channel_id=1, source_target_pairs={{0,4},{1,5},{2,6},{3,7},{4,8},{5,9},{6,10},{7,11},{8,12},{9,13},{1... | collective-permute-start | bytes 368648 | tf_op jit(solution)/shard_map/ppermute | solution.py:353
  82.4 9.6 %collective-permute-start.16 = (bf16[96,640]{1,0:T(8,128)(2,1)S(1)}, bf16[96,640]{1,0:T(8,128)(2,1)S(1)}, u32[]{:S(2)}, u32[]{:S(2)}) collective-permute-start(bf16[96,640]{1,0:T(8,128)(2,1)S(1)} %get-tuple-element.58), channel_id=1, source_target_pairs={{0,12},{1,13},{2,14},{3,15},{4,0},{5,1},{6,2},{7,3},{8,4},{9,5},{1... | collective-permute-start | bytes 368648 | tf_op jit(solution)/shard_map/ppermute | solution.py:353

commit v3 on v2

--- a/solution.py
+++ b/solution.py
@@ -11,10 +11,11 @@
 REQ = 16
 HD = 128
 NZ = 8
-CUT = 176
+CUT = 160
 SMEM = pltpu.SMEM
 VMEM = pltpu.VMEM
 VMEM_LIMIT = 63 * 1024 * 1024
+FRONT_LIMIT = 52 * 1024 * 1024
 SMALL_LIMIT = 8 * 1024 * 1024
 
 
@@ -236,7 +237,7 @@
             pltpu.SemaphoreType.DMA,
             pltpu.SemaphoreType.DMA,
         ],
-        compiler_params=pltpu.CompilerParams(vmem_limit_bytes=VMEM_LIMIT - 2560 * 1024),
+        compiler_params=pltpu.CompilerParams(vmem_limit_bytes=FRONT_LIMIT),
         cost_estimate=pl.CostEstimate(
             flops=400_000_000, bytes_accessed=9_500_000, transcendentals=30_000
         ),

time: 94.6 us -> 90.8 us (0.960); the launches traced: 93.2 us -> 90.5 us
  other arithmetic: 1.9 us -> 0.13 us
  local copies, waits for them, and re-layouts: 1.8 us -> 0.28 us
  waiting for transfers between devices: 19.2 us -> 20.6 us
    all_to_all x2, waiting for transfers between devices: 1.86 us -> 4.48 us  [deliver(): lax.all_to_all(blocks, both, split_axis=0, concat_axis=0, tiled=True)]
    ppermute x10, waiting for transfers between devices: 8.89 us -> 7.22 us  [round_z(): lax.ppermute(array, 'tp', [(t, (t + 2 * shift) % ranks) for t in range(ra...]
    unnamed x10 -> x26, local copies, waits for them, and re-layouts: 1.66 us -> 0.14 us
    ppermute x5, starting transfers between devices: 10 us -> 8.9 us  [over_groups(): return lax.ppermute(array, both, [(s, s ^ flip) for s in range(groups)])]
    all_to_all x2, starting transfers between devices: 16.4 us -> 17.5 us  [deliver(): lax.all_to_all(blocks, both, split_axis=0, concat_axis=0, tiled=True)]
  transfers between devices with their start and end apart: 19 -> 19, of which waited for: 11 -> 10; matrix products, arithmetic and copies ran while one was open for 2% -> 0% of each run, Pallas kernels for 11% -> 11%
where the time goes in v3:
time: 90.8 us; the launch traced here: 90.5 us
  starting transfers between devices  53.8 us (59%)
  waiting for transfers between devices  20.6 us (23%)
  Pallas kernels  14.7 us (16%)
  between operations  1.01 us (1%)
    ppermute x10, starting transfers between devices, round_z(): lax.ppermute(array, 'tp', [(t, (t + 2 * shift) % ranks) for t in range(ra...  27 us
    all_to_all x2, starting transfers between devices, deliver(): lax.all_to_all(blocks, both, split_axis=0, concat_axis=0, tiled=True)  17.5 us
    ppermute x5, starting transfers between devices, over_groups(): return lax.ppermute(array, both, [(s, s ^ flip) for s in range(groups)])  8.9 us
    ppermute x5, waiting for transfers between devices, over_groups(): return lax.ppermute(array, both, [(s, s ^ flip) for s in range(groups)])  8.26 us
    ppermute x10, waiting for transfers between devices, round_z(): lax.ppermute(array, 'tp', [(t, (t + 2 * shift) % ranks) for t in range(ra...  7.22 us
    pallas_call x1, Pallas kernels, front(): pl.pallas_call(front_kernel, out_shape=[jax.ShapeDtypeStruct((2 * REQ, wi...  5.13 us
    pallas_call x2, Pallas kernels, place(): pl.pallas_call(functools.partial(place_kernel, start), out_shape=jax.Shap...  4.56 us
    all_to_all x2, waiting for transfers between devices, deliver(): lax.all_to_all(blocks, both, split_axis=0, concat_axis=0, tiled=True)  4.48 us
  transfers between devices with their start and end apart: 19, of which 10 were waited for; matrix products, arithmetic and copies ran while one was open for 0% of the time, Pallas kernels for 11%

profile of v3, /device:TPU:1, one launch (start us, length us, event | category | flops | bytes accessed | tf_op | source)
XLA Modules:
  0.0 90.5 jit_solution(6628011609380798217)
XLA Ops:
  0.6 3.7 %pack.1 = (bf16[32,160,256]{2,1,0:T(8,128)(2,1)}, bf16[32,96,256]{2,1,0:T(8,128)(2,1)}) custom-call(s32[16]{0:T(128)} %bitcast.37, s32[16]{0:T(128)} %bitcast.39, bf16[16,256]{1,0:T(8,128)(2,1)} %bitcast.32, bf16[16,256,256]{2,1,0:T(8,128)(2,1)} %bitcast.44), custom_call_target="tpu_custom_call" | custom-call | flops 1000000 | bytes 6400000 | tf_op jit(solution)/shard_map/pack/pallas_call | solution.py:114
  4.3 0.0 copy-start
  4.4 0.0 copy-start.1
  4.4 0.0 copy-start.2
  4.4 0.0 copy-start.3
  4.4 0.0 copy-start.4
  4.4 0.0 copy-start.5
  4.4 0.0 copy-start.6
  4.4 0.0 copy-start.7
  4.4 0.0 copy-start.8
  4.4 0.0 copy-start.9
  4.5 8.6 %all-to-all-start = ((bf16[16,2,160,256]{3,2,1,0:T(8,128)(2,1)}), bf16[16,2,160,256]{3,2,1,0:T(8,128)(2,1)S(1)}, u32[]{:S(2)}, u32[]{:S(2)}) async-start(bf16[16,2,160,256]{3,2,1,0:T(8,128)(2,1)} %bitcast.47), calls=%async_computation | async-start | bytes 5242880 | tf_op jit(solution)/shard_map/all_to_all | solution.py:361
  13.1 0.0 copy-done
  13.1 0.0 copy-done.1
  13.1 0.0 copy-done.2
  13.1 0.0 copy-done.3
  13.1 0.0 copy-done.4
  13.1 0.0 copy-done.5
  13.1 0.0 copy-done.6
  13.1 0.0 copy-done.7
  13.1 0.0 copy-done.8
  13.1 0.0 copy-start.10
  13.2 5.1 %front.1 = (f32[32,640]{1,0:T(8,128)S(1)}, f32[32,640]{1,0:T(8,128)S(1)}, f32[32,640]{1,0:T(8,128)S(1)}, bf16[64,640]{1,0:T(8,128)(2,1)S(1)}, bf16[64,640]{1,0:T...) custom-call(s32[16]{0:T(128)S(1)} %bitcast.38, s32[16]{0:T(128)S(1)} %bitcast.41, ...), custom_call_target="tpu_custom_call" | custom-call | flops 400000000 | bytes 9500000 | tf_op jit(solution)/shard_map/front/pallas_call | solution.py:221
  18.3 3.1 %collective-permute-start = (bf16[64,640]{1,0:T(8,128)(2,1)S(1)}, bf16[64,640]{1,0:T(8,128)(2,1)S(1)}, u32[]{:S(2)}, u32[]{:S(2)}) collective-permute-start(bf16[64,640]{1,0:T(8,128)(2,1)S(1)} %get-tuple-element.29), channel_id=1, source_target_pairs={{0,4},{1,5},{2,6},{3,7},{4,8},{5,9},{6,10},{7,11},{8,12},{9,13},{1... | collective-permute-start | bytes 245768 | tf_op jit(solution)/shard_map/ppermute | solution.py:354
  21.4 3.1 %collective-permute-start.1 = (bf16[64,640]{1,0:T(8,128)(2,1)S(1)}, bf16[64,640]{1,0:T(8,128)(2,1)S(1)}, u32[]{:S(2)}, u32[]{:S(2)}) collective-permute-start(bf16[64,640]{1,0:T(8,128)(2,1)S(1)} %get-tuple-element.30), channel_id=1, source_target_pairs={{0,12},{1,13},{2,14},{3,15},{4,0},{5,1},{6,2},{7,3},{8,4},{9,5},{1... | collective-permute-start | bytes 245768 | tf_op jit(solution)/shard_map/ppermute | solution.py:354
  24.5 4.4 %collective-permute-start.2 = (bf16[32,640]{1,0:T(8,128)(2,1)S(1)}, bf16[32,640]{1,0:T(8,128)(2,1)S(1)}, u32[]{:S(2)}, u32[]{:S(2)}) collective-permute-start(bf16[32,640]{1,0:T(8,128)(2,1)S(1)} %get-tuple-element.31), channel_id=1, source_target_pairs={{0,8},{1,9},{2,10},{3,11},{4,12},{5,13},{6,14},{7,15},{8,0},{9,1},... | collective-permute-start | bytes 122888 | tf_op jit(solution)/shard_map/ppermute | solution.py:354
  28.9 2.8 %collective-permute-done.2.refs_2_ = bf16[32,640]{1,0:T(8,128)(2,1)S(1)} collective-permute-done((bf16[32,640]{1,0:T(8,128)(2,1)S(1)}, bf16[32,640]{1,0:T(8,128)(2,1)S(1)}, u32[]{:S(2)}, u32[]{:S(2)}) %collective-permute-start.2) | collective-permute-done | bytes 40992 | tf_op jit(solution)/shard_map/ppermute | solution.py:354
  31.7 0.0 collective-permute-done.refs_0_
  31.7 0.0 collective-permute-done.1.refs_1_
  31.8 3.0 %collective-permute-start.3 = (bf16[32,640]{1,0:T(8,128)(2,1)S(1)}, bf16[32,640]{1,0:T(8,128)(2,1)S(1)}, u32[]{:S(2)}, u32[]{:S(2)}) collective-permute-start(bf16[32,640]{1,0:T(8,128)(2,1)S(1)} %add_convert_fusion.2), channel_id=1, source_target_pairs={{0,2},{1,3},{2,4},{3,5},{4,6},{5,7},{6,8},{7,9},{8,10},{9,11},{10,... | collective-permute-start | bytes 122888 | tf_op jit(solution)/shard_map/ppermute | solution.py:354
  34.8 0.1 collective-permute-start.4
  34.9 1.3 %collective-permute-done.3.refs_3_ = bf16[32,640]{1,0:T(8,128)(2,1)S(1)} collective-permute-done((bf16[32,640]{1,0:T(8,128)(2,1)S(1)}, bf16[32,640]{1,0:T(8,128)(2,1)S(1)}, u32[]{:S(2)}, u32[]{:S(2)}) %collective-permute-start.3) | collective-permute-done | bytes 40992 | tf_op jit(solution)/shard_map/ppermute | solution.py:354
  36.2 1.9 %collective-permute-done.4.refs_4_ = bf16[32,640]{1,0:T(8,128)(2,1)S(1)} collective-permute-done((bf16[32,640]{1,0:T(8,128)(2,1)S(1)}, bf16[32,640]{1,0:T(8,128)(2,1)S(1)}, u32[]{:S(2)}, u32[]{:S(2)}) %collective-permute-start.4) | collective-permute-done | bytes 40992 | tf_op jit(solution)/shard_map/ppermute | solution.py:354
  38.0 0.1 spread.1
  38.2 3.1 %collective-permute-start.6 = (bf16[16,640]{1,0:T(8,128)(2,1)S(1)}, bf16[16,640]{1,0:T(8,128)(2,1)S(1)}, u32[]{:S(2)}, u32[]{:S(2)}) collective-permute-start(bf16[16,640]{1,0:T(8,128)(2,1)S(1)} %get-tuple-element.42), channel_id=1, source_target_pairs={{0,128},{16,144},{32,160},{48,176},{64,192},{80,208},{96,224},{112... | collective-permute-start | bytes 61448 | tf_op jit(solution)/shard_map/ppermute | solution.py:357
  41.2 0.0 collective-permute-start.7
  41.2 0.3 collective-permute-start.5
  41.6 4.8 %collective-permute-done.6 = bf16[16,640]{1,0:T(8,128)(2,1)S(1)} collective-permute-done((bf16[16,640]{1,0:T(8,128)(2,1)S(1)}, bf16[16,640]{1,0:T(8,128)(2,1)S(1)}, u32[]{:S(2)}, u32[]{:S(2)}) %collective-permute-start.6) | collective-permute-done | bytes 20512 | tf_op jit(solution)/shard_map/ppermute | solution.py:357
  46.3 0.6 collective-permute-done.7
  46.9 0.0 collective-permute-done.5
  47.0 2.4 %collective-permute-start.10 = (bf16[8,640]{1,0:T(8,128)(2,1)S(1)}, bf16[8,640]{1,0:T(8,128)(2,1)S(1)}, u32[]{:S(2)}, u32[]{:S(2)}) collective-permute-start(bf16[8,640]{1,0:T(8,128)(2,1)S(1)} %pad_maximum_fusion.7), channel_id=1, source_target_pairs={{0,96},{16,112},{32,64},{48,80},{64,32},{80,48},{96,0},{112,16},{1... | collective-permute-start | bytes 30728 | tf_op jit(solution)/shard_map/ppermute | solution.py:357
  49.4 3.1 %collective-permute-start.9 = (bf16[8,640]{1,0:T(8,128)(2,1)S(1)}, bf16[8,640]{1,0:T(8,128)(2,1)S(1)}, u32[]{:S(2)}, u32[]{:S(2)}) collective-permute-start(bf16[8,640]{1,0:T(8,128)(2,1)S(1)} %pad_maximum_fusion.6), channel_id=1, source_target_pairs={{0,64},{16,80},{32,96},{48,112},{64,0},{80,16},{96,32},{112,48},{1... | collective-permute-start | bytes 30728 | tf_op jit(solution)/shard_map/ppermute | solution.py:357
  52.6 0.1 collective-permute-start.8
  52.7 0.0 collective-permute-done.10
  52.7 0.9 %collective-permute-done.9 = bf16[8,640]{1,0:T(8,128)(2,1)S(1)} collective-permute-done((bf16[8,640]{1,0:T(8,128)(2,1)S(1)}, bf16[8,640]{1,0:T(8,128)(2,1)S(1)}, u32[]{:S(2)}, u32[]{:S(2)}) %collective-permute-start.9) | collective-permute-done | bytes 10272 | tf_op jit(solution)/shard_map/ppermute | solution.py:357
  53.6 1.6 %collective-permute-done.8 = bf16[8,640]{1,0:T(8,128)(2,1)S(1)} collective-permute-done((bf16[8,640]{1,0:T(8,128)(2,1)S(1)}, bf16[8,640]{1,0:T(8,128)(2,1)S(1)}, u32[]{:S(2)}, u32[]{:S(2)}) %collective-permute-start.8) | collective-permute-done | bytes 10272 | tf_op jit(solution)/shard_map/ppermute | solution.py:357
  55.2 0.0 all-to-all-done
  55.2 8.9 %all-to-all-start.1 = ((bf16[16,2,96,256]{3,2,1,0:T(8,128)(2,1)}), bf16[16,2,96,256]{3,2,1,0:T(8,128)(2,1)}, u32[]{:S(2)}, u32[]{:S(2)}) async-start(bf16[16,2,96,256]{3,2,1,0:T(8,128)(2,1)} %bitcast.48), calls=%async_computation.1 | async-start | bytes 3145728 | tf_op jit(solution)/shard_map/all_to_all | solution.py:361
  64.3 0.2 collective-permute-start.11
  64.5 1.0 %collective-permute-done.11 = bf16[16,640]{1,0:T(8,128)(2,1)S(1)} collective-permute-done((bf16[16,640]{1,0:T(8,128)(2,1)S(1)}, bf16[16,640]{1,0:T(8,128)(2,1)S(1)}, u32[]{:S(2)}, u32[]{:S(2)}) %collective-permute-start.11) | collective-permute-done | bytes 20512 | tf_op jit(solution)/shard_map/ppermute | solution.py:357
  65.6 1.7 %collective-permute-start.12 = (bf16[48,640]{1,0:T(8,128)(2,1)S(1)}, bf16[48,640]{1,0:T(8,128)(2,1)S(1)}, u32[]{:S(2)}, u32[]{:S(2)}) collective-permute-start(bf16[48,640]{1,0:T(8,128)(2,1)S(1)} %pad_maximum_fusion.3.refs_0_), channel_id=1, source_target_pairs={{0,2},{1,3},{2,4},{3,5},{4,6},{5,7},{6,8},{7,9},{8,10},{9,11},{10,... | collective-permute-start | bytes 184328 | tf_op jit(solution)/shard_map/ppermute | solution.py:354
  67.2 4.3 %collective-permute-start.13 = (bf16[48,640]{1,0:T(8,128)(2,1)S(1)}, bf16[48,640]{1,0:T(8,128)(2,1)S(1)}, u32[]{:S(2)}, u32[]{:S(2)}) collective-permute-start(bf16[48,640]{1,0:T(8,128)(2,1)S(1)} %pad_maximum_fusion.3.refs_0_), channel_id=1, source_target_pairs={{0,14},{1,15},{2,0},{3,1},{4,2},{5,3},{6,4},{7,5},{8,6},{9,7},{10,... | collective-permute-start | bytes 184328 | tf_op jit(solution)/shard_map/ppermute | solution.py:354
  71.5 3.7 %collective-permute-start.14 = (bf16[48,640]{1,0:T(8,128)(2,1)S(1)}, bf16[48,640]{1,0:T(8,128)(2,1)S(1)}, u32[]{:S(2)}, u32[]{:S(2)}) collective-permute-start(bf16[48,640]{1,0:T(8,128)(2,1)S(1)} %pad_maximum_fusion.3.refs_0_), channel_id=1, source_target_pairs={{0,8},{1,9},{2,10},{3,11},{4,12},{5,13},{6,14},{7,15},{8,0},{9,1},... | collective-permute-start | bytes 184328 | tf_op jit(solution)/shard_map/ppermute | solution.py:354
  75.3 2.4 %place.2.refs_0_ = bf16[32,256,256]{2,1,0:T(8,128)(2,1)} custom-call(bf16[32,160,256]{2,1,0:T(8,128)(2,1)S(1)} %bitcast.29), custom_call_target="tpu_custom_call" | custom-call | bytes 5242880 | tf_op jit(solution)/shard_map/place/pallas_call | solution.py:310
  77.6 0.0 collective-permute-done.12.refs_1_
  77.6 0.0 collective-permute-done.13.refs_2_
  77.7 1.2 %collective-permute-done.14.refs_3_ = bf16[48,640]{1,0:T(8,128)(2,1)S(1)} collective-permute-done((bf16[48,640]{1,0:T(8,128)(2,1)S(1)}, bf16[48,640]{1,0:T(8,128)(2,1)S(1)}, u32[]{:S(2)}, u32[]{:S(2)}) %collective-permute-start.14) | collective-permute-done | bytes 61472 | tf_op jit(solution)/shard_map/ppermute | solution.py:354
  78.9 0.1 collective-permute-start.15
  79.0 3.6 %collective-permute-start.16 = (bf16[96,640]{1,0:T(8,128)(2,1)S(1)}, bf16[96,640]{1,0:T(8,128)(2,1)S(1)}, u32[]{:S(2)}, u32[]{:S(2)}) collective-permute-start(bf16[96,640]{1,0:T(8,128)(2,1)S(1)} %get-tuple-element.58), channel_id=1, source_target_pairs={{0,12},{1,13},{2,14},{3,15},{4,0},{5,1},{6,2},{7,3},{8,4},{9,5},{1... | collective-permute-start | bytes 368648 | tf_op jit(solution)/shard_map/ppermute | solution.py:354
  82.6 4.5 %all-to-all-done.1 = bf16[16,2,96,256]{3,2,1,0:T(8,128)(2,1)} async-done(((bf16[16,2,96,256]{3,2,1,0:T(8,128)(2,1)}), bf16[16,2,96,256]{3,2,1,0:T(8,128)(2,1)}, u32[]{:S(2)}, u32[]{:S(2)}) %all-to-all-start.1) | async-done | bytes 1572896 | tf_op jit(solution)/shard_map/all_to_all | solution.py:361
  87.1 2.2 %place.3 = bf16[32,256,256]{2,1,0:T(8,128)(2,1)} custom-call(bf16[32,96,256]{2,1,0:T(8,128)(2,1)} %bitcast.17.part, bf16[32,256,256]{2,1,0:T(8,128)(2,1)} %place.2.refs_0_), custom_call_target="tpu_custom_call", output_to_operand_aliasing={{}: (1, {})} | custom-call | bytes 3145728 | tf_op jit(solution)/shard_map/place/pallas_call | solution.py:310
  89.3 0.0 collective-permute-done.15.refs_4_
  89.3 0.0 collective-permute-done.16.refs_5_
  89.3 1.2 %finish.1 = (bf16[48,5120]{1,0:T(8,128)(2,1)}, bf16[48,5120]{1,0:T(8,128)(2,1)}) custom-call(bf16[1,5120]{1,0:T(2,128)(2,1)S(1)} %reshape.30.gain, bf16[48,640]{1,0:T(8,128)(2,1)S(1)} %pad_maximum_fusion.3.refs_0_, bf16[48,640]{1,0:T(8,128)(2,1)S(1)} %collective-permute-done.12.refs_1_, bf16[48,640]{1,0:T(8,128)(2,1)S(1)} %collective-permute-done.13.refs_2_, ...), custom_call_target="tpu_custom_call" | custom-call | tf_op jit(solution)/shard_map/finish/pallas_call | solution.py:427
  (27 shorter events, 0.3 us)
Async XLA Ops:
  4.3 8.7 %copy-start = (bf16[1,1,16,5120]{3,2,1,0:T(8,128)(2,1)S(1)}, bf16[1,1,16,5120]{3,2,1,0:T(8,128)(2,1)}, u32[]{:S(2)}) copy-start(bf16[1,1,16,5120]{3,2,1,0:T(8,128)(2,1)} %param.19) | copy-start | bytes 491524
  4.4 8.7 %copy-start.1 = (bf16[1,1,16,5120]{3,2,1,0:T(8,128)(2,1)S(1)}, bf16[1,1,16,5120]{3,2,1,0:T(8,128)(2,1)}, u32[]{:S(2)}) copy-start(bf16[1,1,16,5120]{3,2,1,0:T(8,128)(2,1)} %param.24) | copy-start | bytes 491524
  4.4 8.7 %copy-start.2 = (bf16[1,1,16,1,256]{4,2,3,1,0:T(8,128)(2,1)S(1)}, bf16[1,1,16,1,256]{4,2,3,1,0:T(8,128)(2,1)}, u32[]{:S(2)}) copy-start(bf16[1,1,16,1,256]{4,2,3,1,0:T(8,128)(2,1)} %param.23) | copy-start | bytes 24580
  4.4 8.7 %copy-start.3 = (bf16[1,1,16,256]{3,2,1,0:T(8,128)(2,1)S(1)}, bf16[1,1,16,256]{3,2,1,0:T(8,128)(2,1)}, u32[]{:S(2)}) copy-start(bf16[1,1,16,256]{3,2,1,0:T(8,128)(2,1)} %param.17) | copy-start | bytes 24580
  4.4 8.7 %copy-start.4 = (bf16[1,1,16,1,256]{4,2,3,1,0:T(8,128)(2,1)S(1)}, bf16[1,1,16,1,256]{4,2,3,1,0:T(8,128)(2,1)}, u32[]{:S(2)}) copy-start(bf16[1,1,16,1,256]{4,2,3,1,0:T(8,128)(2,1)} %param.18) | copy-start | bytes 24580
  4.4 8.7 %copy-start.5 = (bf16[1,1,16,256]{3,2,1,0:T(8,128)(2,1)S(1)}, bf16[1,1,16,256]{3,2,1,0:T(8,128)(2,1)}, u32[]{:S(2)}) copy-start(bf16[1,1,16,256]{3,2,1,0:T(8,128)(2,1)} %param.22) | copy-start | bytes 24580
  4.4 8.7 %copy-start.6 = (s32[1,1,16,1]{2,3,1,0:T(1,128)S(1)}, s32[1,1,16,1]{2,3,1,0:T(1,128)}, u32[]{:S(2)}) copy-start(s32[1,1,16,1]{2,3,1,0:T(1,128)} %param.25) | copy-start | bytes 196
  4.4 8.7 %copy-start.7 = (s32[1,1,16]{2,1,0:T(1,128)S(1)}, s32[1,1,16]{2,1,0:T(1,128)}, u32[]{:S(2)}) copy-start(s32[1,1,16]{2,1,0:T(1,128)} %param.21) | copy-start | bytes 196
  4.4 8.7 %copy-start.8 = (s32[1,1,16]{2,1,0:T(1,128)S(1)}, s32[1,1,16]{2,1,0:T(1,128)}, u32[]{:S(2)}) copy-start(s32[1,1,16]{2,1,0:T(1,128)} %param.16) | copy-start | bytes 196
  4.4 8.7 %copy-start.9 = (s32[1,1,64]{2,1,0:T(1,128)S(1)}, s32[1,1,64]{2,1,0:T(1,128)}, u32[]{:S(2)}) copy-start(s32[1,1,64]{2,1,0:T(1,128)} %param.15) | copy-start | bytes 772
  4.5 50.7 %all-to-all-start = ((bf16[16,2,160,256]{3,2,1,0:T(8,128)(2,1)}), bf16[16,2,160,256]{3,2,1,0:T(8,128)(2,1)S(1)}, u32[]{:S(2)}, u32[]{:S(2)}) async-start(bf16[16,2,160,256]{3,2,1,0:T(8,128)(2,1)} %bitcast.47), calls=%async_computation | async-start | bytes 5242880 | tf_op jit(solution)/shard_map/all_to_all | solution.py:361
  13.1 15.7 %copy-start.10 = (bf16[5120]{0:T(1024)(128)(2,1)S(1)}, bf16[5120]{0:T(1024)(128)(2,1)}, u32[]{:S(2)}) copy-start(bf16[5120]{0:T(1024)(128)(2,1)} %param.27) | copy-start | bytes 30724
  18.3 13.4 %collective-permute-start = (bf16[64,640]{1,0:T(8,128)(2,1)S(1)}, bf16[64,640]{1,0:T(8,128)(2,1)S(1)}, u32[]{:S(2)}, u32[]{:S(2)}) collective-permute-start(bf16[64,640]{1,0:T(8,128)(2,1)S(1)} %get-tuple-element.29), channel_id=1, source_target_pairs={{0,4},{1,5},{2,6},{3,7},{4,8},{5,9},{6,10},{7,11},{8,12},{9,13},{1... | collective-permute-start | bytes 245768 | tf_op jit(solution)/shard_map/ppermute | solution.py:354
  21.4 10.4 %collective-permute-start.1 = (bf16[64,640]{1,0:T(8,128)(2,1)S(1)}, bf16[64,640]{1,0:T(8,128)(2,1)S(1)}, u32[]{:S(2)}, u32[]{:S(2)}) collective-permute-start(bf16[64,640]{1,0:T(8,128)(2,1)S(1)} %get-tuple-element.30), channel_id=1, source_target_pairs={{0,12},{1,13},{2,14},{3,15},{4,0},{5,1},{6,2},{7,3},{8,4},{9,5},{1... | collective-permute-start | bytes 245768 | tf_op jit(solution)/shard_map/ppermute | solution.py:354
  24.5 7.2 %collective-permute-start.2 = (bf16[32,640]{1,0:T(8,128)(2,1)S(1)}, bf16[32,640]{1,0:T(8,128)(2,1)S(1)}, u32[]{:S(2)}, u32[]{:S(2)}) collective-permute-start(bf16[32,640]{1,0:T(8,128)(2,1)S(1)} %get-tuple-element.31), channel_id=1, source_target_pairs={{0,8},{1,9},{2,10},{3,11},{4,12},{5,13},{6,14},{7,15},{8,0},{9,1},... | collective-permute-start | bytes 122888 | tf_op jit(solution)/shard_map/ppermute | solution.py:354
  31.8 4.4 %collective-permute-start.3 = (bf16[32,640]{1,0:T(8,128)(2,1)S(1)}, bf16[32,640]{1,0:T(8,128)(2,1)S(1)}, u32[]{:S(2)}, u32[]{:S(2)}) collective-permute-start(bf16[32,640]{1,0:T(8,128)(2,1)S(1)} %add_convert_fusion.2), channel_id=1, source_target_pairs={{0,2},{1,3},{2,4},{3,5},{4,6},{5,7},{6,8},{7,9},{8,10},{9,11},{10,... | collective-permute-start | bytes 122888 | tf_op jit(solution)/shard_map/ppermute | solution.py:354
  34.8 3.2 %collective-permute-start.4 = (bf16[32,640]{1,0:T(8,128)(2,1)S(1)}, bf16[32,640]{1,0:T(8,128)(2,1)S(1)}, u32[]{:S(2)}, u32[]{:S(2)}) collective-permute-start(bf16[32,640]{1,0:T(8,128)(2,1)S(1)} %add_convert_fusion.1), channel_id=1, source_target_pairs={{0,14},{1,15},{2,0},{3,1},{4,2},{5,3},{6,4},{7,5},{8,6},{9,7},{10,... | collective-permute-start | bytes 122888 | tf_op jit(solution)/shard_map/ppermute | solution.py:354
  38.2 8.1 %collective-permute-start.6 = (bf16[16,640]{1,0:T(8,128)(2,1)S(1)}, bf16[16,640]{1,0:T(8,128)(2,1)S(1)}, u32[]{:S(2)}, u32[]{:S(2)}) collective-permute-start(bf16[16,640]{1,0:T(8,128)(2,1)S(1)} %get-tuple-element.42), channel_id=1, source_target_pairs={{0,128},{16,144},{32,160},{48,176},{64,192},{80,208},{96,224},{112... | collective-permute-start | bytes 61448 | tf_op jit(solution)/shard_map/ppermute | solution.py:357
  41.2 5.7 %collective-permute-start.7 = (bf16[16,640]{1,0:T(8,128)(2,1)S(1)}, bf16[16,640]{1,0:T(8,128)(2,1)S(1)}, u32[]{:S(2)}, u32[]{:S(2)}) collective-permute-start(bf16[16,640]{1,0:T(8,128)(2,1)S(1)} %get-tuple-element.42), channel_id=1, source_target_pairs={{0,129},{1,128},{2,131},{3,130},{4,133},{5,132},{6,135},{7,134},{8... | collective-permute-start | bytes 61448 | tf_op jit(solution)/shard_map/ppermute | solution.py:405
  41.2 5.7 %collective-permute-start.5 = (bf16[32,640]{1,0:T(8,128)(2,1)S(1)}, bf16[32,640]{1,0:T(8,128)(2,1)S(1)}, u32[]{:S(2)}, u32[]{:S(2)}) collective-permute-start(bf16[32,640]{1,0:T(8,128)(2,1)S(1)} %get-tuple-element.40), channel_id=1, source_target_pairs={{0,1},{1,0},{2,3},{3,2},{4,5},{5,4},{6,7},{7,6},{8,9},{9,8},{10,11... | collective-permute-start | bytes 122888 | tf_op jit(solution)/shard_map/ppermute | solution.py:351
  47.0 5.7 %collective-permute-start.10 = (bf16[8,640]{1,0:T(8,128)(2,1)S(1)}, bf16[8,640]{1,0:T(8,128)(2,1)S(1)}, u32[]{:S(2)}, u32[]{:S(2)}) collective-permute-start(bf16[8,640]{1,0:T(8,128)(2,1)S(1)} %pad_maximum_fusion.7), channel_id=1, source_target_pairs={{0,96},{16,112},{32,64},{48,80},{64,32},{80,48},{96,0},{112,16},{1... | collective-permute-start | bytes 30728 | tf_op jit(solution)/shard_map/ppermute | solution.py:357
  49.4 4.2 %collective-permute-start.9 = (bf16[8,640]{1,0:T(8,128)(2,1)S(1)}, bf16[8,640]{1,0:T(8,128)(2,1)S(1)}, u32[]{:S(2)}, u32[]{:S(2)}) collective-permute-start(bf16[8,640]{1,0:T(8,128)(2,1)S(1)} %pad_maximum_fusion.6), channel_id=1, source_target_pairs={{0,64},{16,80},{32,96},{48,112},{64,0},{80,16},{96,32},{112,48},{1... | collective-permute-start | bytes 30728 | tf_op jit(solution)/shard_map/ppermute | solution.py:357
  52.6 2.6 %collective-permute-start.8 = (bf16[8,640]{1,0:T(8,128)(2,1)S(1)}, bf16[8,640]{1,0:T(8,128)(2,1)S(1)}, u32[]{:S(2)}, u32[]{:S(2)}) collective-permute-start(bf16[8,640]{1,0:T(8,128)(2,1)S(1)} %pad_maximum_fusion.5), channel_id=1, source_target_pairs={{0,32},{16,48},{32,0},{48,16},{64,96},{80,112},{96,64},{112,80},{1... | collective-permute-start | bytes 30728 | tf_op jit(solution)/shard_map/ppermute | solution.py:357
  55.2 31.9 %all-to-all-start.1 = ((bf16[16,2,96,256]{3,2,1,0:T(8,128)(2,1)}), bf16[16,2,96,256]{3,2,1,0:T(8,128)(2,1)}, u32[]{:S(2)}, u32[]{:S(2)}) async-start(bf16[16,2,96,256]{3,2,1,0:T(8,128)(2,1)} %bitcast.48), calls=%async_computation.1 | async-start | bytes 3145728 | tf_op jit(solution)/shard_map/all_to_all | solution.py:361
  64.3 1.3 %collective-permute-start.11 = (bf16[16,640]{1,0:T(8,128)(2,1)S(1)}, bf16[16,640]{1,0:T(8,128)(2,1)S(1)}, u32[]{:S(2)}, u32[]{:S(2)}) collective-permute-start(bf16[16,640]{1,0:T(8,128)(2,1)S(1)} %reshape_squeeze.7), channel_id=1, source_target_pairs={{0,16},{16,0},{32,48},{48,32},{64,80},{80,64},{96,112},{112,96},{1... | collective-permute-start | bytes 61448 | tf_op jit(solution)/shard_map/ppermute | solution.py:357
  65.6 12.1 %collective-permute-start.12 = (bf16[48,640]{1,0:T(8,128)(2,1)S(1)}, bf16[48,640]{1,0:T(8,128)(2,1)S(1)}, u32[]{:S(2)}, u32[]{:S(2)}) collective-permute-start(bf16[48,640]{1,0:T(8,128)(2,1)S(1)} %pad_maximum_fusion.3.refs_0_), channel_id=1, source_target_pairs={{0,2},{1,3},{2,4},{3,5},{4,6},{5,7},{6,8},{7,9},{8,10},{9,11},{10,... | collective-permute-start | bytes 184328 | tf_op jit(solution)/shard_map/ppermute | solution.py:354
  67.2 10.4 %collective-permute-start.13 = (bf16[48,640]{1,0:T(8,128)(2,1)S(1)}, bf16[48,640]{1,0:T(8,128)(2,1)S(1)}, u32[]{:S(2)}, u32[]{:S(2)}) collective-permute-start(bf16[48,640]{1,0:T(8,128)(2,1)S(1)} %pad_maximum_fusion.3.refs_0_), channel_id=1, source_target_pairs={{0,14},{1,15},{2,0},{3,1},{4,2},{5,3},{6,4},{7,5},{8,6},{9,7},{10,... | collective-permute-start | bytes 184328 | tf_op jit(solution)/shard_map/ppermute | solution.py:354
  71.5 7.4 %collective-permute-start.14 = (bf16[48,640]{1,0:T(8,128)(2,1)S(1)}, bf16[48,640]{1,0:T(8,128)(2,1)S(1)}, u32[]{:S(2)}, u32[]{:S(2)}) collective-permute-start(bf16[48,640]{1,0:T(8,128)(2,1)S(1)} %pad_maximum_fusion.3.refs_0_), channel_id=1, source_target_pairs={{0,8},{1,9},{2,10},{3,11},{4,12},{5,13},{6,14},{7,15},{8,0},{9,1},... | collective-permute-start | bytes 184328 | tf_op jit(solution)/shard_map/ppermute | solution.py:354
  78.9 10.3 %collective-permute-start.15 = (bf16[96,640]{1,0:T(8,128)(2,1)S(1)}, bf16[96,640]{1,0:T(8,128)(2,1)S(1)}, u32[]{:S(2)}, u32[]{:S(2)}) collective-permute-start(bf16[96,640]{1,0:T(8,128)(2,1)S(1)} %get-tuple-element.59), channel_id=1, source_target_pairs={{0,4},{1,5},{2,6},{3,7},{4,8},{5,9},{6,10},{7,11},{8,12},{9,13},{1... | collective-permute-start | bytes 368648 | tf_op jit(solution)/shard_map/ppermute | solution.py:354
  79.0 10.3 %collective-permute-start.16 = (bf16[96,640]{1,0:T(8,128)(2,1)S(1)}, bf16[96,640]{1,0:T(8,128)(2,1)S(1)}, u32[]{:S(2)}, u32[]{:S(2)}) collective-permute-start(bf16[96,640]{1,0:T(8,128)(2,1)S(1)} %get-tuple-element.58), channel_id=1, source_target_pairs={{0,12},{1,13},{2,14},{3,15},{4,0},{5,1},{6,2},{7,3},{8,4},{9,5},{1... | collective-permute-start | bytes 368648 | tf_op jit(solution)/shard_map/ppermute | solution.py:354

commit v4 on v3

--- a/solution.py
+++ b/solution.py
@@ -11,7 +11,7 @@
 REQ = 16
 HD = 128
 NZ = 8
-CUT = 160
+CUT = 144
 SMEM = pltpu.SMEM
 VMEM = pltpu.VMEM
 VMEM_LIMIT = 63 * 1024 * 1024
@@ -67,7 +67,8 @@
     return lax.axis_index("pool") * lax.axis_size("group") + lax.axis_index("group")
 
 
-def pack_kernel(pairing_in, lengths_in, own_in, new_cache, early, late, buf, own, pairing, lengths, taken, count, small_sem, in_sem, early_sem, late_sem):
+def pack_kernel(start, pairing_in, lengths_in, own_in, new_cache, send, buf, own, pairing, lengths, taken, count, small_sem, in_sem, out_sem):
+    tokens = send.shape[1]
     small = [
         pltpu.make_async_copy(pairing_in, pairing, small_sem.at[0]),
         pltpu.make_async_copy(lengths_in, lengths, small_sem.at[1]),
@@ -75,7 +76,9 @@
     ]
     for copy in small:
         copy.start()
-    load = pltpu.make_async_copy(new_cache, buf.at[pl.ds(0, REQ)], in_sem)
+    load = pltpu.make_async_copy(
+        new_cache.at[:, pl.ds(start, tokens)], buf.at[pl.ds(0, REQ)], in_sem
+    )
     load.start()
     buf[REQ] = jnp.zeros(buf.shape[1:], buf.dtype)
     for j in range(2 * REQ):
@@ -92,33 +95,28 @@
     row = lax.broadcasted_iota(jnp.int32, (16, 1), 0)
     load.wait()
     for i in range(REQ):
-        base = pl.multiple_of(lengths[i] // 16 * 16, 16)
-        window = buf[i, pl.ds(base, 16), :].astype(jnp.float32)
-        token = own[i : i + 1, :].astype(jnp.float32)
-        window = jnp.where(row == lengths[i] - base, token, window)
-        buf[i, pl.ds(base, 16), :] = window.astype(buf.dtype)
-    cut = early.shape[1]
+        at = lengths[i] - start
+
+        @pl.when((at >= 0) & (at < tokens))
+        def _():
+            base = pl.multiple_of(at // 16 * 16, 16)
+            window = buf[i, pl.ds(base, 16), :].astype(jnp.float32)
+            token = own[i : i + 1, :].astype(jnp.float32)
+            window = jnp.where(row == at - base, token, window)
+            buf[i, pl.ds(base, 16), :] = window.astype(buf.dtype)
+
     for j in range(2 * REQ):
-        request = buf.at[taken[j]]
-        pltpu.make_async_copy(request.at[pl.ds(0, cut)], early.at[j], early_sem).start()
-    for j in range(2 * REQ):
-        request = buf.at[taken[j]]
-        pltpu.make_async_copy(request.at[pl.ds(cut, late.shape[1])], late.at[j], late_sem).start()
-    pltpu.make_async_copy(early, early, early_sem).wait()
-    pltpu.make_async_copy(late, late, late_sem).wait()
-
-
-def pack(pairing, new_lengths, new_own, new_cache):
-    tokens = new_cache.shape[1]
-    any_space = pl.BlockSpec(memory_space=pltpu.HBM)
+        pltpu.make_async_copy(buf.at[taken[j]], send.at[j], out_sem).start()
+    pltpu.make_async_copy(send, send, out_sem).wait()
+
+
+def pack(pairing, new_lengths, new_own, new_cache, start, tokens):
+    hbm = pl.BlockSpec(memory_space=pltpu.HBM)
     return pl.pallas_call(
-        pack_kernel,
-        out_shape=[
-            jax.ShapeDtypeStruct((2 * REQ, CUT, 2 * HD), jnp.bfloat16),
-            jax.ShapeDtypeStruct((2 * REQ, tokens - CUT, 2 * HD), jnp.bfloat16),
-        ],
-        in_specs=[any_space] * 4,
-        out_specs=[any_space] * 2,
+        functools.partial(pack_kernel, start),
+        out_shape=jax.ShapeDtypeStruct((2 * REQ, tokens, 2 * HD), jnp.bfloat16),
+        in_specs=[hbm] * 4,
+        out_specs=hbm,
         scratch_shapes=[
             VMEM((REQ + 1, tokens, 2 * HD), jnp.bfloat16),
             VMEM(new_own.shape, jnp.bfloat16),
@@ -129,10 +127,9 @@
             pltpu.SemaphoreType.DMA((3,)),
             pltpu.SemaphoreType.DMA,
             pltpu.SemaphoreType.DMA,
-            pltpu.SemaphoreType.DMA,
         ],
         compiler_params=pltpu.CompilerParams(vmem_limit_bytes=VMEM_LIMIT),
-        cost_estimate=pl.CostEstimate(flops=1_000_000, bytes_accessed=6_400_000, transcendentals=0),
+        cost_estimate=pl.CostEstimate(flops=0, bytes_accessed=25_000 * tokens, transcendentals=0),
         name="pack",
     )(pairing, new_lengths, new_own, new_cache)
 
@@ -360,8 +357,9 @@
         blocks = array.reshape((groups, 2) + array.shape[1:])
         return lax.all_to_all(blocks, both, split_axis=0, concat_axis=0, tiled=True).reshape(array.shape)
 
-    early, late = pack(pair, new_lengths[0, 0], new_step_kv[0, 0, :, 0], prompts)
-    early = deliver(early)
+    prompt = (pair, new_lengths[0, 0], new_step_kv[0, 0, :, 0], prompts)
+    early = deliver(pack(*prompt, 0, CUT))
+    late = pack(*prompt, CUT, prompts.shape[1] - CUT)
 
     first, one_up, one_down, two_up, two_down, opposite, chosen = front(
         pair,
@@ -381,8 +379,8 @@
     from_below, from_above = round_z(two_up, 2), round_z(two_down, -2)
     opposite = round_z(opposite, 4)
     gain = norm_gain.reshape(1, -1)
-    from_below, from_above, opposite, gain = lax.optimization_barrier(
-        (from_below, from_above, opposite, gain)
+    from_below, from_above, opposite, gain, late = lax.optimization_barrier(
+        (from_below, from_above, opposite, gain, late)
     )
     one_up = (one_up + from_below[2 * REQ :].astype(jnp.float32)).astype(jnp.bfloat16)
     one_down = (one_down + from_above[2 * REQ :].astype(jnp.float32)).astype(jnp.bfloat16)
@@ -430,9 +428,11 @@
         in_specs=[vmem] * (len(blocks) + 1),
         out_specs=[vmem] * 2,
         compiler_params=pltpu.CompilerParams(vmem_limit_bytes=SMALL_LIMIT),
+        cost_estimate=pl.CostEstimate(flops=0, bytes_accessed=4_000_000, transcendentals=0),
         name="finish",
     )(gain, *blocks)
 
+    late, hidden = lax.optimization_barrier((late, hidden))
     slot_cache = place(late, CUT, slot_cache)
     return (hidden[None, None], normed[None, None], slot_cache[None, None, :, :, None, :])
 

time: 90.8 us -> 89.5 us (0.986)
  starting transfers between devices: 53.8 us -> 49.6 us
  Pallas kernels: 14.7 us -> 16.9 us
    ppermute x10, waiting for transfers between devices: 7.22 us -> 10.9 us  [round_z(): lax.ppermute(array, 'tp', [(t, (t + 2 * shift) % ranks) for t in range(ra...]
    ppermute x10, starting transfers between devices: 27 us -> 23.6 us  [round_z(): lax.ppermute(array, 'tp', [(t, (t + 2 * shift) % ranks) for t in range(ra...]
    ppermute x5, starting transfers between devices: 8.9 us -> 5.88 us  [over_groups(): return lax.ppermute(array, both, [(s, s ^ flip) for s in range(groups)])]
    ppermute x5, waiting for transfers between devices: 8.26 us -> 5.28 us  [over_groups(): return lax.ppermute(array, both, [(s, s ^ flip) for s in range(groups)])]
    ppermute x1, starting transfers between devices: 0.01 us -> 2.49 us  [body(): far_there = lax.ppermute(far, ('pool', 'tp'), across)]
    pallas_call x1 -> x2, Pallas kernels: 3.7 us -> 5.52 us  [pack(): pl.pallas_call(functools.partial(pack_kernel, start), out_shape=jax.Shape...]
    all_to_all x2, waiting for transfers between devices: 4.48 us -> 3.32 us  [deliver(): lax.all_to_all(blocks, both, split_axis=0, concat_axis=0, tiled=True)]
    ppermute x1, waiting for transfers between devices: 0.59 us -> 1.71 us  [body(): far_there = lax.ppermute(far, ('pool', 'tp'), across)]
  transfers between devices with their start and end apart: 19 -> 19, of which waited for: 10 -> 11; matrix products, arithmetic and copies ran while one was open for 0% -> 0% of each run, Pallas kernels for 11% -> 13%
where the time goes in v4:
time: 89.5 us; the launch traced here: 89.2 us
  starting transfers between devices  49.6 us (55%)
  waiting for transfers between devices  21.2 us (24%)
  Pallas kernels  16.9 us (19%)
  between operations  1.15 us (1%)
    ppermute x10, starting transfers between devices, round_z(): lax.ppermute(array, 'tp', [(t, (t + 2 * shift) % ranks) for t in range(ra...  23.6 us
    all_to_all x2, starting transfers between devices, deliver(): lax.all_to_all(blocks, both, split_axis=0, concat_axis=0, tiled=True)  17.3 us
    ppermute x10, waiting for transfers between devices, round_z(): lax.ppermute(array, 'tp', [(t, (t + 2 * shift) % ranks) for t in range(ra...  10.9 us
    ppermute x5, starting transfers between devices, over_groups(): return lax.ppermute(array, both, [(s, s ^ flip) for s in range(groups)])  5.88 us
    pallas_call x2, Pallas kernels, pack(): pl.pallas_call(functools.partial(pack_kernel, start), out_shape=jax.Shape...  5.52 us
    ppermute x5, waiting for transfers between devices, over_groups(): return lax.ppermute(array, both, [(s, s ^ flip) for s in range(groups)])  5.28 us
    pallas_call x1, Pallas kernels, front(): pl.pallas_call(front_kernel, out_shape=[jax.ShapeDtypeStruct((2 * REQ, wi...  5.13 us
    pallas_call x2, Pallas kernels, place(): pl.pallas_call(functools.partial(place_kernel, start), out_shape=jax.Shap...  4.9 us
  transfers between devices with their start and end apart: 19, of which 11 were waited for; matrix products, arithmetic and copies ran while one was open for 0% of the time, Pallas kernels for 13%

profile of v4, /device:TPU:1, one launch (start us, length us, event | category | flops | bytes accessed | tf_op | source)
XLA Modules:
  0.0 89.2 jit_solution(1692737010937314885)
XLA Ops:
  0.6 2.9 %pack.3 = bf16[32,144,256]{2,1,0:T(8,128)(2,1)} custom-call(s32[16]{0:T(128)} %bitcast.38, s32[16]{0:T(128)} %bitcast.41, bf16[16,256]{1,0:T(8,128)(2,1)} %bitcast.32, bf16[16,256,256]{2,1,0:T(8,128)(2,1)} %bitcast.46), custom_call_target="tpu_custom_call" | custom-call | bytes 3600000 | tf_op jit(solution)/shard_map/pack/pallas_call | solution.py:115
  3.5 0.0 copy-start
  3.5 0.0 copy-start.1
  3.5 0.0 copy-start.2
  3.6 0.0 copy-start.3
  3.6 0.0 copy-start.4
  3.6 0.0 copy-start.5
  3.6 0.0 copy-start.6
  3.6 0.0 copy-start.7
  3.6 0.0 copy-start.8
  3.6 0.0 copy-start.9
  3.6 8.6 %all-to-all-start.1 = ((bf16[16,2,144,256]{3,2,1,0:T(8,128)(2,1)}), bf16[16,2,144,256]{3,2,1,0:T(8,128)(2,1)}, u32[]{:S(2)}, u32[]{:S(2)}) async-start(bf16[16,2,144,256]{3,2,1,0:T(8,128)(2,1)} %bitcast.50), calls=%async_computation.1 | async-start | bytes 4718592 | tf_op jit(solution)/shard_map/all_to_all | solution.py:358
  12.2 0.0 copy-done
  12.2 0.0 copy-done.1
  12.2 0.0 copy-done.2
  12.3 0.0 copy-done.3
  12.3 0.0 copy-done.4
  12.3 0.0 copy-done.5
  12.3 0.0 copy-done.6
  12.3 5.1 %front.1 = (f32[32,640]{1,0:T(8,128)S(1)}, f32[32,640]{1,0:T(8,128)S(1)}, f32[32,640]{1,0:T(8,128)S(1)}, bf16[64,640]{1,0:T(8,128)(2,1)S(1)}, bf16[64,640]{1,0:T...) custom-call(s32[16]{0:T(128)S(1)} %bitcast.40, s32[16]{0:T(128)S(1)} %bitcast.44, ...), custom_call_target="tpu_custom_call" | custom-call | flops 400000000 | bytes 9500000 | tf_op jit(solution)/shard_map/front/pallas_call | solution.py:218
  17.5 0.0 copy-start.10
  17.5 3.1 %collective-permute-start = (bf16[64,640]{1,0:T(8,128)(2,1)S(1)}, bf16[64,640]{1,0:T(8,128)(2,1)S(1)}, u32[]{:S(2)}, u32[]{:S(2)}) collective-permute-start(bf16[64,640]{1,0:T(8,128)(2,1)S(1)} %get-tuple-element.30), channel_id=1, source_target_pairs={{0,4},{1,5},{2,6},{3,7},{4,8},{5,9},{6,10},{7,11},{8,12},{9,13},{1... | collective-permute-start | bytes 245768 | tf_op jit(solution)/shard_map/ppermute | solution.py:351
  20.5 3.1 %collective-permute-start.1 = (bf16[64,640]{1,0:T(8,128)(2,1)S(1)}, bf16[64,640]{1,0:T(8,128)(2,1)S(1)}, u32[]{:S(2)}, u32[]{:S(2)}) collective-permute-start(bf16[64,640]{1,0:T(8,128)(2,1)S(1)} %get-tuple-element.31), channel_id=1, source_target_pairs={{0,12},{1,13},{2,14},{3,15},{4,0},{5,1},{6,2},{7,3},{8,4},{9,5},{1... | collective-permute-start | bytes 245768 | tf_op jit(solution)/shard_map/ppermute | solution.py:351
  23.7 4.4 %collective-permute-start.2 = (bf16[32,640]{1,0:T(8,128)(2,1)S(1)}, bf16[32,640]{1,0:T(8,128)(2,1)S(1)}, u32[]{:S(2)}, u32[]{:S(2)}) collective-permute-start(bf16[32,640]{1,0:T(8,128)(2,1)S(1)} %get-tuple-element.32), channel_id=1, source_target_pairs={{0,8},{1,9},{2,10},{3,11},{4,12},{5,13},{6,14},{7,15},{8,0},{9,1},... | collective-permute-start | bytes 122888 | tf_op jit(solution)/shard_map/ppermute | solution.py:351
  28.0 2.6 %pack.2 = bf16[32,112,256]{2,1,0:T(8,128)(2,1)} custom-call(s32[16]{0:T(128)} %bitcast.39, s32[16]{0:T(128)} %bitcast.42, bf16[16,256]{1,0:T(8,128)(2,1)} %bitcast.33, bf16[16,256,256]{2,1,0:T(8,128)(2,1)} %bitcast.48), custom_call_target="tpu_custom_call" | custom-call | bytes 2800000 | tf_op jit(solution)/shard_map/pack/pallas_call | solution.py:115
  30.7 0.0 copy-done.10
  30.7 0.2 collective-permute-done.2.refs_2_
  30.9 0.0 collective-permute-done.refs_0_
  31.0 0.0 collective-permute-done.1.refs_1_
  31.0 3.2 %collective-permute-start.3 = (bf16[32,640]{1,0:T(8,128)(2,1)S(1)}, bf16[32,640]{1,0:T(8,128)(2,1)S(1)}, u32[]{:S(2)}, u32[]{:S(2)}) collective-permute-start(bf16[32,640]{1,0:T(8,128)(2,1)S(1)} %add_convert_fusion.2), channel_id=1, source_target_pairs={{0,2},{1,3},{2,4},{3,5},{4,6},{5,7},{6,8},{7,9},{8,10},{9,11},{10,... | collective-permute-start | bytes 122888 | tf_op jit(solution)/shard_map/ppermute | solution.py:351
  34.2 0.1 collective-permute-start.4
  34.3 1.2 %collective-permute-done.3.refs_3_ = bf16[32,640]{1,0:T(8,128)(2,1)S(1)} collective-permute-done((bf16[32,640]{1,0:T(8,128)(2,1)S(1)}, bf16[32,640]{1,0:T(8,128)(2,1)S(1)}, u32[]{:S(2)}, u32[]{:S(2)}) %collective-permute-start.3) | collective-permute-done | bytes 40992 | tf_op jit(solution)/shard_map/ppermute | solution.py:351
  35.5 2.0 %collective-permute-done.4.refs_4_ = bf16[32,640]{1,0:T(8,128)(2,1)S(1)} collective-permute-done((bf16[32,640]{1,0:T(8,128)(2,1)S(1)}, bf16[32,640]{1,0:T(8,128)(2,1)S(1)}, u32[]{:S(2)}, u32[]{:S(2)}) %collective-permute-start.4) | collective-permute-done | bytes 40992 | tf_op jit(solution)/shard_map/ppermute | solution.py:351
  37.5 0.1 spread.1
  37.7 2.5 %collective-permute-start.7 = (bf16[16,640]{1,0:T(8,128)(2,1)S(1)}, bf16[16,640]{1,0:T(8,128)(2,1)S(1)}, u32[]{:S(2)}, u32[]{:S(2)}) collective-permute-start(bf16[16,640]{1,0:T(8,128)(2,1)S(1)} %get-tuple-element.42), channel_id=1, source_target_pairs={{0,129},{1,128},{2,131},{3,130},{4,133},{5,132},{6,135},{7,134},{8... | collective-permute-start | bytes 61448 | tf_op jit(solution)/shard_map/ppermute | solution.py:403
  40.2 0.6 collective-permute-start.6
  40.7 0.3 collective-permute-start.5
  41.0 1.7 %collective-permute-done.7 = bf16[16,640]{1,0:T(8,128)(2,1)S(1)} collective-permute-done((bf16[16,640]{1,0:T(8,128)(2,1)S(1)}, bf16[16,640]{1,0:T(8,128)(2,1)S(1)}, u32[]{:S(2)}, u32[]{:S(2)}) %collective-permute-start.7) | collective-permute-done | bytes 20512 | tf_op jit(solution)/shard_map/ppermute | solution.py:403
  42.7 1.7 %collective-permute-done.6 = bf16[16,640]{1,0:T(8,128)(2,1)S(1)} collective-permute-done((bf16[16,640]{1,0:T(8,128)(2,1)S(1)}, bf16[16,640]{1,0:T(8,128)(2,1)S(1)}, u32[]{:S(2)}, u32[]{:S(2)}) %collective-permute-start.6) | collective-permute-done | bytes 20512 | tf_op jit(solution)/shard_map/ppermute | solution.py:354
  44.5 0.0 collective-permute-done.5
  44.5 2.4 %collective-permute-start.8 = (bf16[8,640]{1,0:T(8,128)(2,1)S(1)}, bf16[8,640]{1,0:T(8,128)(2,1)S(1)}, u32[]{:S(2)}, u32[]{:S(2)}) collective-permute-start(bf16[8,640]{1,0:T(8,128)(2,1)S(1)} %pad_maximum_fusion.5), channel_id=1, source_target_pairs={{0,32},{16,48},{32,0},{48,16},{64,96},{80,112},{96,64},{112,80},{1... | collective-permute-start | bytes 30728 | tf_op jit(solution)/shard_map/ppermute | solution.py:354
  47.0 1.4 %collective-permute-start.9 = (bf16[8,640]{1,0:T(8,128)(2,1)S(1)}, bf16[8,640]{1,0:T(8,128)(2,1)S(1)}, u32[]{:S(2)}, u32[]{:S(2)}) collective-permute-start(bf16[8,640]{1,0:T(8,128)(2,1)S(1)} %pad_maximum_fusion.6), channel_id=1, source_target_pairs={{0,64},{16,80},{32,96},{48,112},{64,0},{80,16},{96,32},{112,48},{1... | collective-permute-start | bytes 30728 | tf_op jit(solution)/shard_map/ppermute | solution.py:354
  48.4 1.2 %collective-permute-start.10 = (bf16[8,640]{1,0:T(8,128)(2,1)S(1)}, bf16[8,640]{1,0:T(8,128)(2,1)S(1)}, u32[]{:S(2)}, u32[]{:S(2)}) collective-permute-start(bf16[8,640]{1,0:T(8,128)(2,1)S(1)} %pad_maximum_fusion.7), channel_id=1, source_target_pairs={{0,96},{16,112},{32,64},{48,80},{64,32},{80,48},{96,0},{112,16},{1... | collective-permute-start | bytes 30728 | tf_op jit(solution)/shard_map/ppermute | solution.py:354
  49.6 0.0 collective-permute-done.8
  49.6 1.5 %collective-permute-done.9 = bf16[8,640]{1,0:T(8,128)(2,1)S(1)} collective-permute-done((bf16[8,640]{1,0:T(8,128)(2,1)S(1)}, bf16[8,640]{1,0:T(8,128)(2,1)S(1)}, u32[]{:S(2)}, u32[]{:S(2)}) %collective-permute-start.9) | collective-permute-done | bytes 10272 | tf_op jit(solution)/shard_map/ppermute | solution.py:354
  51.1 1.1 %collective-permute-done.10 = bf16[8,640]{1,0:T(8,128)(2,1)S(1)} collective-permute-done((bf16[8,640]{1,0:T(8,128)(2,1)S(1)}, bf16[8,640]{1,0:T(8,128)(2,1)S(1)}, u32[]{:S(2)}, u32[]{:S(2)}) %collective-permute-start.10) | collective-permute-done | bytes 10272 | tf_op jit(solution)/shard_map/ppermute | solution.py:354
  52.2 0.0 all-to-all-done.1
  52.2 8.7 %all-to-all-start = ((bf16[16,2,112,256]{3,2,1,0:T(8,128)(2,1)}), bf16[16,2,112,256]{3,2,1,0:T(8,128)(2,1)S(1)}, u32[]{:S(2)}, u32[]{:S(2)}) async-start(bf16[16,2,112,256]{3,2,1,0:T(8,128)(2,1)} %bitcast.51), calls=%async_computation | async-start | bytes 3670016 | tf_op jit(solution)/shard_map/all_to_all | solution.py:358
  61.1 0.3 collective-permute-start.11
  61.5 0.9 %collective-permute-done.11 = bf16[16,640]{1,0:T(8,128)(2,1)S(1)} collective-permute-done((bf16[16,640]{1,0:T(8,128)(2,1)S(1)}, bf16[16,640]{1,0:T(8,128)(2,1)S(1)}, u32[]{:S(2)}, u32[]{:S(2)}) %collective-permute-start.11) | collective-permute-done | bytes 20512 | tf_op jit(solution)/shard_map/ppermute | solution.py:354
  62.4 5.9 %collective-permute-start.14 = (bf16[48,640]{1,0:T(8,128)(2,1)S(1)}, bf16[48,640]{1,0:T(8,128)(2,1)S(1)}, u32[]{:S(2)}, u32[]{:S(2)}) collective-permute-start(bf16[48,640]{1,0:T(8,128)(2,1)S(1)} %pad_maximum_fusion.3.refs_0_), channel_id=1, source_target_pairs={{0,8},{1,9},{2,10},{3,11},{4,12},{5,13},{6,14},{7,15},{8,0},{9,1},... | collective-permute-start | bytes 184328 | tf_op jit(solution)/shard_map/ppermute | solution.py:351
  68.3 0.0 collective-permute-start.13
  68.3 1.4 %collective-permute-start.12 = (bf16[48,640]{1,0:T(8,128)(2,1)S(1)}, bf16[48,640]{1,0:T(8,128)(2,1)S(1)}, u32[]{:S(2)}, u32[]{:S(2)}) collective-permute-start(bf16[48,640]{1,0:T(8,128)(2,1)S(1)} %pad_maximum_fusion.3.refs_0_), channel_id=1, source_target_pairs={{0,2},{1,3},{2,4},{3,5},{4,6},{5,7},{6,8},{7,9},{8,10},{9,11},{10,... | collective-permute-start | bytes 184328 | tf_op jit(solution)/shard_map/ppermute | solution.py:351
  69.8 2.5 %place.2.refs_0_ = bf16[32,256,256]{2,1,0:T(8,128)(2,1)} custom-call(bf16[32,144,256]{2,1,0:T(8,128)(2,1)} %bitcast.15.part), custom_call_target="tpu_custom_call" | custom-call | bytes 4718592 | tf_op jit(solution)/shard_map/place/pallas_call | solution.py:307
  72.3 0.0 collective-permute-done.14.refs_3_
  72.3 1.3 %collective-permute-done.13.refs_2_ = bf16[48,640]{1,0:T(8,128)(2,1)S(1)} collective-permute-done((bf16[48,640]{1,0:T(8,128)(2,1)S(1)}, bf16[48,640]{1,0:T(8,128)(2,1)S(1)}, u32[]{:S(2)}, u32[]{:S(2)}) %collective-permute-start.13) | collective-permute-done | bytes 61472 | tf_op jit(solution)/shard_map/ppermute | solution.py:351
  73.6 0.0 collective-permute-done.12.refs_1_
  73.7 1.2 %collective-permute-start.16 = (bf16[96,640]{1,0:T(8,128)(2,1)S(1)}, bf16[96,640]{1,0:T(8,128)(2,1)S(1)}, u32[]{:S(2)}, u32[]{:S(2)}) collective-permute-start(bf16[96,640]{1,0:T(8,128)(2,1)S(1)} %get-tuple-element.60), channel_id=1, source_target_pairs={{0,12},{1,13},{2,14},{3,15},{4,0},{5,1},{6,2},{7,3},{8,4},{9,5},{1... | collective-permute-start | bytes 368648 | tf_op jit(solution)/shard_map/ppermute | solution.py:351
  74.8 1.3 %collective-permute-start.15 = (bf16[96,640]{1,0:T(8,128)(2,1)S(1)}, bf16[96,640]{1,0:T(8,128)(2,1)S(1)}, u32[]{:S(2)}, u32[]{:S(2)}) collective-permute-start(bf16[96,640]{1,0:T(8,128)(2,1)S(1)} %get-tuple-element.61), channel_id=1, source_target_pairs={{0,4},{1,5},{2,6},{3,7},{4,8},{5,9},{6,10},{7,11},{8,12},{9,13},{1... | collective-permute-start | bytes 368648 | tf_op jit(solution)/shard_map/ppermute | solution.py:351
  76.1 6.1 %collective-permute-done.16.refs_5_ = bf16[96,640]{1,0:T(8,128)(2,1)S(1)} collective-permute-done((bf16[96,640]{1,0:T(8,128)(2,1)S(1)}, bf16[96,640]{1,0:T(8,128)(2,1)S(1)}, u32[]{:S(2)}, u32[]{:S(2)}) %collective-permute-start.16) | collective-permute-done | bytes 122912 | tf_op jit(solution)/shard_map/ppermute | solution.py:351
  82.2 0.0 collective-permute-done.15.refs_4_
  82.2 1.2 %finish.1 = (bf16[48,5120]{1,0:T(8,128)(2,1)}, bf16[48,5120]{1,0:T(8,128)(2,1)}) custom-call(bf16[1,5120]{1,0:T(2,128)(2,1)S(1)} %reshape.30.gain, bf16[48,640]{1,0:T(8,128)(2,1)S(1)} %pad_maximum_fusion.3.refs_0_, bf16[48,640]{1,0:T(8,128)(2,1)S(1)} %collective-permute-done.12.refs_1_, bf16[48,640]{1,0:T(8,128)(2,1)S(1)} %collective-permute-done.13.refs_2_, ...), custom_call_target="tpu_custom_call" | custom-call | bytes 4000000 | tf_op jit(solution)/shard_map/finish/pallas_call | solution.py:425
  83.4 3.3 %all-to-all-done = bf16[16,2,112,256]{3,2,1,0:T(8,128)(2,1)S(1)} async-done(((bf16[16,2,112,256]{3,2,1,0:T(8,128)(2,1)}), bf16[16,2,112,256]{3,2,1,0:T(8,128)(2,1)S(1)}, u32[]{:S(2)}, u32[]{:S(2)}) %all-to-all-start) | async-done | bytes 1835040 | tf_op jit(solution)/shard_map/all_to_all | solution.py:358
  86.7 2.4 %place.3 = bf16[32,256,256]{2,1,0:T(8,128)(2,1)} custom-call(bf16[32,112,256]{2,1,0:T(8,128)(2,1)S(1)} %bitcast.29, bf16[32,256,256]{2,1,0:T(8,128)(2,1)} %place.2.refs_0_), custom_call_target="tpu_custom_call", output_to_operand_aliasing={{}: (1, {})} | custom-call | bytes 3670016 | tf_op jit(solution)/shard_map/place/pallas_call | solution.py:307
  (28 shorter events, 0.3 us)
Async XLA Ops:
  3.5 8.7 %copy-start = (bf16[1,1,16,5120]{3,2,1,0:T(8,128)(2,1)S(1)}, bf16[1,1,16,5120]{3,2,1,0:T(8,128)(2,1)}, u32[]{:S(2)}) copy-start(bf16[1,1,16,5120]{3,2,1,0:T(8,128)(2,1)} %param.19) | copy-start | bytes 491524
  3.5 8.7 %copy-start.1 = (bf16[1,1,16,5120]{3,2,1,0:T(8,128)(2,1)S(1)}, bf16[1,1,16,5120]{3,2,1,0:T(8,128)(2,1)}, u32[]{:S(2)}) copy-start(bf16[1,1,16,5120]{3,2,1,0:T(8,128)(2,1)} %param.24) | copy-start | bytes 491524
  3.5 8.7 %copy-start.2 = (bf16[1,1,16,1,256]{4,2,3,1,0:T(8,128)(2,1)S(1)}, bf16[1,1,16,1,256]{4,2,3,1,0:T(8,128)(2,1)}, u32[]{:S(2)}) copy-start(bf16[1,1,16,1,256]{4,2,3,1,0:T(8,128)(2,1)} %param.23) | copy-start | bytes 24580
  3.6 8.7 %copy-start.3 = (bf16[1,1,16,256]{3,2,1,0:T(8,128)(2,1)S(1)}, bf16[1,1,16,256]{3,2,1,0:T(8,128)(2,1)}, u32[]{:S(2)}) copy-start(bf16[1,1,16,256]{3,2,1,0:T(8,128)(2,1)} %param.17) | copy-start | bytes 24580
  3.6 8.7 %copy-start.4 = (bf16[1,1,16,1,256]{4,2,3,1,0:T(8,128)(2,1)S(1)}, bf16[1,1,16,1,256]{4,2,3,1,0:T(8,128)(2,1)}, u32[]{:S(2)}) copy-start(bf16[1,1,16,1,256]{4,2,3,1,0:T(8,128)(2,1)} %param.18) | copy-start | bytes 24580
  3.6 8.7 %copy-start.5 = (bf16[1,1,16,256]{3,2,1,0:T(8,128)(2,1)S(1)}, bf16[1,1,16,256]{3,2,1,0:T(8,128)(2,1)}, u32[]{:S(2)}) copy-start(bf16[1,1,16,256]{3,2,1,0:T(8,128)(2,1)} %param.22) | copy-start | bytes 24580
  3.6 8.7 %copy-start.6 = (s32[1,1,16,1]{2,3,1,0:T(1,128)S(1)}, s32[1,1,16,1]{2,3,1,0:T(1,128)}, u32[]{:S(2)}) copy-start(s32[1,1,16,1]{2,3,1,0:T(1,128)} %param.25) | copy-start | bytes 196
  3.6 8.7 %copy-start.7 = (s32[1,1,16]{2,1,0:T(1,128)S(1)}, s32[1,1,16]{2,1,0:T(1,128)}, u32[]{:S(2)}) copy-start(s32[1,1,16]{2,1,0:T(1,128)} %param.21) | copy-start | bytes 196
  3.6 8.7 %copy-start.8 = (s32[1,1,16]{2,1,0:T(1,128)S(1)}, s32[1,1,16]{2,1,0:T(1,128)}, u32[]{:S(2)}) copy-start(s32[1,1,16]{2,1,0:T(1,128)} %param.16) | copy-start | bytes 196
  3.6 8.7 %copy-start.9 = (s32[1,1,64]{2,1,0:T(1,128)S(1)}, s32[1,1,64]{2,1,0:T(1,128)}, u32[]{:S(2)}) copy-start(s32[1,1,64]{2,1,0:T(1,128)} %param.15) | copy-start | bytes 772
  3.6 48.6 %all-to-all-start.1 = ((bf16[16,2,144,256]{3,2,1,0:T(8,128)(2,1)}), bf16[16,2,144,256]{3,2,1,0:T(8,128)(2,1)}, u32[]{:S(2)}, u32[]{:S(2)}) async-start(bf16[16,2,144,256]{3,2,1,0:T(8,128)(2,1)} %bitcast.50), calls=%async_computation.1 | async-start | bytes 4718592 | tf_op jit(solution)/shard_map/all_to_all | solution.py:358
  17.5 13.2 %copy-start.10 = (bf16[5120]{0:T(1024)(128)(2,1)S(1)}, bf16[5120]{0:T(1024)(128)(2,1)}, u32[]{:S(2)}) copy-start(bf16[5120]{0:T(1024)(128)(2,1)} %param.27) | copy-start | bytes 30724
  17.5 13.5 %collective-permute-start = (bf16[64,640]{1,0:T(8,128)(2,1)S(1)}, bf16[64,640]{1,0:T(8,128)(2,1)S(1)}, u32[]{:S(2)}, u32[]{:S(2)}) collective-permute-start(bf16[64,640]{1,0:T(8,128)(2,1)S(1)} %get-tuple-element.30), channel_id=1, source_target_pairs={{0,4},{1,5},{2,6},{3,7},{4,8},{5,9},{6,10},{7,11},{8,12},{9,13},{1... | collective-permute-start | bytes 245768 | tf_op jit(solution)/shard_map/ppermute | solution.py:351
  20.5 10.4 %collective-permute-start.1 = (bf16[64,640]{1,0:T(8,128)(2,1)S(1)}, bf16[64,640]{1,0:T(8,128)(2,1)S(1)}, u32[]{:S(2)}, u32[]{:S(2)}) collective-permute-start(bf16[64,640]{1,0:T(8,128)(2,1)S(1)} %get-tuple-element.31), channel_id=1, source_target_pairs={{0,12},{1,13},{2,14},{3,15},{4,0},{5,1},{6,2},{7,3},{8,4},{9,5},{1... | collective-permute-start | bytes 245768 | tf_op jit(solution)/shard_map/ppermute | solution.py:351
  23.7 7.3 %collective-permute-start.2 = (bf16[32,640]{1,0:T(8,128)(2,1)S(1)}, bf16[32,640]{1,0:T(8,128)(2,1)S(1)}, u32[]{:S(2)}, u32[]{:S(2)}) collective-permute-start(bf16[32,640]{1,0:T(8,128)(2,1)S(1)} %get-tuple-element.32), channel_id=1, source_target_pairs={{0,8},{1,9},{2,10},{3,11},{4,12},{5,13},{6,14},{7,15},{8,0},{9,1},... | collective-permute-start | bytes 122888 | tf_op jit(solution)/shard_map/ppermute | solution.py:351
  31.0 4.5 %collective-permute-start.3 = (bf16[32,640]{1,0:T(8,128)(2,1)S(1)}, bf16[32,640]{1,0:T(8,128)(2,1)S(1)}, u32[]{:S(2)}, u32[]{:S(2)}) collective-permute-start(bf16[32,640]{1,0:T(8,128)(2,1)S(1)} %add_convert_fusion.2), channel_id=1, source_target_pairs={{0,2},{1,3},{2,4},{3,5},{4,6},{5,7},{6,8},{7,9},{8,10},{9,11},{10,... | collective-permute-start | bytes 122888 | tf_op jit(solution)/shard_map/ppermute | solution.py:351
  34.2 3.3 %collective-permute-start.4 = (bf16[32,640]{1,0:T(8,128)(2,1)S(1)}, bf16[32,640]{1,0:T(8,128)(2,1)S(1)}, u32[]{:S(2)}, u32[]{:S(2)}) collective-permute-start(bf16[32,640]{1,0:T(8,128)(2,1)S(1)} %add_convert_fusion.1), channel_id=1, source_target_pairs={{0,14},{1,15},{2,0},{3,1},{4,2},{5,3},{6,4},{7,5},{8,6},{9,7},{10,... | collective-permute-start | bytes 122888 | tf_op jit(solution)/shard_map/ppermute | solution.py:351
  37.7 5.1 %collective-permute-start.7 = (bf16[16,640]{1,0:T(8,128)(2,1)S(1)}, bf16[16,640]{1,0:T(8,128)(2,1)S(1)}, u32[]{:S(2)}, u32[]{:S(2)}) collective-permute-start(bf16[16,640]{1,0:T(8,128)(2,1)S(1)} %get-tuple-element.42), channel_id=1, source_target_pairs={{0,129},{1,128},{2,131},{3,130},{4,133},{5,132},{6,135},{7,134},{8... | collective-permute-start | bytes 61448 | tf_op jit(solution)/shard_map/ppermute | solution.py:403
  40.2 4.3 %collective-permute-start.6 = (bf16[16,640]{1,0:T(8,128)(2,1)S(1)}, bf16[16,640]{1,0:T(8,128)(2,1)S(1)}, u32[]{:S(2)}, u32[]{:S(2)}) collective-permute-start(bf16[16,640]{1,0:T(8,128)(2,1)S(1)} %get-tuple-element.42), channel_id=1, source_target_pairs={{0,128},{16,144},{32,160},{48,176},{64,192},{80,208},{96,224},{112... | collective-permute-start | bytes 61448 | tf_op jit(solution)/shard_map/ppermute | solution.py:354
  40.7 3.7 %collective-permute-start.5 = (bf16[32,640]{1,0:T(8,128)(2,1)S(1)}, bf16[32,640]{1,0:T(8,128)(2,1)S(1)}, u32[]{:S(2)}, u32[]{:S(2)}) collective-permute-start(bf16[32,640]{1,0:T(8,128)(2,1)S(1)} %get-tuple-element.41), channel_id=1, source_target_pairs={{0,1},{1,0},{2,3},{3,2},{4,5},{5,4},{6,7},{7,6},{8,9},{9,8},{10,11... | collective-permute-start | bytes 122888 | tf_op jit(solution)/shard_map/ppermute | solution.py:348
  44.5 5.0 %collective-permute-start.8 = (bf16[8,640]{1,0:T(8,128)(2,1)S(1)}, bf16[8,640]{1,0:T(8,128)(2,1)S(1)}, u32[]{:S(2)}, u32[]{:S(2)}) collective-permute-start(bf16[8,640]{1,0:T(8,128)(2,1)S(1)} %pad_maximum_fusion.5), channel_id=1, source_target_pairs={{0,32},{16,48},{32,0},{48,16},{64,96},{80,112},{96,64},{112,80},{1... | collective-permute-start | bytes 30728 | tf_op jit(solution)/shard_map/ppermute | solution.py:354
  47.0 4.1 %collective-permute-start.9 = (bf16[8,640]{1,0:T(8,128)(2,1)S(1)}, bf16[8,640]{1,0:T(8,128)(2,1)S(1)}, u32[]{:S(2)}, u32[]{:S(2)}) collective-permute-start(bf16[8,640]{1,0:T(8,128)(2,1)S(1)} %pad_maximum_fusion.6), channel_id=1, source_target_pairs={{0,64},{16,80},{32,96},{48,112},{64,0},{80,16},{96,32},{112,48},{1... | collective-permute-start | bytes 30728 | tf_op jit(solution)/shard_map/ppermute | solution.py:354
  48.4 3.8 %collective-permute-start.10 = (bf16[8,640]{1,0:T(8,128)(2,1)S(1)}, bf16[8,640]{1,0:T(8,128)(2,1)S(1)}, u32[]{:S(2)}, u32[]{:S(2)}) collective-permute-start(bf16[8,640]{1,0:T(8,128)(2,1)S(1)} %pad_maximum_fusion.7), channel_id=1, source_target_pairs={{0,96},{16,112},{32,64},{48,80},{64,32},{80,48},{96,0},{112,16},{1... | collective-permute-start | bytes 30728 | tf_op jit(solution)/shard_map/ppermute | solution.py:354
  52.2 34.5 %all-to-all-start = ((bf16[16,2,112,256]{3,2,1,0:T(8,128)(2,1)}), bf16[16,2,112,256]{3,2,1,0:T(8,128)(2,1)S(1)}, u32[]{:S(2)}, u32[]{:S(2)}) async-start(bf16[16,2,112,256]{3,2,1,0:T(8,128)(2,1)} %bitcast.51), calls=%async_computation | async-start | bytes 3670016 | tf_op jit(solution)/shard_map/all_to_all | solution.py:358
  61.1 1.3 %collective-permute-start.11 = (bf16[16,640]{1,0:T(8,128)(2,1)S(1)}, bf16[16,640]{1,0:T(8,128)(2,1)S(1)}, u32[]{:S(2)}, u32[]{:S(2)}) collective-permute-start(bf16[16,640]{1,0:T(8,128)(2,1)S(1)} %reshape_squeeze.7), channel_id=1, source_target_pairs={{0,16},{16,0},{32,48},{48,32},{64,80},{80,64},{96,112},{112,96},{1... | collective-permute-start | bytes 61448 | tf_op jit(solution)/shard_map/ppermute | solution.py:354
  62.4 9.9 %collective-permute-start.14 = (bf16[48,640]{1,0:T(8,128)(2,1)S(1)}, bf16[48,640]{1,0:T(8,128)(2,1)S(1)}, u32[]{:S(2)}, u32[]{:S(2)}) collective-permute-start(bf16[48,640]{1,0:T(8,128)(2,1)S(1)} %pad_maximum_fusion.3.refs_0_), channel_id=1, source_target_pairs={{0,8},{1,9},{2,10},{3,11},{4,12},{5,13},{6,14},{7,15},{8,0},{9,1},... | collective-permute-start | bytes 184328 | tf_op jit(solution)/shard_map/ppermute | solution.py:351
  68.3 5.3 %collective-permute-start.13 = (bf16[48,640]{1,0:T(8,128)(2,1)S(1)}, bf16[48,640]{1,0:T(8,128)(2,1)S(1)}, u32[]{:S(2)}, u32[]{:S(2)}) collective-permute-start(bf16[48,640]{1,0:T(8,128)(2,1)S(1)} %pad_maximum_fusion.3.refs_0_), channel_id=1, source_target_pairs={{0,14},{1,15},{2,0},{3,1},{4,2},{5,3},{6,4},{7,5},{8,6},{9,7},{10,... | collective-permute-start | bytes 184328 | tf_op jit(solution)/shard_map/ppermute | solution.py:351
  68.3 5.3 %collective-permute-start.12 = (bf16[48,640]{1,0:T(8,128)(2,1)S(1)}, bf16[48,640]{1,0:T(8,128)(2,1)S(1)}, u32[]{:S(2)}, u32[]{:S(2)}) collective-permute-start(bf16[48,640]{1,0:T(8,128)(2,1)S(1)} %pad_maximum_fusion.3.refs_0_), channel_id=1, source_target_pairs={{0,2},{1,3},{2,4},{3,5},{4,6},{5,7},{6,8},{7,9},{8,10},{9,11},{10,... | collective-permute-start | bytes 184328 | tf_op jit(solution)/shard_map/ppermute | solution.py:351
  73.7 8.5 %collective-permute-start.16 = (bf16[96,640]{1,0:T(8,128)(2,1)S(1)}, bf16[96,640]{1,0:T(8,128)(2,1)S(1)}, u32[]{:S(2)}, u32[]{:S(2)}) collective-permute-start(bf16[96,640]{1,0:T(8,128)(2,1)S(1)} %get-tuple-element.60), channel_id=1, source_target_pairs={{0,12},{1,13},{2,14},{3,15},{4,0},{5,1},{6,2},{7,3},{8,4},{9,5},{1... | collective-permute-start | bytes 368648 | tf_op jit(solution)/shard_map/ppermute | solution.py:351
  74.8 7.3 %collective-permute-start.15 = (bf16[96,640]{1,0:T(8,128)(2,1)S(1)}, bf16[96,640]{1,0:T(8,128)(2,1)S(1)}, u32[]{:S(2)}, u32[]{:S(2)}) collective-permute-start(bf16[96,640]{1,0:T(8,128)(2,1)S(1)} %get-tuple-element.61), channel_id=1, source_target_pairs={{0,4},{1,5},{2,6},{3,7},{4,8},{5,9},{6,10},{7,11},{8,12},{9,13},{1... | collective-permute-start | bytes 368648 | tf_op jit(solution)/shard_map/ppermute | solution.py:351

commit v5 on v4

--- a/solution.py
+++ b/solution.py
@@ -136,8 +136,8 @@
 
 def front_kernel(*refs):
     ins, refs = refs[:13], refs[13:]
-    first, one_up, one_down, two_up, two_down, opposite, chosen = refs[:7]
-    refs = refs[7:]
+    first, keep_three, send_four, chosen = refs[:4]
+    refs = refs[4:]
     bufs, (count, table_sem, small_sem, new_sem, kv_sem, weight_sem) = refs[:13], refs[13:]
     pairing, lengths, table, new_lengths, query, own, new_query, new_own, resid, new_resid, weight, new_buf, kv_buf = bufs
     new_cache, cache = ins[11], ins[12]
@@ -179,20 +179,15 @@
     attended = jnp.concatenate([rows, new_rows], axis=0)
     weight_copy.wait()
 
-    def block_of(shift):
-        return pl.ds(pl.multiple_of((z + shift + NZ) % NZ * width, 128), width)
-
-    def part(shift):
-        return jnp.dot(attended, weight[:, block_of(shift)], preferred_element_type=jnp.float32)
-
-    two_up[: 2 * REQ] = part(2).astype(jnp.bfloat16)
-    two_up[2 * REQ :] = part(3).astype(jnp.bfloat16)
-    two_down[: 2 * REQ] = part(-2).astype(jnp.bfloat16)
-    two_down[2 * REQ :] = part(-3).astype(jnp.bfloat16)
-    opposite[...] = part(4).astype(jnp.bfloat16)
-    one_up[...] = part(1)
-    one_down[...] = part(-1)
-    columns = block_of(0)
+    def part(flip):
+        columns = pl.ds(pl.multiple_of((z ^ flip) * width, 128), width)
+        return jnp.dot(attended, weight[:, columns], preferred_element_type=jnp.float32)
+
+    for n, flip in enumerate((1, 3, 5, 7)):
+        send_four[2 * REQ * n : 2 * REQ * (n + 1)] = part(flip).astype(jnp.bfloat16)
+    for n, flip in enumerate((2, 4, 6)):
+        keep_three[2 * REQ * n : 2 * REQ * (n + 1)] = part(flip)
+    columns = pl.ds(pl.multiple_of(z * width, 128), width)
     block = jnp.concatenate([resid[:, columns], new_resid[:, columns]], axis=0)
     first[...] = part(0) + jnp.where(x_lo == 0, block.astype(jnp.float32), 0.0)
 
@@ -217,12 +212,14 @@
     vmem = pl.BlockSpec(memory_space=VMEM)
     return pl.pallas_call(
         front_kernel,
-        out_shape=[jax.ShapeDtypeStruct((2 * REQ, width), jnp.float32)] * 3
-        + [jax.ShapeDtypeStruct((4 * REQ, width), jnp.bfloat16)] * 2
-        + [jax.ShapeDtypeStruct((2 * REQ, width), jnp.bfloat16)]
-        + [jax.ShapeDtypeStruct((2 * REQ, REQ), jnp.bfloat16)],
+        out_shape=[
+            jax.ShapeDtypeStruct((2 * REQ, width), jnp.float32),
+            jax.ShapeDtypeStruct((6 * REQ, width), jnp.float32),
+            jax.ShapeDtypeStruct((8 * REQ, width), jnp.bfloat16),
+            jax.ShapeDtypeStruct((2 * REQ, REQ), jnp.bfloat16),
+        ],
         in_specs=[any_space] * 13,
-        out_specs=[vmem] * 7,
+        out_specs=[vmem] * 4,
         scratch_shapes=[SMEM(array.shape, array.dtype) for array in args[:4]]
         + [VMEM(array.shape, array.dtype) for array in args[4:12]]
         + [
@@ -258,7 +255,7 @@
 def finish_kernel(gain, *refs):
     *blocks, hidden, normed = refs
     z, me = lax.axis_index("tp") // 2, group_index()
-    rows, width = blocks[0].shape
+    rows, width = hidden.shape[0], blocks[0].shape[1]
     slots = rows - REQ
     slot = lax.broadcasted_iota(jnp.int32, (slots, slots), 0)
     column = lax.broadcasted_iota(jnp.int32, (slots, slots), 1)
@@ -266,9 +263,9 @@
     at = (offset & 1) * 16 + ((offset >> 1) & 3) * 4 + (offset >> 3) * 2 + (slot & 1)
     order = jnp.where(column == at, 1.0, 0.0).astype(jnp.bfloat16)
     square = jnp.zeros((rows, 1), jnp.float32)
-    places = [(0, 0, 0), (1, 0, -1), (2, 0, 1), (3, 0, 4), (4, 0, -2), (4, 1, -3), (5, 0, 2), (5, 1, 3)]
+    places = [(0, 0, 0), (0, 1, 2), (0, 2, 6), (0, 3, 4), (1, 0, 1), (1, 1, 3), (1, 2, 7), (1, 3, 5)]
     for n, part, shift in places:
-        columns = pl.ds(pl.multiple_of((z + shift + NZ) % NZ * width, 128), width)
+        columns = pl.ds(pl.multiple_of((z ^ shift) * width, 128), width)
         block = blocks[n][rows * part : rows * (part + 1)]
         placed = jnp.dot(order, block[REQ:], preferred_element_type=jnp.float32)
         wide = jnp.concatenate([block[:REQ].astype(jnp.float32), placed], axis=0)
@@ -284,20 +281,20 @@
 
 
 def place_kernel(start, part, *refs):
-    whole, buf, in_sem, out_sem = refs[-4:]
+    whole, sem = refs[-2:]
     size = part.shape[0] // 4
-    for n in range(4):
-        rows = pl.ds(n * size, size)
-        pltpu.make_async_copy(part.at[rows], buf.at[rows], in_sem.at[n]).start()
-    for n in range(4):
-        rows = pl.ds(n * size, size)
-        pltpu.make_async_copy(part.at[rows], buf.at[rows], in_sem.at[n]).wait()
-        target = whole.at[rows, pl.ds(start, part.shape[1])]
-        pltpu.make_async_copy(buf.at[rows], target, out_sem.at[n]).start()
-    for n in range(4):
-        rows = pl.ds(n * size, size)
-        target = whole.at[rows, pl.ds(start, part.shape[1])]
-        pltpu.make_async_copy(buf.at[rows], target, out_sem.at[n]).wait()
+    copies = [
+        pltpu.make_async_copy(
+            part.at[pl.ds(n * size, size)],
+            whole.at[pl.ds(n * size, size), pl.ds(start, part.shape[1])],
+            sem.at[n],
+        )
+        for n in range(4)
+    ]
+    for copy in copies:
+        copy.start()
+    for copy in copies:
+        copy.wait()
 
 
 def place(part, start, whole):
@@ -307,11 +304,9 @@
     return pl.pallas_call(
         functools.partial(place_kernel, start),
         out_shape=jax.ShapeDtypeStruct(shape, part.dtype),
-        in_specs=[any_space] * len(given),
+        in_specs=[pl.BlockSpec(memory_space=VMEM)] + [any_space] * (len(given) - 1),
         out_specs=any_space,
         scratch_shapes=[
-            VMEM(part.shape, part.dtype),
-            pltpu.SemaphoreType.DMA((4,)),
             pltpu.SemaphoreType.DMA((4,)),
         ],
         compiler_params=pltpu.CompilerParams(vmem_limit_bytes=SMALL_LIMIT),
@@ -347,9 +342,6 @@
     def over_tp(array, flip):
         return lax.ppermute(array, "tp", [(t, t ^ flip) for t in range(ranks)])
 
-    def round_z(array, shift):
-        return lax.ppermute(array, "tp", [(t, (t + 2 * shift) % ranks) for t in range(ranks)])
-
     def over_groups(array, flip):
         return lax.ppermute(array, both, [(s, s ^ flip) for s in range(groups)])
 
@@ -361,7 +353,7 @@
     early = deliver(pack(*prompt, 0, CUT))
     late = pack(*prompt, CUT, prompts.shape[1] - CUT)
 
-    first, one_up, one_down, two_up, two_down, opposite, chosen = front(
+    first, keep_three, send_four, chosen = front(
         pair,
         lengths[0, 0],
         table[0, 0],
@@ -376,15 +368,14 @@
         prompts,
         cache[0, 0, :, :, 0],
     )
-    from_below, from_above = round_z(two_up, 2), round_z(two_down, -2)
-    opposite = round_z(opposite, 4)
-    gain = norm_gain.reshape(1, -1)
-    from_below, from_above, opposite, gain, late = lax.optimization_barrier(
-        (from_below, from_above, opposite, gain, late)
-    )
-    one_up = (one_up + from_below[2 * REQ :].astype(jnp.float32)).astype(jnp.bfloat16)
-    one_down = (one_down + from_above[2 * REQ :].astype(jnp.float32)).astype(jnp.bfloat16)
-    parts = [from_below, from_above, opposite, round_z(one_up, 1), round_z(one_down, -1)]
+    four, gain, late = lax.optimization_barrier(
+        (over_tp(send_four, 2), norm_gain.reshape(1, -1), late)
+    )
+    parts = [four]
+    for n, flip in enumerate((2, 4, 6)):
+        summed = keep_three[2 * REQ * n : 2 * REQ * (n + 1)]
+        summed = summed + four[2 * REQ * (n + 1) : 2 * REQ * (n + 2)].astype(jnp.float32)
+        parts.append(over_tp(summed.astype(jnp.bfloat16), 2 * flip))
     width = first.shape[1]
     near, far = pl.pallas_call(
         spread_kernel,
@@ -416,12 +407,10 @@
     block = jnp.concatenate([near[:REQ], kept, over_groups(given, 1)], axis=0)
 
     slot_cache = place(early, 0, (2 * REQ,) + prompts.shape[1:])
-    below, above, opposite, slot_cache = lax.optimization_barrier(
-        (round_z(block, 1), round_z(block, -1), round_z(block, 4), slot_cache)
-    )
-    two_below = round_z(jnp.concatenate([block, below], axis=0), 2)
-    two_above = round_z(jnp.concatenate([block, above], axis=0), -2)
-    blocks = [block, below, above, opposite, two_below, two_above]
+    flips = [over_tp(block, 2 * k) for k in (2, 6, 4)]
+    *flips, slot_cache = lax.optimization_barrier((*flips, slot_cache))
+    four = jnp.concatenate([block, *flips], axis=0)
+    blocks = [four, over_tp(four, 2)]
     hidden, normed = pl.pallas_call(
         finish_kernel,
         out_shape=[jax.ShapeDtypeStruct((block.shape[0], width * NZ), jnp.bfloat16)] * 2,

time: 89.5 us -> 87.7 us (0.980)
  starting transfers between devices: 49.6 us -> 43.8 us
  waiting for transfers between devices: 21.2 us -> 25.9 us
    ppermute x10 -> x0, starting transfers between devices: 23.6 us -> none  [round_z(): lax.ppermute(array, 'tp', [(t, (t + 2 * shift) % ranks) for t in range(ra...]
    ppermute x1 -> x9, starting transfers between devices: 0.28 us -> 18.6 us  [over_tp(): return lax.ppermute(array, 'tp', [(t, t ^ flip) for t in range(ranks)])]
    ppermute x1 -> x9, waiting for transfers between devices: 0.01 us -> 15.6 us  [over_tp(): return lax.ppermute(array, 'tp', [(t, t ^ flip) for t in range(ranks)])]
    ppermute x10 -> x0, waiting for transfers between devices: 10.9 us -> none  [round_z(): lax.ppermute(array, 'tp', [(t, (t + 2 * shift) % ranks) for t in range(ra...]
    ppermute x1, waiting for transfers between devices: 1.71 us -> 2.69 us  [body(): far_there = lax.ppermute(far, ('pool', 'tp'), across)]
  transfers between devices with their start and end apart: 19 -> 17, of which waited for: 11 -> 11; matrix products, arithmetic and copies ran while one was open for 0% -> 0% of each run, Pallas kernels for 13% -> 14%
where the time goes in v5:
time: 87.7 us; the launch traced here: 87.4 us
  starting transfers between devices  43.8 us (50%)
  waiting for transfers between devices  25.9 us (30%)
  Pallas kernels  16.3 us (19%)
  between operations  0.99 us (1%)
    ppermute x9, starting transfers between devices, over_tp(): return lax.ppermute(array, 'tp', [(t, t ^ flip) for t in range(ranks)])  18.6 us
    all_to_all x2, starting transfers between devices, deliver(): lax.all_to_all(blocks, both, split_axis=0, concat_axis=0, tiled=True)  17.1 us
    ppermute x9, waiting for transfers between devices, over_tp(): return lax.ppermute(array, 'tp', [(t, t ^ flip) for t in range(ranks)])  15.6 us
    ppermute x5, starting transfers between devices, over_groups(): return lax.ppermute(array, both, [(s, s ^ flip) for s in range(groups)])  5.61 us
    pallas_call x2, Pallas kernels, pack(): pl.pallas_call(functools.partial(pack_kernel, start), out_shape=jax.Shape...  5.51 us
    pallas_call x1, Pallas kernels, front(): pl.pallas_call(front_kernel, out_shape=[jax.ShapeDtypeStruct((2 * REQ, wi...  5.11 us
    ppermute x5, waiting for transfers between devices, over_groups(): return lax.ppermute(array, both, [(s, s ^ flip) for s in range(groups)])  5 us
    pallas_call x2, Pallas kernels, place(): pl.pallas_call(functools.partial(place_kernel, start), out_shape=jax.Shap...  4.35 us
  transfers between devices with their start and end apart: 17, of which 11 were waited for; matrix products, arithmetic and copies ran while one was open for 0% of the time, Pallas kernels for 14%

profile of v5, /device:TPU:1, one launch (start us, length us, event | category | flops | bytes accessed | tf_op | source)
XLA Modules:
  0.0 87.4 jit_solution(7118148222302236425)
XLA Ops:
  0.6 2.9 %pack.3 = bf16[32,144,256]{2,1,0:T(8,128)(2,1)} custom-call(s32[16]{0:T(128)} %bitcast.38, s32[16]{0:T(128)} %bitcast.41, bf16[16,256]{1,0:T(8,128)(2,1)} %bitcast.32, bf16[16,256,256]{2,1,0:T(8,128)(2,1)} %bitcast.46), custom_call_target="tpu_custom_call" | custom-call | bytes 3600000 | tf_op jit(solution)/shard_map/pack/pallas_call | solution.py:115
  3.5 0.0 copy-start
  3.5 0.0 copy-start.1
  3.5 0.0 copy-start.2
  3.6 0.0 copy-start.3
  3.6 0.0 copy-start.4
  3.6 0.0 copy-start.5
  3.6 0.0 copy-start.6
  3.6 0.0 copy-start.7
  3.6 0.0 copy-start.8
  3.6 0.0 copy-start.9
  3.6 8.6 %all-to-all-start.1 = ((bf16[16,2,144,256]{3,2,1,0:T(8,128)(2,1)}), bf16[16,2,144,256]{3,2,1,0:T(8,128)(2,1)}, u32[]{:S(2)}, u32[]{:S(2)}) async-start(bf16[16,2,144,256]{3,2,1,0:T(8,128)(2,1)} %bitcast.50), calls=%async_computation.1 | async-start | bytes 4718592 | tf_op jit(solution)/shard_map/all_to_all | solution.py:350
  12.2 0.0 copy-done
  12.2 0.0 copy-done.1
  12.2 0.0 copy-done.2
  12.2 0.0 copy-done.3
  12.3 0.0 copy-done.4
  12.3 0.0 copy-done.5
  12.3 0.0 copy-done.6
  12.3 0.0 copy-done.7
  12.3 0.0 copy-done.8
  12.3 0.0 copy-done.9
  12.3 5.1 %front.1 = (f32[32,640]{1,0:T(8,128)S(1)}, f32[96,640]{1,0:T(8,128)S(1)}, bf16[128,640]{1,0:T(8,128)(2,1)S(1)}, bf16[32,16]{1,0:T(8,128)(2,1)S(1)}) custom-call(s32[16]{0:T(128)S(1)} %bitcast.40, s32[16]{0:T(128)S(1)} %bitcast.44, s32[64]{0:T(128)S(1)} %bitcast.45, s32[16]{0:T(128)S(1)} %bitcast.43, bf16[16,256]{1,0:T(8,128)(2,1)S(1)} %bitcast.35, ...), custom_call_target="tpu_custom_call" | custom-call | flops 400000000 | bytes 9500000 | tf_op jit(solution)/shard_map/front/pallas_call | solution.py:213
  17.4 0.0 copy-start.10
  17.4 1.7 %collective-permute-start = (bf16[128,640]{1,0:T(8,128)(2,1)S(1)}, bf16[128,640]{1,0:T(8,128)(2,1)S(1)}, u32[]{:S(2)}, u32[]{:S(2)}) collective-permute-start(bf16[128,640]{1,0:T(8,128)(2,1)S(1)} %get-tuple-element.25), channel_id=1, source_target_pairs={{0,2},{1,3},{2,0},{3,1},{4,6},{5,7},{6,4},{7,5},{8,10},{9,11},{10,... | collective-permute-start | bytes 491528 | tf_op jit(solution)/shard_map/ppermute | solution.py:343
  19.2 2.6 %pack.2 = bf16[32,112,256]{2,1,0:T(8,128)(2,1)} custom-call(s32[16]{0:T(128)} %bitcast.39, s32[16]{0:T(128)} %bitcast.42, bf16[16,256]{1,0:T(8,128)(2,1)} %bitcast.33, bf16[16,256,256]{2,1,0:T(8,128)(2,1)} %bitcast.48), custom_call_target="tpu_custom_call" | custom-call | bytes 2800000 | tf_op jit(solution)/shard_map/pack/pallas_call | solution.py:115
  21.8 0.0 copy-done.10
  21.8 1.8 %collective-permute-done.refs_0_ = bf16[128,640]{1,0:T(8,128)(2,1)S(1)} collective-permute-done((bf16[128,640]{1,0:T(8,128)(2,1)S(1)}, bf16[128,640]{1,0:T(8,128)(2,1)S(1)}, u32[]{:S(2)}, u32[]{:S(2)}) %collective-permute-start) | collective-permute-done | bytes 163872 | tf_op jit(solution)/shard_map/ppermute | solution.py:343
  23.7 5.7 %collective-permute-start.3 = (bf16[32,640]{1,0:T(8,128)(2,1)S(1)}, bf16[32,640]{1,0:T(8,128)(2,1)S(1)}, u32[]{:S(2)}, u32[]{:S(2)}) collective-permute-start(bf16[32,640]{1,0:T(8,128)(2,1)S(1)} %get-tuple-element.50), channel_id=1, source_target_pairs={{0,12},{1,13},{2,14},{3,15},{4,8},{5,9},{6,10},{7,11},{8,4},{9,5},... | collective-permute-start | bytes 122888 | tf_op jit(solution)/shard_map/ppermute | solution.py:343
  29.4 1.0 %collective-permute-start.2 = (bf16[32,640]{1,0:T(8,128)(2,1)S(1)}, bf16[32,640]{1,0:T(8,128)(2,1)S(1)}, u32[]{:S(2)}, u32[]{:S(2)}) collective-permute-start(bf16[32,640]{1,0:T(8,128)(2,1)S(1)} %get-tuple-element.51), channel_id=1, source_target_pairs={{0,8},{1,9},{2,10},{3,11},{4,12},{5,13},{6,14},{7,15},{8,0},{9,1},... | collective-permute-start | bytes 122888 | tf_op jit(solution)/shard_map/ppermute | solution.py:343
  30.4 1.2 %collective-permute-start.1 = (bf16[32,640]{1,0:T(8,128)(2,1)S(1)}, bf16[32,640]{1,0:T(8,128)(2,1)S(1)}, u32[]{:S(2)}, u32[]{:S(2)}) collective-permute-start(bf16[32,640]{1,0:T(8,128)(2,1)S(1)} %get-tuple-element.52), channel_id=1, source_target_pairs={{0,4},{1,5},{2,6},{3,7},{4,0},{5,1},{6,2},{7,3},{8,12},{9,13},{10,... | collective-permute-start | bytes 122888 | tf_op jit(solution)/shard_map/ppermute | solution.py:343
  31.6 0.0 collective-permute-done.3.refs_3_
  31.6 4.9 %collective-permute-done.2.refs_2_ = bf16[32,640]{1,0:T(8,128)(2,1)S(1)} collective-permute-done((bf16[32,640]{1,0:T(8,128)(2,1)S(1)}, bf16[32,640]{1,0:T(8,128)(2,1)S(1)}, u32[]{:S(2)}, u32[]{:S(2)}) %collective-permute-start.2) | collective-permute-done | bytes 40992 | tf_op jit(solution)/shard_map/ppermute | solution.py:343
  36.5 0.0 collective-permute-done.1.refs_1_
  36.5 0.1 spread.1
  36.7 2.5 %collective-permute-start.6 = (bf16[16,640]{1,0:T(8,128)(2,1)S(1)}, bf16[16,640]{1,0:T(8,128)(2,1)S(1)}, u32[]{:S(2)}, u32[]{:S(2)}) collective-permute-start(bf16[16,640]{1,0:T(8,128)(2,1)S(1)} %get-tuple-element.32), channel_id=1, source_target_pairs={{0,129},{1,128},{2,131},{3,130},{4,133},{5,132},{6,135},{7,134},{8... | collective-permute-start | bytes 61448 | tf_op jit(solution)/shard_map/ppermute | solution.py:394
  39.2 0.4 collective-permute-start.5
  39.6 0.5 collective-permute-start.4
  40.0 2.7 %collective-permute-done.6 = bf16[16,640]{1,0:T(8,128)(2,1)S(1)} collective-permute-done((bf16[16,640]{1,0:T(8,128)(2,1)S(1)}, bf16[16,640]{1,0:T(8,128)(2,1)S(1)}, u32[]{:S(2)}, u32[]{:S(2)}) %collective-permute-start.6) | collective-permute-done | bytes 20512 | tf_op jit(solution)/shard_map/ppermute | solution.py:394
  42.7 1.0 %collective-permute-done.5 = bf16[16,640]{1,0:T(8,128)(2,1)S(1)} collective-permute-done((bf16[16,640]{1,0:T(8,128)(2,1)S(1)}, bf16[16,640]{1,0:T(8,128)(2,1)S(1)}, u32[]{:S(2)}, u32[]{:S(2)}) %collective-permute-start.5) | collective-permute-done | bytes 20512 | tf_op jit(solution)/shard_map/ppermute | solution.py:346
  43.7 0.0 collective-permute-done.4
  43.8 2.3 %collective-permute-start.7 = (bf16[8,640]{1,0:T(8,128)(2,1)S(1)}, bf16[8,640]{1,0:T(8,128)(2,1)S(1)}, u32[]{:S(2)}, u32[]{:S(2)}) collective-permute-start(bf16[8,640]{1,0:T(8,128)(2,1)S(1)} %pad_maximum_fusion.2), channel_id=1, source_target_pairs={{0,32},{16,48},{32,0},{48,16},{64,96},{80,112},{96,64},{112,80},{1... | collective-permute-start | bytes 30728 | tf_op jit(solution)/shard_map/ppermute | solution.py:346
  46.2 1.8 %collective-permute-start.8 = (bf16[8,640]{1,0:T(8,128)(2,1)S(1)}, bf16[8,640]{1,0:T(8,128)(2,1)S(1)}, u32[]{:S(2)}, u32[]{:S(2)}) collective-permute-start(bf16[8,640]{1,0:T(8,128)(2,1)S(1)} %pad_maximum_fusion.3), channel_id=1, source_target_pairs={{0,64},{16,80},{32,96},{48,112},{64,0},{80,16},{96,32},{112,48},{1... | collective-permute-start | bytes 30728 | tf_op jit(solution)/shard_map/ppermute | solution.py:346
  48.0 0.8 collective-permute-start.9
  48.8 0.0 collective-permute-done.7
  48.8 1.5 %collective-permute-done.8 = bf16[8,640]{1,0:T(8,128)(2,1)S(1)} collective-permute-done((bf16[8,640]{1,0:T(8,128)(2,1)S(1)}, bf16[8,640]{1,0:T(8,128)(2,1)S(1)}, u32[]{:S(2)}, u32[]{:S(2)}) %collective-permute-start.8) | collective-permute-done | bytes 10272 | tf_op jit(solution)/shard_map/ppermute | solution.py:346
  50.3 1.5 %collective-permute-done.9 = bf16[8,640]{1,0:T(8,128)(2,1)S(1)} collective-permute-done((bf16[8,640]{1,0:T(8,128)(2,1)S(1)}, bf16[8,640]{1,0:T(8,128)(2,1)S(1)}, u32[]{:S(2)}, u32[]{:S(2)}) %collective-permute-start.9) | collective-permute-done | bytes 10272 | tf_op jit(solution)/shard_map/ppermute | solution.py:346
  51.8 0.0 all-to-all-done.1
  51.8 8.5 %all-to-all-start = ((bf16[16,2,112,256]{3,2,1,0:T(8,128)(2,1)}), bf16[16,2,112,256]{3,2,1,0:T(8,128)(2,1)S(1)}, u32[]{:S(2)}, u32[]{:S(2)}) async-start(bf16[16,2,112,256]{3,2,1,0:T(8,128)(2,1)} %bitcast.51), calls=%async_computation | async-start | bytes 3670016 | tf_op jit(solution)/shard_map/all_to_all | solution.py:350
  60.6 0.3 collective-permute-start.10
  60.9 1.0 %collective-permute-done.10 = bf16[16,640]{1,0:T(8,128)(2,1)S(1)} collective-permute-done((bf16[16,640]{1,0:T(8,128)(2,1)S(1)}, bf16[16,640]{1,0:T(8,128)(2,1)S(1)}, u32[]{:S(2)}, u32[]{:S(2)}) %collective-permute-start.10) | collective-permute-done | bytes 20512 | tf_op jit(solution)/shard_map/ppermute | solution.py:346
  61.9 6.4 %collective-permute-start.13 = (bf16[48,640]{1,0:T(8,128)(2,1)S(1)}, bf16[48,640]{1,0:T(8,128)(2,1)S(1)}, u32[]{:S(2)}, u32[]{:S(2)}) collective-permute-start(bf16[48,640]{1,0:T(8,128)(2,1)S(1)} %pad_maximum_fusion), channel_id=1, source_target_pairs={{0,8},{1,9},{2,10},{3,11},{4,12},{5,13},{6,14},{7,15},{8,0},{9,1},... | collective-permute-start | bytes 184328 | tf_op jit(solution)/shard_map/ppermute | solution.py:343
  68.3 0.0 collective-permute-start.12
  68.3 1.2 %collective-permute-start.11 = (bf16[48,640]{1,0:T(8,128)(2,1)S(1)}, bf16[48,640]{1,0:T(8,128)(2,1)S(1)}, u32[]{:S(2)}, u32[]{:S(2)}) collective-permute-start(bf16[48,640]{1,0:T(8,128)(2,1)S(1)} %pad_maximum_fusion), channel_id=1, source_target_pairs={{0,4},{1,5},{2,6},{3,7},{4,0},{5,1},{6,2},{7,3},{8,12},{9,13},{10,... | collective-permute-start | bytes 184328 | tf_op jit(solution)/shard_map/ppermute | solution.py:343
  69.5 3.1 %place.2.refs_0_ = bf16[32,256,256]{2,1,0:T(8,128)(2,1)} custom-call(bf16[32,144,256]{2,1,0:T(8,128)(2,1)} %bitcast.15.part), custom_call_target="tpu_custom_call" | custom-call | bytes 4718592 | tf_op jit(solution)/shard_map/place/pallas_call | solution.py:304
  72.6 0.0 collective-permute-done.13
  72.6 1.2 %collective-permute-done.12 = bf16[48,640]{1,0:T(8,128)(2,1)S(1)} collective-permute-done((bf16[48,640]{1,0:T(8,128)(2,1)S(1)}, bf16[48,640]{1,0:T(8,128)(2,1)S(1)}, u32[]{:S(2)}, u32[]{:S(2)}) %collective-permute-start.12) | collective-permute-done | bytes 61472 | tf_op jit(solution)/shard_map/ppermute | solution.py:343
  73.8 1.4 %collective-permute-done.11 = bf16[48,640]{1,0:T(8,128)(2,1)S(1)} collective-permute-done((bf16[48,640]{1,0:T(8,128)(2,1)S(1)}, bf16[48,640]{1,0:T(8,128)(2,1)S(1)}, u32[]{:S(2)}, u32[]{:S(2)}) %collective-permute-start.11) | collective-permute-done | bytes 61472 | tf_op jit(solution)/shard_map/ppermute | solution.py:343
  75.3 0.9 collective-permute-start.14
  76.1 6.3 %collective-permute-done.14.refs_1_ = bf16[192,640]{1,0:T(8,128)(2,1)S(1)} collective-permute-done((bf16[192,640]{1,0:T(8,128)(2,1)S(1)}, bf16[192,640]{1,0:T(8,128)(2,1)S(1)}, u32[]{:S(2)}, u32[]{:S(2)}) %collective-permute-start.14) | collective-permute-done | bytes 245792 | tf_op jit(solution)/shard_map/ppermute | solution.py:343
  82.4 1.2 %finish.1 = (bf16[48,5120]{1,0:T(8,128)(2,1)}, bf16[48,5120]{1,0:T(8,128)(2,1)}) custom-call(bf16[1,5120]{1,0:T(2,128)(2,1)S(1)} %reshape.30.gain, bf16[192,640]{1,0:T(8,128)(2,1)S(1)} %constant_dynamic-update-slice_fusion.4.refs_0_, bf16[192,640]{1,0:T(8,128)(2,1)S(1)} %collective-permute-done.14.refs_1_), custom_call_target="tpu_custom_call" | custom-call | bytes 4000000 | tf_op jit(solution)/shard_map/finish/pallas_call | solution.py:414
  83.6 2.5 %all-to-all-done = bf16[16,2,112,256]{3,2,1,0:T(8,128)(2,1)S(1)} async-done(((bf16[16,2,112,256]{3,2,1,0:T(8,128)(2,1)}), bf16[16,2,112,256]{3,2,1,0:T(8,128)(2,1)S(1)}, u32[]{:S(2)}, u32[]{:S(2)}) %all-to-all-start) | async-done | bytes 1835040 | tf_op jit(solution)/shard_map/all_to_all | solution.py:350
  86.1 1.3 %place.3 = bf16[32,256,256]{2,1,0:T(8,128)(2,1)} custom-call(bf16[32,112,256]{2,1,0:T(8,128)(2,1)S(1)} %bitcast.29, bf16[32,256,256]{2,1,0:T(8,128)(2,1)} %place.2.refs_0_), custom_call_target="tpu_custom_call", output_to_operand_aliasing={{}: (1, {})} | custom-call | bytes 3670016 | tf_op jit(solution)/shard_map/place/pallas_call | solution.py:304
  (28 shorter events, 0.4 us)
Async XLA Ops:
  3.5 8.7 %copy-start = (bf16[1,1,16,5120]{3,2,1,0:T(8,128)(2,1)S(1)}, bf16[1,1,16,5120]{3,2,1,0:T(8,128)(2,1)}, u32[]{:S(2)}) copy-start(bf16[1,1,16,5120]{3,2,1,0:T(8,128)(2,1)} %param.19) | copy-start | bytes 491524
  3.5 8.7 %copy-start.1 = (bf16[1,1,16,5120]{3,2,1,0:T(8,128)(2,1)S(1)}, bf16[1,1,16,5120]{3,2,1,0:T(8,128)(2,1)}, u32[]{:S(2)}) copy-start(bf16[1,1,16,5120]{3,2,1,0:T(8,128)(2,1)} %param.24) | copy-start | bytes 491524
  3.5 8.7 %copy-start.2 = (bf16[1,1,16,1,256]{4,2,3,1,0:T(8,128)(2,1)S(1)}, bf16[1,1,16,1,256]{4,2,3,1,0:T(8,128)(2,1)}, u32[]{:S(2)}) copy-start(bf16[1,1,16,1,256]{4,2,3,1,0:T(8,128)(2,1)} %param.23) | copy-start | bytes 24580
  3.6 8.7 %copy-start.3 = (bf16[1,1,16,256]{3,2,1,0:T(8,128)(2,1)S(1)}, bf16[1,1,16,256]{3,2,1,0:T(8,128)(2,1)}, u32[]{:S(2)}) copy-start(bf16[1,1,16,256]{3,2,1,0:T(8,128)(2,1)} %param.17) | copy-start | bytes 24580
  3.6 8.7 %copy-start.4 = (bf16[1,1,16,1,256]{4,2,3,1,0:T(8,128)(2,1)S(1)}, bf16[1,1,16,1,256]{4,2,3,1,0:T(8,128)(2,1)}, u32[]{:S(2)}) copy-start(bf16[1,1,16,1,256]{4,2,3,1,0:T(8,128)(2,1)} %param.18) | copy-start | bytes 24580
  3.6 8.7 %copy-start.5 = (bf16[1,1,16,256]{3,2,1,0:T(8,128)(2,1)S(1)}, bf16[1,1,16,256]{3,2,1,0:T(8,128)(2,1)}, u32[]{:S(2)}) copy-start(bf16[1,1,16,256]{3,2,1,0:T(8,128)(2,1)} %param.22) | copy-start | bytes 24580
  3.6 8.7 %copy-start.6 = (s32[1,1,16,1]{2,3,1,0:T(1,128)S(1)}, s32[1,1,16,1]{2,3,1,0:T(1,128)}, u32[]{:S(2)}) copy-start(s32[1,1,16,1]{2,3,1,0:T(1,128)} %param.25) | copy-start | bytes 196
  3.6 8.7 %copy-start.7 = (s32[1,1,16]{2,1,0:T(1,128)S(1)}, s32[1,1,16]{2,1,0:T(1,128)}, u32[]{:S(2)}) copy-start(s32[1,1,16]{2,1,0:T(1,128)} %param.21) | copy-start | bytes 196
  3.6 8.7 %copy-start.8 = (s32[1,1,16]{2,1,0:T(1,128)S(1)}, s32[1,1,16]{2,1,0:T(1,128)}, u32[]{:S(2)}) copy-start(s32[1,1,16]{2,1,0:T(1,128)} %param.16) | copy-start | bytes 196
  3.6 8.7 %copy-start.9 = (s32[1,1,64]{2,1,0:T(1,128)S(1)}, s32[1,1,64]{2,1,0:T(1,128)}, u32[]{:S(2)}) copy-start(s32[1,1,64]{2,1,0:T(1,128)} %param.15) | copy-start | bytes 772
  3.6 48.2 %all-to-all-start.1 = ((bf16[16,2,144,256]{3,2,1,0:T(8,128)(2,1)}), bf16[16,2,144,256]{3,2,1,0:T(8,128)(2,1)}, u32[]{:S(2)}, u32[]{:S(2)}) async-start(bf16[16,2,144,256]{3,2,1,0:T(8,128)(2,1)} %bitcast.50), calls=%async_computation.1 | async-start | bytes 4718592 | tf_op jit(solution)/shard_map/all_to_all | solution.py:350
  17.4 4.4 %copy-start.10 = (bf16[5120]{0:T(1024)(128)(2,1)S(1)}, bf16[5120]{0:T(1024)(128)(2,1)}, u32[]{:S(2)}) copy-start(bf16[5120]{0:T(1024)(128)(2,1)} %param.27) | copy-start | bytes 30724
  17.4 6.2 %collective-permute-start = (bf16[128,640]{1,0:T(8,128)(2,1)S(1)}, bf16[128,640]{1,0:T(8,128)(2,1)S(1)}, u32[]{:S(2)}, u32[]{:S(2)}) collective-permute-start(bf16[128,640]{1,0:T(8,128)(2,1)S(1)} %get-tuple-element.25), channel_id=1, source_target_pairs={{0,2},{1,3},{2,0},{3,1},{4,6},{5,7},{6,4},{7,5},{8,10},{9,11},{10,... | collective-permute-start | bytes 491528 | tf_op jit(solution)/shard_map/ppermute | solution.py:343
  23.7 7.9 %collective-permute-start.3 = (bf16[32,640]{1,0:T(8,128)(2,1)S(1)}, bf16[32,640]{1,0:T(8,128)(2,1)S(1)}, u32[]{:S(2)}, u32[]{:S(2)}) collective-permute-start(bf16[32,640]{1,0:T(8,128)(2,1)S(1)} %get-tuple-element.50), channel_id=1, source_target_pairs={{0,12},{1,13},{2,14},{3,15},{4,8},{5,9},{6,10},{7,11},{8,4},{9,5},... | collective-permute-start | bytes 122888 | tf_op jit(solution)/shard_map/ppermute | solution.py:343
  29.4 7.1 %collective-permute-start.2 = (bf16[32,640]{1,0:T(8,128)(2,1)S(1)}, bf16[32,640]{1,0:T(8,128)(2,1)S(1)}, u32[]{:S(2)}, u32[]{:S(2)}) collective-permute-start(bf16[32,640]{1,0:T(8,128)(2,1)S(1)} %get-tuple-element.51), channel_id=1, source_target_pairs={{0,8},{1,9},{2,10},{3,11},{4,12},{5,13},{6,14},{7,15},{8,0},{9,1},... | collective-permute-start | bytes 122888 | tf_op jit(solution)/shard_map/ppermute | solution.py:343
  30.4 6.1 %collective-permute-start.1 = (bf16[32,640]{1,0:T(8,128)(2,1)S(1)}, bf16[32,640]{1,0:T(8,128)(2,1)S(1)}, u32[]{:S(2)}, u32[]{:S(2)}) collective-permute-start(bf16[32,640]{1,0:T(8,128)(2,1)S(1)} %get-tuple-element.52), channel_id=1, source_target_pairs={{0,4},{1,5},{2,6},{3,7},{4,0},{5,1},{6,2},{7,3},{8,12},{9,13},{10,... | collective-permute-start | bytes 122888 | tf_op jit(solution)/shard_map/ppermute | solution.py:343
  36.7 6.0 %collective-permute-start.6 = (bf16[16,640]{1,0:T(8,128)(2,1)S(1)}, bf16[16,640]{1,0:T(8,128)(2,1)S(1)}, u32[]{:S(2)}, u32[]{:S(2)}) collective-permute-start(bf16[16,640]{1,0:T(8,128)(2,1)S(1)} %get-tuple-element.32), channel_id=1, source_target_pairs={{0,129},{1,128},{2,131},{3,130},{4,133},{5,132},{6,135},{7,134},{8... | collective-permute-start | bytes 61448 | tf_op jit(solution)/shard_map/ppermute | solution.py:394
  39.2 4.5 %collective-permute-start.5 = (bf16[16,640]{1,0:T(8,128)(2,1)S(1)}, bf16[16,640]{1,0:T(8,128)(2,1)S(1)}, u32[]{:S(2)}, u32[]{:S(2)}) collective-permute-start(bf16[16,640]{1,0:T(8,128)(2,1)S(1)} %get-tuple-element.32), channel_id=1, source_target_pairs={{0,128},{16,144},{32,160},{48,176},{64,192},{80,208},{96,224},{112... | collective-permute-start | bytes 61448 | tf_op jit(solution)/shard_map/ppermute | solution.py:346
  39.6 4.2 %collective-permute-start.4 = (bf16[32,640]{1,0:T(8,128)(2,1)S(1)}, bf16[32,640]{1,0:T(8,128)(2,1)S(1)}, u32[]{:S(2)}, u32[]{:S(2)}) collective-permute-start(bf16[32,640]{1,0:T(8,128)(2,1)S(1)} %get-tuple-element.31), channel_id=1, source_target_pairs={{0,1},{1,0},{2,3},{3,2},{4,5},{5,4},{6,7},{7,6},{8,9},{9,8},{10,11... | collective-permute-start | bytes 122888 | tf_op jit(solution)/shard_map/ppermute | solution.py:343
  43.8 5.0 %collective-permute-start.7 = (bf16[8,640]{1,0:T(8,128)(2,1)S(1)}, bf16[8,640]{1,0:T(8,128)(2,1)S(1)}, u32[]{:S(2)}, u32[]{:S(2)}) collective-permute-start(bf16[8,640]{1,0:T(8,128)(2,1)S(1)} %pad_maximum_fusion.2), channel_id=1, source_target_pairs={{0,32},{16,48},{32,0},{48,16},{64,96},{80,112},{96,64},{112,80},{1... | collective-permute-start | bytes 30728 | tf_op jit(solution)/shard_map/ppermute | solution.py:346
  46.2 4.1 %collective-permute-start.8 = (bf16[8,640]{1,0:T(8,128)(2,1)S(1)}, bf16[8,640]{1,0:T(8,128)(2,1)S(1)}, u32[]{:S(2)}, u32[]{:S(2)}) collective-permute-start(bf16[8,640]{1,0:T(8,128)(2,1)S(1)} %pad_maximum_fusion.3), channel_id=1, source_target_pairs={{0,64},{16,80},{32,96},{48,112},{64,0},{80,16},{96,32},{112,48},{1... | collective-permute-start | bytes 30728 | tf_op jit(solution)/shard_map/ppermute | solution.py:346
  48.0 3.8 %collective-permute-start.9 = (bf16[8,640]{1,0:T(8,128)(2,1)S(1)}, bf16[8,640]{1,0:T(8,128)(2,1)S(1)}, u32[]{:S(2)}, u32[]{:S(2)}) collective-permute-start(bf16[8,640]{1,0:T(8,128)(2,1)S(1)} %pad_maximum_fusion.4), channel_id=1, source_target_pairs={{0,96},{16,112},{32,64},{48,80},{64,32},{80,48},{96,0},{112,16},{1... | collective-permute-start | bytes 30728 | tf_op jit(solution)/shard_map/ppermute | solution.py:346
  51.8 34.3 %all-to-all-start = ((bf16[16,2,112,256]{3,2,1,0:T(8,128)(2,1)}), bf16[16,2,112,256]{3,2,1,0:T(8,128)(2,1)S(1)}, u32[]{:S(2)}, u32[]{:S(2)}) async-start(bf16[16,2,112,256]{3,2,1,0:T(8,128)(2,1)} %bitcast.51), calls=%async_computation | async-start | bytes 3670016 | tf_op jit(solution)/shard_map/all_to_all | solution.py:350
  60.6 1.3 %collective-permute-start.10 = (bf16[16,640]{1,0:T(8,128)(2,1)S(1)}, bf16[16,640]{1,0:T(8,128)(2,1)S(1)}, u32[]{:S(2)}, u32[]{:S(2)}) collective-permute-start(bf16[16,640]{1,0:T(8,128)(2,1)S(1)} %reshape_squeeze.7), channel_id=1, source_target_pairs={{0,16},{16,0},{32,48},{48,32},{64,80},{80,64},{96,112},{112,96},{1... | collective-permute-start | bytes 61448 | tf_op jit(solution)/shard_map/ppermute | solution.py:346
  61.9 10.7 %collective-permute-start.13 = (bf16[48,640]{1,0:T(8,128)(2,1)S(1)}, bf16[48,640]{1,0:T(8,128)(2,1)S(1)}, u32[]{:S(2)}, u32[]{:S(2)}) collective-permute-start(bf16[48,640]{1,0:T(8,128)(2,1)S(1)} %pad_maximum_fusion), channel_id=1, source_target_pairs={{0,8},{1,9},{2,10},{3,11},{4,12},{5,13},{6,14},{7,15},{8,0},{9,1},... | collective-permute-start | bytes 184328 | tf_op jit(solution)/shard_map/ppermute | solution.py:343
  68.3 5.5 %collective-permute-start.12 = (bf16[48,640]{1,0:T(8,128)(2,1)S(1)}, bf16[48,640]{1,0:T(8,128)(2,1)S(1)}, u32[]{:S(2)}, u32[]{:S(2)}) collective-permute-start(bf16[48,640]{1,0:T(8,128)(2,1)S(1)} %pad_maximum_fusion), channel_id=1, source_target_pairs={{0,12},{1,13},{2,14},{3,15},{4,8},{5,9},{6,10},{7,11},{8,4},{9,5},... | collective-permute-start | bytes 184328 | tf_op jit(solution)/shard_map/ppermute | solution.py:343
  68.3 6.9 %collective-permute-start.11 = (bf16[48,640]{1,0:T(8,128)(2,1)S(1)}, bf16[48,640]{1,0:T(8,128)(2,1)S(1)}, u32[]{:S(2)}, u32[]{:S(2)}) collective-permute-start(bf16[48,640]{1,0:T(8,128)(2,1)S(1)} %pad_maximum_fusion), channel_id=1, source_target_pairs={{0,4},{1,5},{2,6},{3,7},{4,0},{5,1},{6,2},{7,3},{8,12},{9,13},{10,... | collective-permute-start | bytes 184328 | tf_op jit(solution)/shard_map/ppermute | solution.py:343
  75.3 7.1 %collective-permute-start.14 = (bf16[192,640]{1,0:T(8,128)(2,1)S(1)}, bf16[192,640]{1,0:T(8,128)(2,1)S(1)}, u32[]{:S(2)}, u32[]{:S(2)}) collective-permute-start(bf16[192,640]{1,0:T(8,128)(2,1)S(1)} %constant_dynamic-update-slice_fusion.4.refs_0_), channel_id=1, source_target_pairs={{0,2},{1,3},{2,0},{3,1},{4,6},{5,7},{6,4},{7,5},{8,10},{9,11},{10,... | collective-permute-start | bytes 737288 | tf_op jit(solution)/shard_map/ppermute | solution.py:343

commit v6 on v5

--- a/solution.py
+++ b/solution.py
@@ -11,7 +11,7 @@
 REQ = 16
 HD = 128
 NZ = 8
-CUT = 144
+CUTS = (144, 144)
 SMEM = pltpu.SMEM
 VMEM = pltpu.VMEM
 VMEM_LIMIT = 63 * 1024 * 1024
@@ -67,8 +67,14 @@
     return lax.axis_index("pool") * lax.axis_size("group") + lax.axis_index("group")
 
 
-def pack_kernel(start, pairing_in, lengths_in, own_in, new_cache, send, buf, own, pairing, lengths, taken, count, small_sem, in_sem, out_sem):
-    tokens = send.shape[1]
+def pieces_of(late, tokens):
+    if late:
+        return (CUTS[0], 0, tokens - CUTS[0]), (CUTS[1], tokens - CUTS[0], tokens - CUTS[1])
+    return (0, 0, CUTS[0]), (0, CUTS[0], CUTS[1])
+
+
+def pack_kernel(pieces, pairing_in, lengths_in, own_in, new_cache, send, buf, own, pairing, lengths, taken, count, small_sem, in_sem, out_sem):
+    first, tokens = pieces[0][0], buf.shape[1]
     small = [
         pltpu.make_async_copy(pairing_in, pairing, small_sem.at[0]),
         pltpu.make_async_copy(lengths_in, lengths, small_sem.at[1]),
@@ -77,7 +83,7 @@
     for copy in small:
         copy.start()
     load = pltpu.make_async_copy(
-        new_cache.at[:, pl.ds(start, tokens)], buf.at[pl.ds(0, REQ)], in_sem
+        new_cache.at[:, pl.ds(first, tokens)], buf.at[pl.ds(0, REQ)], in_sem
     )
     load.start()
     buf[REQ] = jnp.zeros(buf.shape[1:], buf.dtype)
@@ -92,10 +98,18 @@
         k = count[target]
         count[target] = k + 1
         taken[2 * target + k] = i
+
+    def store(j):
+        start, row, size = pieces[j % 2]
+        source = buf.at[taken[j], pl.ds(start - first, size)]
+        pltpu.make_async_copy(source, send.at[j // 2, pl.ds(row, size)], out_sem).start()
+
+    for j in range(2 * REQ):
+        pl.when(taken[j] == REQ)(functools.partial(store, j))
     row = lax.broadcasted_iota(jnp.int32, (16, 1), 0)
     load.wait()
     for i in range(REQ):
-        at = lengths[i] - start
+        at = lengths[i] - first
 
         @pl.when((at >= 0) & (at < tokens))
         def _():
@@ -106,15 +120,17 @@
             buf[i, pl.ds(base, 16), :] = window.astype(buf.dtype)
 
     for j in range(2 * REQ):
-        pltpu.make_async_copy(buf.at[taken[j]], send.at[j], out_sem).start()
+        pl.when(taken[j] < REQ)(functools.partial(store, j))
     pltpu.make_async_copy(send, send, out_sem).wait()
 
 
-def pack(pairing, new_lengths, new_own, new_cache, start, tokens):
+def pack(pairing, new_lengths, new_own, new_cache, late):
+    pieces = pieces_of(late, new_cache.shape[1])
+    tokens = max(start + size for start, _, size in pieces) - pieces[0][0]
     hbm = pl.BlockSpec(memory_space=pltpu.HBM)
     return pl.pallas_call(
-        functools.partial(pack_kernel, start),
-        out_shape=jax.ShapeDtypeStruct((2 * REQ, tokens, 2 * HD), jnp.bfloat16),
+        functools.partial(pack_kernel, pieces),
+        out_shape=jax.ShapeDtypeStruct((REQ, pieces[0][2] + pieces[1][2], 2 * HD), jnp.bfloat16),
         in_specs=[hbm] * 4,
         out_specs=hbm,
         scratch_shapes=[
@@ -280,35 +296,33 @@
         )
 
 
-def place_kernel(start, part, *refs):
+def place_kernel(pieces, part, *refs):
     whole, sem = refs[-2:]
     size = part.shape[0] // 4
-    copies = [
-        pltpu.make_async_copy(
-            part.at[pl.ds(n * size, size)],
-            whole.at[pl.ds(n * size, size), pl.ds(start, part.shape[1])],
-            sem.at[n],
-        )
-        for n in range(4)
-    ]
+    copies = []
+    for n in range(4):
+        for k in range(2):
+            start, row, tokens = pieces[k]
+            groups = pl.ds(n * size, size)
+            source = part.at[groups, pl.ds(row, tokens)]
+            target = whole.at[groups, k, pl.ds(start, tokens)]
+            copies.append(pltpu.make_async_copy(source, target, sem.at[2 * n + k]))
     for copy in copies:
         copy.start()
     for copy in copies:
         copy.wait()
 
 
-def place(part, start, whole):
+def place(part, late, whole):
     given = [part] if isinstance(whole, tuple) else [part, whole]
     shape = whole if isinstance(whole, tuple) else whole.shape
-    any_space = pl.BlockSpec(memory_space=pltpu.HBM)
+    hbm = pl.BlockSpec(memory_space=pltpu.HBM)
     return pl.pallas_call(
-        functools.partial(place_kernel, start),
+        functools.partial(place_kernel, pieces_of(late, shape[2])),
         out_shape=jax.ShapeDtypeStruct(shape, part.dtype),
-        in_specs=[pl.BlockSpec(memory_space=VMEM)] + [any_space] * (len(given) - 1),
-        out_specs=any_space,
-        scratch_shapes=[
-            pltpu.SemaphoreType.DMA((4,)),
-        ],
+        in_specs=[pl.BlockSpec(memory_space=VMEM)] + [hbm] * (len(given) - 1),
+        out_specs=hbm,
+        scratch_shapes=[pltpu.SemaphoreType.DMA((8,))],
         compiler_params=pltpu.CompilerParams(vmem_limit_bytes=SMALL_LIMIT),
         input_output_aliases={} if len(given) == 1 else {1: 0},
         cost_estimate=pl.CostEstimate(flops=0, bytes_accessed=2 * part.size * 2, transcendentals=0),
@@ -346,12 +360,11 @@
         return lax.ppermute(array, both, [(s, s ^ flip) for s in range(groups)])
 
     def deliver(array):
-        blocks = array.reshape((groups, 2) + array.shape[1:])
-        return lax.all_to_all(blocks, both, split_axis=0, concat_axis=0, tiled=True).reshape(array.shape)
+        return lax.all_to_all(array, both, split_axis=0, concat_axis=0, tiled=True)
 
     prompt = (pair, new_lengths[0, 0], new_step_kv[0, 0, :, 0], prompts)
-    early = deliver(pack(*prompt, 0, CUT))
-    late = pack(*prompt, CUT, prompts.shape[1] - CUT)
+    early = deliver(pack(*prompt, False))
+    late = pack(*prompt, True)
 
     first, keep_three, send_four, chosen = front(
         pair,
@@ -372,7 +385,7 @@
         (over_tp(send_four, 2), norm_gain.reshape(1, -1), late)
     )
     parts = [four]
-    for n, flip in enumerate((2, 4, 6)):
+    for n, flip in ((0, 2), (2, 6), (1, 4)):
         summed = keep_three[2 * REQ * n : 2 * REQ * (n + 1)]
         summed = summed + four[2 * REQ * (n + 1) : 2 * REQ * (n + 2)].astype(jnp.float32)
         parts.append(over_tp(summed.astype(jnp.bfloat16), 2 * flip))
@@ -406,7 +419,7 @@
     kept, given = (slots[:, :, c].reshape(REQ, width) for c in range(2))
     block = jnp.concatenate([near[:REQ], kept, over_groups(given, 1)], axis=0)
 
-    slot_cache = place(early, 0, (2 * REQ,) + prompts.shape[1:])
+    slot_cache = place(early, False, (groups, 2) + prompts.shape[1:])
     flips = [over_tp(block, 2 * k) for k in (2, 6, 4)]
     *flips, slot_cache = lax.optimization_barrier((*flips, slot_cache))
     four = jnp.concatenate([block, *flips], axis=0)
@@ -422,7 +435,7 @@
     )(gain, *blocks)
 
     late, hidden = lax.optimization_barrier((late, hidden))
-    slot_cache = place(late, CUT, slot_cache)
+    slot_cache = place(late, True, slot_cache).reshape((2 * groups,) + prompts.shape[1:])
     return (hidden[None, None], normed[None, None], slot_cache[None, None, :, :, None, :])
 
 

time: 87.7 us -> 86.7 us (0.989)
  waiting for transfers between devices: 25.9 us -> 23.8 us
  starting transfers between devices: 43.8 us -> 45.5 us
    ppermute x5, waiting for transfers between devices: 5 us -> 2.95 us  [over_groups(): return lax.ppermute(array, both, [(s, s ^ flip) for s in range(groups)])]
    ppermute x1, waiting for transfers between devices: 2.69 us -> 4.03 us  [body(): far_there = lax.ppermute(far, ('pool', 'tp'), across)]
where the time goes in v6:
time: 86.7 us; the launch traced here: 86.4 us
  starting transfers between devices  45.5 us (52%)
  waiting for transfers between devices  23.8 us (27%)
  Pallas kernels  15.7 us (18%)
  between operations  1 us (1%)
    ppermute x9, starting transfers between devices, over_tp(): return lax.ppermute(array, 'tp', [(t, t ^ flip) for t in range(ranks)])  19 us
    all_to_all x2, starting transfers between devices, deliver(): return lax.all_to_all(array, both, split_axis=0, concat_axis=0, tiled=True)  17.8 us
    ppermute x9, waiting for transfers between devices, over_tp(): return lax.ppermute(array, 'tp', [(t, t ^ flip) for t in range(ranks)])  14.9 us
    ppermute x5, starting transfers between devices, over_groups(): return lax.ppermute(array, both, [(s, s ^ flip) for s in range(groups)])  6.05 us
    pallas_call x1, Pallas kernels, front(): pl.pallas_call(front_kernel, out_shape=[jax.ShapeDtypeStruct((2 * REQ, wi...  5.11 us
    pallas_call x2, Pallas kernels, pack(): pl.pallas_call(functools.partial(pack_kernel, pieces), out_shape=jax.Shap...  4.87 us
    pallas_call x2, Pallas kernels, place(): pl.pallas_call(functools.partial(place_kernel, pieces_of(late, shape[2]))...  4.41 us
    ppermute x1, waiting for transfers between devices, body(): far_there = lax.ppermute(far, ('pool', 'tp'), across)  4.03 us
  transfers between devices with their start and end apart: 17, of which 11 were waited for; matrix products, arithmetic and copies ran while one was open for 0% of the time, Pallas kernels for 14%

profile of v6, /device:TPU:1, one launch (start us, length us, event | category | flops | bytes accessed | tf_op | source)
XLA Modules:
  0.0 86.4 jit_solution(1751846837395352320)
XLA Ops:
  0.6 2.5 %pack.3 = bf16[16,288,256]{2,1,0:T(8,128)(2,1)} custom-call(s32[16]{0:T(128)} %bitcast.33, s32[16]{0:T(128)} %bitcast.36, bf16[16,256]{1,0:T(8,128)(2,1)} %bitcast.27, bf16[16,256,256]{2,1,0:T(8,128)(2,1)} %bitcast.41), custom_call_target="tpu_custom_call" | custom-call | bytes 3600000 | tf_op jit(solution)/shard_map/pack/pallas_call | solution.py:131
  3.2 0.0 copy-start
  3.2 0.0 copy-start.1
  3.2 0.0 copy-start.2
  3.2 0.0 copy-start.3
  3.2 0.0 copy-start.4
  3.2 0.0 copy-start.5
  3.3 0.0 copy-start.6
  3.3 0.0 copy-start.7
  3.3 0.0 copy-start.8
  3.3 0.0 copy-start.9
  3.3 8.6 %all-to-all-start.1 = ((bf16[16,288,256]{2,1,0:T(8,128)(2,1)}), bf16[16,288,256]{2,1,0:T(8,128)(2,1)}, u32[]{:S(2)}, u32[]{:S(2)}) async-start(bf16[16,288,256]{2,1,0:T(8,128)(2,1)} %pack.3), calls=%async_computation.1 | async-start | bytes 4718592 | tf_op jit(solution)/shard_map/all_to_all | solution.py:363
  11.9 0.0 copy-done
  11.9 0.0 copy-done.1
  11.9 0.0 copy-done.2
  11.9 0.0 copy-done.3
  11.9 0.0 copy-done.4
  11.9 0.0 copy-done.5
  11.9 0.0 copy-done.6
  12.0 0.0 copy-done.7
  12.0 0.0 copy-done.8
  12.0 0.0 copy-done.9
  12.0 5.1 %front.1 = (f32[32,640]{1,0:T(8,128)S(1)}, f32[96,640]{1,0:T(8,128)S(1)}, bf16[128,640]{1,0:T(8,128)(2,1)S(1)}, bf16[32,16]{1,0:T(8,128)(2,1)S(1)}) custom-call(s32[16]{0:T(128)S(1)} %bitcast.35, s32[16]{0:T(128)S(1)} %bitcast.39, s32[64]{0:T(128)S(1)} %bitcast.40, s32[16]{0:T(128)S(1)} %bitcast.38, bf16[16,256]{1,0:T(8,128)(2,1)S(1)} %bitcast.30, ...), custom_call_target="tpu_custom_call" | custom-call | flops 400000000 | bytes 9500000 | tf_op jit(solution)/shard_map/front/pallas_call | solution.py:229
  17.1 0.0 copy-start.10
  17.1 1.7 %collective-permute-start = (bf16[128,640]{1,0:T(8,128)(2,1)S(1)}, bf16[128,640]{1,0:T(8,128)(2,1)S(1)}, u32[]{:S(2)}, u32[]{:S(2)}) collective-permute-start(bf16[128,640]{1,0:T(8,128)(2,1)S(1)} %get-tuple-element.25), channel_id=1, source_target_pairs={{0,2},{1,3},{2,0},{3,1},{4,6},{5,7},{6,4},{7,5},{8,10},{9,11},{10,... | collective-permute-start | bytes 491528 | tf_op jit(solution)/shard_map/ppermute | solution.py:357
  18.8 2.3 %pack.2 = bf16[16,224,256]{2,1,0:T(8,128)(2,1)} custom-call(s32[16]{0:T(128)} %bitcast.34, s32[16]{0:T(128)} %bitcast.37, bf16[16,256]{1,0:T(8,128)(2,1)} %bitcast.28, bf16[16,256,256]{2,1,0:T(8,128)(2,1)} %bitcast.43), custom_call_target="tpu_custom_call" | custom-call | bytes 2800000 | tf_op jit(solution)/shard_map/pack/pallas_call | solution.py:131
  21.2 0.0 copy-done.10
  21.2 2.1 %collective-permute-done.refs_0_ = bf16[128,640]{1,0:T(8,128)(2,1)S(1)} collective-permute-done((bf16[128,640]{1,0:T(8,128)(2,1)S(1)}, bf16[128,640]{1,0:T(8,128)(2,1)S(1)}, u32[]{:S(2)}, u32[]{:S(2)}) %collective-permute-start) | collective-permute-done | bytes 163872 | tf_op jit(solution)/shard_map/ppermute | solution.py:357
  23.4 6.6 %collective-permute-start.3 = (bf16[32,640]{1,0:T(8,128)(2,1)S(1)}, bf16[32,640]{1,0:T(8,128)(2,1)S(1)}, u32[]{:S(2)}, u32[]{:S(2)}) collective-permute-start(bf16[32,640]{1,0:T(8,128)(2,1)S(1)} %get-tuple-element.50), channel_id=1, source_target_pairs={{0,8},{1,9},{2,10},{3,11},{4,12},{5,13},{6,14},{7,15},{8,0},{9,1},... | collective-permute-start | bytes 122888 | tf_op jit(solution)/shard_map/ppermute | solution.py:357
  30.0 0.0 collective-permute-start.2
  30.0 1.2 %collective-permute-start.1 = (bf16[32,640]{1,0:T(8,128)(2,1)S(1)}, bf16[32,640]{1,0:T(8,128)(2,1)S(1)}, u32[]{:S(2)}, u32[]{:S(2)}) collective-permute-start(bf16[32,640]{1,0:T(8,128)(2,1)S(1)} %get-tuple-element.52), channel_id=1, source_target_pairs={{0,4},{1,5},{2,6},{3,7},{4,0},{5,1},{6,2},{7,3},{8,12},{9,13},{10,... | collective-permute-start | bytes 122888 | tf_op jit(solution)/shard_map/ppermute | solution.py:357
  31.2 0.6 collective-permute-done.3.refs_3_
  31.8 3.4 %collective-permute-done.2.refs_2_ = bf16[32,640]{1,0:T(8,128)(2,1)S(1)} collective-permute-done((bf16[32,640]{1,0:T(8,128)(2,1)S(1)}, bf16[32,640]{1,0:T(8,128)(2,1)S(1)}, u32[]{:S(2)}, u32[]{:S(2)}) %collective-permute-start.2) | collective-permute-done | bytes 40992 | tf_op jit(solution)/shard_map/ppermute | solution.py:357
  35.2 0.0 collective-permute-done.1.refs_1_
  35.2 0.1 spread.1
  35.3 2.6 %collective-permute-start.6 = (bf16[16,640]{1,0:T(8,128)(2,1)S(1)}, bf16[16,640]{1,0:T(8,128)(2,1)S(1)}, u32[]{:S(2)}, u32[]{:S(2)}) collective-permute-start(bf16[16,640]{1,0:T(8,128)(2,1)S(1)} %get-tuple-element.32), channel_id=1, source_target_pairs={{0,129},{1,128},{2,131},{3,130},{4,133},{5,132},{6,135},{7,134},{8... | collective-permute-start | bytes 61448 | tf_op jit(solution)/shard_map/ppermute | solution.py:407
  38.0 0.4 collective-permute-start.5
  38.3 0.4 collective-permute-start.4
  38.7 4.0 %collective-permute-done.6 = bf16[16,640]{1,0:T(8,128)(2,1)S(1)} collective-permute-done((bf16[16,640]{1,0:T(8,128)(2,1)S(1)}, bf16[16,640]{1,0:T(8,128)(2,1)S(1)}, u32[]{:S(2)}, u32[]{:S(2)}) %collective-permute-start.6) | collective-permute-done | bytes 20512 | tf_op jit(solution)/shard_map/ppermute | solution.py:407
  42.7 0.0 collective-permute-done.5
  42.7 0.0 collective-permute-done.4
  42.8 2.9 %collective-permute-start.7 = (bf16[8,640]{1,0:T(8,128)(2,1)S(1)}, bf16[8,640]{1,0:T(8,128)(2,1)S(1)}, u32[]{:S(2)}, u32[]{:S(2)}) collective-permute-start(bf16[8,640]{1,0:T(8,128)(2,1)S(1)} %pad_maximum_fusion.2), channel_id=1, source_target_pairs={{0,32},{16,48},{32,0},{48,16},{64,96},{80,112},{96,64},{112,80},{1... | collective-permute-start | bytes 30728 | tf_op jit(solution)/shard_map/ppermute | solution.py:360
  45.7 0.7 collective-permute-start.8
  46.4 1.9 %collective-permute-start.9 = (bf16[8,640]{1,0:T(8,128)(2,1)S(1)}, bf16[8,640]{1,0:T(8,128)(2,1)S(1)}, u32[]{:S(2)}, u32[]{:S(2)}) collective-permute-start(bf16[8,640]{1,0:T(8,128)(2,1)S(1)} %pad_maximum_fusion.4), channel_id=1, source_target_pairs={{0,96},{16,112},{32,64},{48,80},{64,32},{80,48},{96,0},{112,16},{1... | collective-permute-start | bytes 30728 | tf_op jit(solution)/shard_map/ppermute | solution.py:360
  48.3 0.0 collective-permute-done.7
  48.4 1.5 %collective-permute-done.8 = bf16[8,640]{1,0:T(8,128)(2,1)S(1)} collective-permute-done((bf16[8,640]{1,0:T(8,128)(2,1)S(1)}, bf16[8,640]{1,0:T(8,128)(2,1)S(1)}, u32[]{:S(2)}, u32[]{:S(2)}) %collective-permute-start.8) | collective-permute-done | bytes 10272 | tf_op jit(solution)/shard_map/ppermute | solution.py:360
  49.9 0.4 collective-permute-done.9
  50.2 0.0 all-to-all-done.1.part
  50.2 9.2 %all-to-all-start = ((bf16[16,224,256]{2,1,0:T(8,128)(2,1)}), bf16[16,224,256]{2,1,0:T(8,128)(2,1)S(1)}, u32[]{:S(2)}, u32[]{:S(2)}) async-start(bf16[16,224,256]{2,1,0:T(8,128)(2,1)} %pack.2), calls=%async_computation | async-start | bytes 3670016 | tf_op jit(solution)/shard_map/all_to_all | solution.py:363
  59.7 0.2 collective-permute-start.10
  59.9 1.1 %collective-permute-done.10 = bf16[16,640]{1,0:T(8,128)(2,1)S(1)} collective-permute-done((bf16[16,640]{1,0:T(8,128)(2,1)S(1)}, bf16[16,640]{1,0:T(8,128)(2,1)S(1)}, u32[]{:S(2)}, u32[]{:S(2)}) %collective-permute-start.10) | collective-permute-done | bytes 20512 | tf_op jit(solution)/shard_map/ppermute | solution.py:360
  61.0 7.0 %collective-permute-start.13 = (bf16[48,640]{1,0:T(8,128)(2,1)S(1)}, bf16[48,640]{1,0:T(8,128)(2,1)S(1)}, u32[]{:S(2)}, u32[]{:S(2)}) collective-permute-start(bf16[48,640]{1,0:T(8,128)(2,1)S(1)} %pad_maximum_fusion), channel_id=1, source_target_pairs={{0,8},{1,9},{2,10},{3,11},{4,12},{5,13},{6,14},{7,15},{8,0},{9,1},... | collective-permute-start | bytes 184328 | tf_op jit(solution)/shard_map/ppermute | solution.py:357
  68.0 0.0 collective-permute-start.12
  68.0 1.2 %collective-permute-start.11 = (bf16[48,640]{1,0:T(8,128)(2,1)S(1)}, bf16[48,640]{1,0:T(8,128)(2,1)S(1)}, u32[]{:S(2)}, u32[]{:S(2)}) collective-permute-start(bf16[48,640]{1,0:T(8,128)(2,1)S(1)} %pad_maximum_fusion), channel_id=1, source_target_pairs={{0,4},{1,5},{2,6},{3,7},{4,0},{5,1},{6,2},{7,3},{8,12},{9,13},{10,... | collective-permute-start | bytes 184328 | tf_op jit(solution)/shard_map/ppermute | solution.py:357
  69.2 3.1 %place.2.refs_0_ = bf16[16,2,256,256]{3,2,1,0:T(8,128)(2,1)} custom-call(bf16[16,288,256]{2,1,0:T(8,128)(2,1)} %all-to-all-done.1.part), custom_call_target="tpu_custom_call" | custom-call | bytes 4718592 | tf_op jit(solution)/shard_map/place/pallas_call | solution.py:320
  72.3 0.0 collective-permute-done.13
  72.4 1.1 %collective-permute-done.12 = bf16[48,640]{1,0:T(8,128)(2,1)S(1)} collective-permute-done((bf16[48,640]{1,0:T(8,128)(2,1)S(1)}, bf16[48,640]{1,0:T(8,128)(2,1)S(1)}, u32[]{:S(2)}, u32[]{:S(2)}) %collective-permute-start.12) | collective-permute-done | bytes 61472 | tf_op jit(solution)/shard_map/ppermute | solution.py:357
  73.4 1.5 %collective-permute-done.11 = bf16[48,640]{1,0:T(8,128)(2,1)S(1)} collective-permute-done((bf16[48,640]{1,0:T(8,128)(2,1)S(1)}, bf16[48,640]{1,0:T(8,128)(2,1)S(1)}, u32[]{:S(2)}, u32[]{:S(2)}) %collective-permute-start.11) | collective-permute-done | bytes 61472 | tf_op jit(solution)/shard_map/ppermute | solution.py:357
  74.9 0.9 %collective-permute-start.14 = (bf16[192,640]{1,0:T(8,128)(2,1)S(1)}, bf16[192,640]{1,0:T(8,128)(2,1)S(1)}, u32[]{:S(2)}, u32[]{:S(2)}) collective-permute-start(bf16[192,640]{1,0:T(8,128)(2,1)S(1)} %constant_dynamic-update-slice_fusion.4.refs_0_), channel_id=1, source_target_pairs={{0,2},{1,3},{2,0},{3,1},{4,6},{5,7},{6,4},{7,5},{8,10},{9,11},{10,... | collective-permute-start | bytes 737288 | tf_op jit(solution)/shard_map/ppermute | solution.py:357
  75.8 6.2 %collective-permute-done.14.refs_1_ = bf16[192,640]{1,0:T(8,128)(2,1)S(1)} collective-permute-done((bf16[192,640]{1,0:T(8,128)(2,1)S(1)}, bf16[192,640]{1,0:T(8,128)(2,1)S(1)}, u32[]{:S(2)}, u32[]{:S(2)}) %collective-permute-start.14) | collective-permute-done | bytes 245792 | tf_op jit(solution)/shard_map/ppermute | solution.py:357
  82.1 1.2 %finish.1 = (bf16[48,5120]{1,0:T(8,128)(2,1)}, bf16[48,5120]{1,0:T(8,128)(2,1)}) custom-call(bf16[1,5120]{1,0:T(2,128)(2,1)S(1)} %reshape.18.gain, bf16[192,640]{1,0:T(8,128)(2,1)S(1)} %constant_dynamic-update-slice_fusion.4.refs_0_, bf16[192,640]{1,0:T(8,128)(2,1)S(1)} %collective-permute-done.14.refs_1_), custom_call_target="tpu_custom_call" | custom-call | bytes 4000000 | tf_op jit(solution)/shard_map/finish/pallas_call | solution.py:427
  83.3 1.9 %all-to-all-done.part = bf16[16,224,256]{2,1,0:T(8,128)(2,1)S(1)} async-done(((bf16[16,224,256]{2,1,0:T(8,128)(2,1)}), bf16[16,224,256]{2,1,0:T(8,128)(2,1)S(1)}, u32[]{:S(2)}, u32[]{:S(2)}) %all-to-all-start) | async-done | bytes 1835040 | tf_op jit(solution)/shard_map/all_to_all | solution.py:363
  85.1 1.3 %place.3 = bf16[16,2,256,256]{3,2,1,0:T(8,128)(2,1)} custom-call(bf16[16,224,256]{2,1,0:T(8,128)(2,1)S(1)} %all-to-all-done.part, bf16[16,2,256,256]{3,2,1,0:T(8,128)(2,1)} %place.2.refs_0_), custom_call_target="tpu_custom_call", output_to_operand_aliasing={{}: (1, {})} | custom-call | bytes 3670016 | tf_op jit(solution)/shard_map/place/pallas_call | solution.py:320
  (28 shorter events, 0.4 us)
Async XLA Ops:
  3.2 8.7 %copy-start = (bf16[1,1,16,5120]{3,2,1,0:T(8,128)(2,1)S(1)}, bf16[1,1,16,5120]{3,2,1,0:T(8,128)(2,1)}, u32[]{:S(2)}) copy-start(bf16[1,1,16,5120]{3,2,1,0:T(8,128)(2,1)} %param.19) | copy-start | bytes 491524
  3.2 8.7 %copy-start.1 = (bf16[1,1,16,5120]{3,2,1,0:T(8,128)(2,1)S(1)}, bf16[1,1,16,5120]{3,2,1,0:T(8,128)(2,1)}, u32[]{:S(2)}) copy-start(bf16[1,1,16,5120]{3,2,1,0:T(8,128)(2,1)} %param.24) | copy-start | bytes 491524
  3.2 8.7 %copy-start.2 = (bf16[1,1,16,1,256]{4,2,3,1,0:T(8,128)(2,1)S(1)}, bf16[1,1,16,1,256]{4,2,3,1,0:T(8,128)(2,1)}, u32[]{:S(2)}) copy-start(bf16[1,1,16,1,256]{4,2,3,1,0:T(8,128)(2,1)} %param.23) | copy-start | bytes 24580
  3.2 8.7 %copy-start.3 = (bf16[1,1,16,256]{3,2,1,0:T(8,128)(2,1)S(1)}, bf16[1,1,16,256]{3,2,1,0:T(8,128)(2,1)}, u32[]{:S(2)}) copy-start(bf16[1,1,16,256]{3,2,1,0:T(8,128)(2,1)} %param.17) | copy-start | bytes 24580
  3.2 8.7 %copy-start.4 = (bf16[1,1,16,1,256]{4,2,3,1,0:T(8,128)(2,1)S(1)}, bf16[1,1,16,1,256]{4,2,3,1,0:T(8,128)(2,1)}, u32[]{:S(2)}) copy-start(bf16[1,1,16,1,256]{4,2,3,1,0:T(8,128)(2,1)} %param.18) | copy-start | bytes 24580
  3.2 8.7 %copy-start.5 = (bf16[1,1,16,256]{3,2,1,0:T(8,128)(2,1)S(1)}, bf16[1,1,16,256]{3,2,1,0:T(8,128)(2,1)}, u32[]{:S(2)}) copy-start(bf16[1,1,16,256]{3,2,1,0:T(8,128)(2,1)} %param.22) | copy-start | bytes 24580
  3.3 8.7 %copy-start.6 = (s32[1,1,16,1]{2,3,1,0:T(1,128)S(1)}, s32[1,1,16,1]{2,3,1,0:T(1,128)}, u32[]{:S(2)}) copy-start(s32[1,1,16,1]{2,3,1,0:T(1,128)} %param.25) | copy-start | bytes 196
  3.3 8.7 %copy-start.7 = (s32[1,1,16]{2,1,0:T(1,128)S(1)}, s32[1,1,16]{2,1,0:T(1,128)}, u32[]{:S(2)}) copy-start(s32[1,1,16]{2,1,0:T(1,128)} %param.21) | copy-start | bytes 196
  3.3 8.7 %copy-start.8 = (s32[1,1,16]{2,1,0:T(1,128)S(1)}, s32[1,1,16]{2,1,0:T(1,128)}, u32[]{:S(2)}) copy-start(s32[1,1,16]{2,1,0:T(1,128)} %param.16) | copy-start | bytes 196
  3.3 8.7 %copy-start.9 = (s32[1,1,64]{2,1,0:T(1,128)S(1)}, s32[1,1,64]{2,1,0:T(1,128)}, u32[]{:S(2)}) copy-start(s32[1,1,64]{2,1,0:T(1,128)} %param.15) | copy-start | bytes 772
  3.3 46.9 %all-to-all-start.1 = ((bf16[16,288,256]{2,1,0:T(8,128)(2,1)}), bf16[16,288,256]{2,1,0:T(8,128)(2,1)}, u32[]{:S(2)}, u32[]{:S(2)}) async-start(bf16[16,288,256]{2,1,0:T(8,128)(2,1)} %pack.3), calls=%async_computation.1 | async-start | bytes 4718592 | tf_op jit(solution)/shard_map/all_to_all | solution.py:363
  17.1 4.1 %copy-start.10 = (bf16[5120]{0:T(1024)(128)(2,1)S(1)}, bf16[5120]{0:T(1024)(128)(2,1)}, u32[]{:S(2)}) copy-start(bf16[5120]{0:T(1024)(128)(2,1)} %param.27) | copy-start | bytes 30724
  17.1 6.2 %collective-permute-start = (bf16[128,640]{1,0:T(8,128)(2,1)S(1)}, bf16[128,640]{1,0:T(8,128)(2,1)S(1)}, u32[]{:S(2)}, u32[]{:S(2)}) collective-permute-start(bf16[128,640]{1,0:T(8,128)(2,1)S(1)} %get-tuple-element.25), channel_id=1, source_target_pairs={{0,2},{1,3},{2,0},{3,1},{4,6},{5,7},{6,4},{7,5},{8,10},{9,11},{10,... | collective-permute-start | bytes 491528 | tf_op jit(solution)/shard_map/ppermute | solution.py:357
  23.4 8.4 %collective-permute-start.3 = (bf16[32,640]{1,0:T(8,128)(2,1)S(1)}, bf16[32,640]{1,0:T(8,128)(2,1)S(1)}, u32[]{:S(2)}, u32[]{:S(2)}) collective-permute-start(bf16[32,640]{1,0:T(8,128)(2,1)S(1)} %get-tuple-element.50), channel_id=1, source_target_pairs={{0,8},{1,9},{2,10},{3,11},{4,12},{5,13},{6,14},{7,15},{8,0},{9,1},... | collective-permute-start | bytes 122888 | tf_op jit(solution)/shard_map/ppermute | solution.py:357
  30.0 5.2 %collective-permute-start.2 = (bf16[32,640]{1,0:T(8,128)(2,1)S(1)}, bf16[32,640]{1,0:T(8,128)(2,1)S(1)}, u32[]{:S(2)}, u32[]{:S(2)}) collective-permute-start(bf16[32,640]{1,0:T(8,128)(2,1)S(1)} %get-tuple-element.51), channel_id=1, source_target_pairs={{0,12},{1,13},{2,14},{3,15},{4,8},{5,9},{6,10},{7,11},{8,4},{9,5},... | collective-permute-start | bytes 122888 | tf_op jit(solution)/shard_map/ppermute | solution.py:357
  30.0 5.2 %collective-permute-start.1 = (bf16[32,640]{1,0:T(8,128)(2,1)S(1)}, bf16[32,640]{1,0:T(8,128)(2,1)S(1)}, u32[]{:S(2)}, u32[]{:S(2)}) collective-permute-start(bf16[32,640]{1,0:T(8,128)(2,1)S(1)} %get-tuple-element.52), channel_id=1, source_target_pairs={{0,4},{1,5},{2,6},{3,7},{4,0},{5,1},{6,2},{7,3},{8,12},{9,13},{10,... | collective-permute-start | bytes 122888 | tf_op jit(solution)/shard_map/ppermute | solution.py:357
  35.3 7.4 %collective-permute-start.6 = (bf16[16,640]{1,0:T(8,128)(2,1)S(1)}, bf16[16,640]{1,0:T(8,128)(2,1)S(1)}, u32[]{:S(2)}, u32[]{:S(2)}) collective-permute-start(bf16[16,640]{1,0:T(8,128)(2,1)S(1)} %get-tuple-element.32), channel_id=1, source_target_pairs={{0,129},{1,128},{2,131},{3,130},{4,133},{5,132},{6,135},{7,134},{8... | collective-permute-start | bytes 61448 | tf_op jit(solution)/shard_map/ppermute | solution.py:407
  38.0 4.8 %collective-permute-start.5 = (bf16[16,640]{1,0:T(8,128)(2,1)S(1)}, bf16[16,640]{1,0:T(8,128)(2,1)S(1)}, u32[]{:S(2)}, u32[]{:S(2)}) collective-permute-start(bf16[16,640]{1,0:T(8,128)(2,1)S(1)} %get-tuple-element.32), channel_id=1, source_target_pairs={{0,128},{16,144},{32,160},{48,176},{64,192},{80,208},{96,224},{112... | collective-permute-start | bytes 61448 | tf_op jit(solution)/shard_map/ppermute | solution.py:360
  38.3 4.4 %collective-permute-start.4 = (bf16[32,640]{1,0:T(8,128)(2,1)S(1)}, bf16[32,640]{1,0:T(8,128)(2,1)S(1)}, u32[]{:S(2)}, u32[]{:S(2)}) collective-permute-start(bf16[32,640]{1,0:T(8,128)(2,1)S(1)} %get-tuple-element.31), channel_id=1, source_target_pairs={{0,1},{1,0},{2,3},{3,2},{4,5},{5,4},{6,7},{7,6},{8,9},{9,8},{10,11... | collective-permute-start | bytes 122888 | tf_op jit(solution)/shard_map/ppermute | solution.py:357
  42.8 5.5 %collective-permute-start.7 = (bf16[8,640]{1,0:T(8,128)(2,1)S(1)}, bf16[8,640]{1,0:T(8,128)(2,1)S(1)}, u32[]{:S(2)}, u32[]{:S(2)}) collective-permute-start(bf16[8,640]{1,0:T(8,128)(2,1)S(1)} %pad_maximum_fusion.2), channel_id=1, source_target_pairs={{0,32},{16,48},{32,0},{48,16},{64,96},{80,112},{96,64},{112,80},{1... | collective-permute-start | bytes 30728 | tf_op jit(solution)/shard_map/ppermute | solution.py:360
  45.7 4.1 %collective-permute-start.8 = (bf16[8,640]{1,0:T(8,128)(2,1)S(1)}, bf16[8,640]{1,0:T(8,128)(2,1)S(1)}, u32[]{:S(2)}, u32[]{:S(2)}) collective-permute-start(bf16[8,640]{1,0:T(8,128)(2,1)S(1)} %pad_maximum_fusion.3), channel_id=1, source_target_pairs={{0,64},{16,80},{32,96},{48,112},{64,0},{80,16},{96,32},{112,48},{1... | collective-permute-start | bytes 30728 | tf_op jit(solution)/shard_map/ppermute | solution.py:360
  46.4 3.8 %collective-permute-start.9 = (bf16[8,640]{1,0:T(8,128)(2,1)S(1)}, bf16[8,640]{1,0:T(8,128)(2,1)S(1)}, u32[]{:S(2)}, u32[]{:S(2)}) collective-permute-start(bf16[8,640]{1,0:T(8,128)(2,1)S(1)} %pad_maximum_fusion.4), channel_id=1, source_target_pairs={{0,96},{16,112},{32,64},{48,80},{64,32},{80,48},{96,0},{112,16},{1... | collective-permute-start | bytes 30728 | tf_op jit(solution)/shard_map/ppermute | solution.py:360
  50.2 34.9 %all-to-all-start = ((bf16[16,224,256]{2,1,0:T(8,128)(2,1)}), bf16[16,224,256]{2,1,0:T(8,128)(2,1)S(1)}, u32[]{:S(2)}, u32[]{:S(2)}) async-start(bf16[16,224,256]{2,1,0:T(8,128)(2,1)} %pack.2), calls=%async_computation | async-start | bytes 3670016 | tf_op jit(solution)/shard_map/all_to_all | solution.py:363
  59.7 1.3 %collective-permute-start.10 = (bf16[16,640]{1,0:T(8,128)(2,1)S(1)}, bf16[16,640]{1,0:T(8,128)(2,1)S(1)}, u32[]{:S(2)}, u32[]{:S(2)}) collective-permute-start(bf16[16,640]{1,0:T(8,128)(2,1)S(1)} %reshape_squeeze.7), channel_id=1, source_target_pairs={{0,16},{16,0},{32,48},{48,32},{64,80},{80,64},{96,112},{112,96},{1... | collective-permute-start | bytes 61448 | tf_op jit(solution)/shard_map/ppermute | solution.py:360
  61.0 11.3 %collective-permute-start.13 = (bf16[48,640]{1,0:T(8,128)(2,1)S(1)}, bf16[48,640]{1,0:T(8,128)(2,1)S(1)}, u32[]{:S(2)}, u32[]{:S(2)}) collective-permute-start(bf16[48,640]{1,0:T(8,128)(2,1)S(1)} %pad_maximum_fusion), channel_id=1, source_target_pairs={{0,8},{1,9},{2,10},{3,11},{4,12},{5,13},{6,14},{7,15},{8,0},{9,1},... | collective-permute-start | bytes 184328 | tf_op jit(solution)/shard_map/ppermute | solution.py:357
  68.0 5.5 %collective-permute-start.12 = (bf16[48,640]{1,0:T(8,128)(2,1)S(1)}, bf16[48,640]{1,0:T(8,128)(2,1)S(1)}, u32[]{:S(2)}, u32[]{:S(2)}) collective-permute-start(bf16[48,640]{1,0:T(8,128)(2,1)S(1)} %pad_maximum_fusion), channel_id=1, source_target_pairs={{0,12},{1,13},{2,14},{3,15},{4,8},{5,9},{6,10},{7,11},{8,4},{9,5},... | collective-permute-start | bytes 184328 | tf_op jit(solution)/shard_map/ppermute | solution.py:357
  68.0 6.9 %collective-permute-start.11 = (bf16[48,640]{1,0:T(8,128)(2,1)S(1)}, bf16[48,640]{1,0:T(8,128)(2,1)S(1)}, u32[]{:S(2)}, u32[]{:S(2)}) collective-permute-start(bf16[48,640]{1,0:T(8,128)(2,1)S(1)} %pad_maximum_fusion), channel_id=1, source_target_pairs={{0,4},{1,5},{2,6},{3,7},{4,0},{5,1},{6,2},{7,3},{8,12},{9,13},{10,... | collective-permute-start | bytes 184328 | tf_op jit(solution)/shard_map/ppermute | solution.py:357
  74.9 7.1 %collective-permute-start.14 = (bf16[192,640]{1,0:T(8,128)(2,1)S(1)}, bf16[192,640]{1,0:T(8,128)(2,1)S(1)}, u32[]{:S(2)}, u32[]{:S(2)}) collective-permute-start(bf16[192,640]{1,0:T(8,128)(2,1)S(1)} %constant_dynamic-update-slice_fusion.4.refs_0_), channel_id=1, source_target_pairs={{0,2},{1,3},{2,0},{3,1},{4,6},{5,7},{6,4},{7,5},{8,10},{9,11},{10,... | collective-permute-start | bytes 737288 | tf_op jit(solution)/shard_map/ppermute | solution.py:357

commit v7 on v6

--- a/solution.py
+++ b/solution.py
@@ -174,38 +174,6 @@
     weight_copy.start()
     for copy in small:
         copy.wait()
-    new_copy.wait()
-
-    new_rows = attend(
-        new_query[...],
-        new_own[...],
-        lambda r: new_buf[r],
-        lambda r: new_lengths[r],
-        new_buf.shape[1],
-    )
-
-    pltpu.make_async_copy(cache, kv_buf, kv_sem).wait()
-    rows = attend(
-        query[...],
-        own[...],
-        lambda r: kv_buf[4 * r : 4 * r + 4].reshape(4 * kv_buf.shape[1], 2 * HD),
-        lambda r: lengths[r],
-        4 * kv_buf.shape[1],
-    )
-    attended = jnp.concatenate([rows, new_rows], axis=0)
-    weight_copy.wait()
-
-    def part(flip):
-        columns = pl.ds(pl.multiple_of((z ^ flip) * width, 128), width)
-        return jnp.dot(attended, weight[:, columns], preferred_element_type=jnp.float32)
-
-    for n, flip in enumerate((1, 3, 5, 7)):
-        send_four[2 * REQ * n : 2 * REQ * (n + 1)] = part(flip).astype(jnp.bfloat16)
-    for n, flip in enumerate((2, 4, 6)):
-        keep_three[2 * REQ * n : 2 * REQ * (n + 1)] = part(flip)
-    columns = pl.ds(pl.multiple_of(z * width, 128), width)
-    block = jnp.concatenate([resid[:, columns], new_resid[:, columns]], axis=0)
-    first[...] = part(0) + jnp.where(x_lo == 0, block.astype(jnp.float32), 0.0)
 
     me = group_index()
     for j in range(REQ):
@@ -219,6 +187,38 @@
         count[target] = k + 1
         target_row = jnp.where(column == i, (me ^ target) * 2 + k, target_row)
     chosen[...] = jnp.where(row == target_row, 1.0, 0.0).astype(jnp.bfloat16)
+    new_copy.wait()
+
+    new_rows = attend(
+        new_query[...],
+        new_own[...],
+        lambda r: new_buf[r],
+        lambda r: new_lengths[r],
+        new_buf.shape[1],
+    )
+
+    pltpu.make_async_copy(cache, kv_buf, kv_sem).wait()
+    rows = attend(
+        query[...],
+        own[...],
+        lambda r: kv_buf[4 * r : 4 * r + 4].reshape(4 * kv_buf.shape[1], 2 * HD),
+        lambda r: lengths[r],
+        4 * kv_buf.shape[1],
+    )
+    attended = jnp.concatenate([rows, new_rows], axis=0)
+    weight_copy.wait()
+
+    def part(flip):
+        columns = pl.ds(pl.multiple_of((z ^ flip) * width, 128), width)
+        return jnp.dot(attended, weight[:, columns], preferred_element_type=jnp.float32)
+
+    for n, flip in enumerate((1, 3, 5, 7)):
+        send_four[2 * REQ * n : 2 * REQ * (n + 1)] = part(flip).astype(jnp.bfloat16)
+    for n, flip in enumerate((2, 4, 6)):
+        keep_three[2 * REQ * n : 2 * REQ * (n + 1)] = part(flip)
+    columns = pl.ds(pl.multiple_of(z * width, 128), width)
+    block = jnp.concatenate([resid[:, columns], new_resid[:, columns]], axis=0)
+    first[...] = part(0) + jnp.where(x_lo == 0, block.astype(jnp.float32), 0.0)
 
 
 def front(*args):

time: 86.7 us -> 86.7 us (level)
  no operation moved by 1% of the time
where the time goes in v7:
time: 86.7 us; the launch traced here: 86.4 us
  starting transfers between devices  45.5 us (52%)
  waiting for transfers between devices  23.8 us (27%)
  Pallas kernels  15.7 us (18%)
  between operations  1 us (1%)
    ppermute x9, starting transfers between devices, over_tp(): return lax.ppermute(array, 'tp', [(t, t ^ flip) for t in range(ranks)])  19 us
    all_to_all x2, starting transfers between devices, deliver(): return lax.all_to_all(array, both, split_axis=0, concat_axis=0, tiled=True)  17.8 us
    ppermute x9, waiting for transfers between devices, over_tp(): return lax.ppermute(array, 'tp', [(t, t ^ flip) for t in range(ranks)])  15 us
    ppermute x5, starting transfers between devices, over_groups(): return lax.ppermute(array, both, [(s, s ^ flip) for s in range(groups)])  6.05 us
    pallas_call x1, Pallas kernels, front(): pl.pallas_call(front_kernel, out_shape=[jax.ShapeDtypeStruct((2 * REQ, wi...  5.11 us
    pallas_call x2, Pallas kernels, pack(): pl.pallas_call(functools.partial(pack_kernel, pieces), out_shape=jax.Shap...  4.85 us
    pallas_call x2, Pallas kernels, place(): pl.pallas_call(functools.partial(place_kernel, pieces_of(late, shape[2]))...  4.41 us
    ppermute x1, waiting for transfers between devices, body(): far_there = lax.ppermute(far, ('pool', 'tp'), across)  4.03 us
  transfers between devices with their start and end apart: 17, of which 11 were waited for; matrix products, arithmetic and copies ran while one was open for 0% of the time, Pallas kernels for 14%

profile of v7, /device:TPU:1, one launch (start us, length us, event | category | flops | bytes accessed | tf_op | source)
XLA Modules:
  0.0 86.4 jit_solution(2705029327374651587)
XLA Ops:
  0.6 2.5 %pack.3 = bf16[16,288,256]{2,1,0:T(8,128)(2,1)} custom-call(s32[16]{0:T(128)} %bitcast.33, s32[16]{0:T(128)} %bitcast.36, bf16[16,256]{1,0:T(8,128)(2,1)} %bitcast.27, bf16[16,256,256]{2,1,0:T(8,128)(2,1)} %bitcast.41), custom_call_target="tpu_custom_call" | custom-call | bytes 3600000 | tf_op jit(solution)/shard_map/pack/pallas_call | solution.py:131
  3.2 0.0 copy-start
  3.2 0.0 copy-start.1
  3.2 0.0 copy-start.2
  3.2 0.0 copy-start.3
  3.2 0.0 copy-start.4
  3.2 0.0 copy-start.5
  3.3 0.0 copy-start.6
  3.3 0.0 copy-start.7
  3.3 0.0 copy-start.8
  3.3 0.0 copy-start.9
  3.3 8.6 %all-to-all-start.1 = ((bf16[16,288,256]{2,1,0:T(8,128)(2,1)}), bf16[16,288,256]{2,1,0:T(8,128)(2,1)}, u32[]{:S(2)}, u32[]{:S(2)}) async-start(bf16[16,288,256]{2,1,0:T(8,128)(2,1)} %pack.3), calls=%async_computation.1 | async-start | bytes 4718592 | tf_op jit(solution)/shard_map/all_to_all | solution.py:363
  11.9 0.0 copy-done
  11.9 0.0 copy-done.1
  11.9 0.0 copy-done.2
  11.9 0.0 copy-done.3
  11.9 0.0 copy-done.4
  11.9 0.0 copy-done.5
  11.9 0.0 copy-done.6
  12.0 0.0 copy-done.7
  12.0 0.0 copy-done.8
  12.0 0.0 copy-done.9
  12.0 5.1 %front.1 = (f32[32,640]{1,0:T(8,128)S(1)}, f32[96,640]{1,0:T(8,128)S(1)}, bf16[128,640]{1,0:T(8,128)(2,1)S(1)}, bf16[32,16]{1,0:T(8,128)(2,1)S(1)}) custom-call(s32[16]{0:T(128)S(1)} %bitcast.35, s32[16]{0:T(128)S(1)} %bitcast.39, s32[64]{0:T(128)S(1)} %bitcast.40, s32[16]{0:T(128)S(1)} %bitcast.38, bf16[16,256]{1,0:T(8,128)(2,1)S(1)} %bitcast.30, ...), custom_call_target="tpu_custom_call" | custom-call | flops 400000000 | bytes 9500000 | tf_op jit(solution)/shard_map/front/pallas_call | solution.py:229
  17.1 0.0 copy-start.10
  17.1 1.7 %collective-permute-start = (bf16[128,640]{1,0:T(8,128)(2,1)S(1)}, bf16[128,640]{1,0:T(8,128)(2,1)S(1)}, u32[]{:S(2)}, u32[]{:S(2)}) collective-permute-start(bf16[128,640]{1,0:T(8,128)(2,1)S(1)} %get-tuple-element.25), channel_id=1, source_target_pairs={{0,2},{1,3},{2,0},{3,1},{4,6},{5,7},{6,4},{7,5},{8,10},{9,11},{10,... | collective-permute-start | bytes 491528 | tf_op jit(solution)/shard_map/ppermute | solution.py:357
  18.8 2.3 %pack.2 = bf16[16,224,256]{2,1,0:T(8,128)(2,1)} custom-call(s32[16]{0:T(128)} %bitcast.34, s32[16]{0:T(128)} %bitcast.37, bf16[16,256]{1,0:T(8,128)(2,1)} %bitcast.28, bf16[16,256,256]{2,1,0:T(8,128)(2,1)} %bitcast.43), custom_call_target="tpu_custom_call" | custom-call | bytes 2800000 | tf_op jit(solution)/shard_map/pack/pallas_call | solution.py:131
  21.1 0.0 copy-done.10
  21.2 2.2 %collective-permute-done.refs_0_ = bf16[128,640]{1,0:T(8,128)(2,1)S(1)} collective-permute-done((bf16[128,640]{1,0:T(8,128)(2,1)S(1)}, bf16[128,640]{1,0:T(8,128)(2,1)S(1)}, u32[]{:S(2)}, u32[]{:S(2)}) %collective-permute-start) | collective-permute-done | bytes 163872 | tf_op jit(solution)/shard_map/ppermute | solution.py:357
  23.4 6.6 %collective-permute-start.3 = (bf16[32,640]{1,0:T(8,128)(2,1)S(1)}, bf16[32,640]{1,0:T(8,128)(2,1)S(1)}, u32[]{:S(2)}, u32[]{:S(2)}) collective-permute-start(bf16[32,640]{1,0:T(8,128)(2,1)S(1)} %get-tuple-element.50), channel_id=1, source_target_pairs={{0,8},{1,9},{2,10},{3,11},{4,12},{5,13},{6,14},{7,15},{8,0},{9,1},... | collective-permute-start | bytes 122888 | tf_op jit(solution)/shard_map/ppermute | solution.py:357
  30.0 0.0 collective-permute-start.2
  30.0 1.2 %collective-permute-start.1 = (bf16[32,640]{1,0:T(8,128)(2,1)S(1)}, bf16[32,640]{1,0:T(8,128)(2,1)S(1)}, u32[]{:S(2)}, u32[]{:S(2)}) collective-permute-start(bf16[32,640]{1,0:T(8,128)(2,1)S(1)} %get-tuple-element.52), channel_id=1, source_target_pairs={{0,4},{1,5},{2,6},{3,7},{4,0},{5,1},{6,2},{7,3},{8,12},{9,13},{10,... | collective-permute-start | bytes 122888 | tf_op jit(solution)/shard_map/ppermute | solution.py:357
  31.2 0.6 collective-permute-done.3.refs_3_
  31.8 3.4 %collective-permute-done.2.refs_2_ = bf16[32,640]{1,0:T(8,128)(2,1)S(1)} collective-permute-done((bf16[32,640]{1,0:T(8,128)(2,1)S(1)}, bf16[32,640]{1,0:T(8,128)(2,1)S(1)}, u32[]{:S(2)}, u32[]{:S(2)}) %collective-permute-start.2) | collective-permute-done | bytes 40992 | tf_op jit(solution)/shard_map/ppermute | solution.py:357
  35.2 0.0 collective-permute-done.1.refs_1_
  35.2 0.1 spread.1
  35.3 2.6 %collective-permute-start.6 = (bf16[16,640]{1,0:T(8,128)(2,1)S(1)}, bf16[16,640]{1,0:T(8,128)(2,1)S(1)}, u32[]{:S(2)}, u32[]{:S(2)}) collective-permute-start(bf16[16,640]{1,0:T(8,128)(2,1)S(1)} %get-tuple-element.32), channel_id=1, source_target_pairs={{0,129},{1,128},{2,131},{3,130},{4,133},{5,132},{6,135},{7,134},{8... | collective-permute-start | bytes 61448 | tf_op jit(solution)/shard_map/ppermute | solution.py:407
  38.0 0.4 collective-permute-start.5
  38.3 0.4 collective-permute-start.4
  38.7 4.0 %collective-permute-done.6 = bf16[16,640]{1,0:T(8,128)(2,1)S(1)} collective-permute-done((bf16[16,640]{1,0:T(8,128)(2,1)S(1)}, bf16[16,640]{1,0:T(8,128)(2,1)S(1)}, u32[]{:S(2)}, u32[]{:S(2)}) %collective-permute-start.6) | collective-permute-done | bytes 20512 | tf_op jit(solution)/shard_map/ppermute | solution.py:407
  42.7 0.0 collective-permute-done.5
  42.7 0.0 collective-permute-done.4
  42.8 2.9 %collective-permute-start.7 = (bf16[8,640]{1,0:T(8,128)(2,1)S(1)}, bf16[8,640]{1,0:T(8,128)(2,1)S(1)}, u32[]{:S(2)}, u32[]{:S(2)}) collective-permute-start(bf16[8,640]{1,0:T(8,128)(2,1)S(1)} %pad_maximum_fusion.2), channel_id=1, source_target_pairs={{0,32},{16,48},{32,0},{48,16},{64,96},{80,112},{96,64},{112,80},{1... | collective-permute-start | bytes 30728 | tf_op jit(solution)/shard_map/ppermute | solution.py:360
  45.7 0.7 collective-permute-start.8
  46.4 1.9 %collective-permute-start.9 = (bf16[8,640]{1,0:T(8,128)(2,1)S(1)}, bf16[8,640]{1,0:T(8,128)(2,1)S(1)}, u32[]{:S(2)}, u32[]{:S(2)}) collective-permute-start(bf16[8,640]{1,0:T(8,128)(2,1)S(1)} %pad_maximum_fusion.4), channel_id=1, source_target_pairs={{0,96},{16,112},{32,64},{48,80},{64,32},{80,48},{96,0},{112,16},{1... | collective-permute-start | bytes 30728 | tf_op jit(solution)/shard_map/ppermute | solution.py:360
  48.3 0.0 collective-permute-done.7
  48.4 1.5 %collective-permute-done.8 = bf16[8,640]{1,0:T(8,128)(2,1)S(1)} collective-permute-done((bf16[8,640]{1,0:T(8,128)(2,1)S(1)}, bf16[8,640]{1,0:T(8,128)(2,1)S(1)}, u32[]{:S(2)}, u32[]{:S(2)}) %collective-permute-start.8) | collective-permute-done | bytes 10272 | tf_op jit(solution)/shard_map/ppermute | solution.py:360
  49.9 0.4 collective-permute-done.9
  50.2 0.0 all-to-all-done.1.part
  50.2 9.3 %all-to-all-start = ((bf16[16,224,256]{2,1,0:T(8,128)(2,1)}), bf16[16,224,256]{2,1,0:T(8,128)(2,1)S(1)}, u32[]{:S(2)}, u32[]{:S(2)}) async-start(bf16[16,224,256]{2,1,0:T(8,128)(2,1)} %pack.2), calls=%async_computation | async-start | bytes 3670016 | tf_op jit(solution)/shard_map/all_to_all | solution.py:363
  59.7 0.2 collective-permute-start.10
  59.9 1.1 %collective-permute-done.10 = bf16[16,640]{1,0:T(8,128)(2,1)S(1)} collective-permute-done((bf16[16,640]{1,0:T(8,128)(2,1)S(1)}, bf16[16,640]{1,0:T(8,128)(2,1)S(1)}, u32[]{:S(2)}, u32[]{:S(2)}) %collective-permute-start.10) | collective-permute-done | bytes 20512 | tf_op jit(solution)/shard_map/ppermute | solution.py:360
  61.0 7.0 %collective-permute-start.13 = (bf16[48,640]{1,0:T(8,128)(2,1)S(1)}, bf16[48,640]{1,0:T(8,128)(2,1)S(1)}, u32[]{:S(2)}, u32[]{:S(2)}) collective-permute-start(bf16[48,640]{1,0:T(8,128)(2,1)S(1)} %pad_maximum_fusion), channel_id=1, source_target_pairs={{0,8},{1,9},{2,10},{3,11},{4,12},{5,13},{6,14},{7,15},{8,0},{9,1},... | collective-permute-start | bytes 184328 | tf_op jit(solution)/shard_map/ppermute | solution.py:357
  68.0 0.0 collective-permute-start.12
  68.0 1.2 %collective-permute-start.11 = (bf16[48,640]{1,0:T(8,128)(2,1)S(1)}, bf16[48,640]{1,0:T(8,128)(2,1)S(1)}, u32[]{:S(2)}, u32[]{:S(2)}) collective-permute-start(bf16[48,640]{1,0:T(8,128)(2,1)S(1)} %pad_maximum_fusion), channel_id=1, source_target_pairs={{0,4},{1,5},{2,6},{3,7},{4,0},{5,1},{6,2},{7,3},{8,12},{9,13},{10,... | collective-permute-start | bytes 184328 | tf_op jit(solution)/shard_map/ppermute | solution.py:357
  69.2 3.1 %place.2.refs_0_ = bf16[16,2,256,256]{3,2,1,0:T(8,128)(2,1)} custom-call(bf16[16,288,256]{2,1,0:T(8,128)(2,1)} %all-to-all-done.1.part), custom_call_target="tpu_custom_call" | custom-call | bytes 4718592 | tf_op jit(solution)/shard_map/place/pallas_call | solution.py:320
  72.3 0.0 collective-permute-done.13
  72.4 1.1 %collective-permute-done.12 = bf16[48,640]{1,0:T(8,128)(2,1)S(1)} collective-permute-done((bf16[48,640]{1,0:T(8,128)(2,1)S(1)}, bf16[48,640]{1,0:T(8,128)(2,1)S(1)}, u32[]{:S(2)}, u32[]{:S(2)}) %collective-permute-start.12) | collective-permute-done | bytes 61472 | tf_op jit(solution)/shard_map/ppermute | solution.py:357
  73.4 1.5 %collective-permute-done.11 = bf16[48,640]{1,0:T(8,128)(2,1)S(1)} collective-permute-done((bf16[48,640]{1,0:T(8,128)(2,1)S(1)}, bf16[48,640]{1,0:T(8,128)(2,1)S(1)}, u32[]{:S(2)}, u32[]{:S(2)}) %collective-permute-start.11) | collective-permute-done | bytes 61472 | tf_op jit(solution)/shard_map/ppermute | solution.py:357
  74.9 0.9 %collective-permute-start.14 = (bf16[192,640]{1,0:T(8,128)(2,1)S(1)}, bf16[192,640]{1,0:T(8,128)(2,1)S(1)}, u32[]{:S(2)}, u32[]{:S(2)}) collective-permute-start(bf16[192,640]{1,0:T(8,128)(2,1)S(1)} %constant_dynamic-update-slice_fusion.4.refs_0_), channel_id=1, source_target_pairs={{0,2},{1,3},{2,0},{3,1},{4,6},{5,7},{6,4},{7,5},{8,10},{9,11},{10,... | collective-permute-start | bytes 737288 | tf_op jit(solution)/shard_map/ppermute | solution.py:357
  75.8 6.2 %collective-permute-done.14.refs_1_ = bf16[192,640]{1,0:T(8,128)(2,1)S(1)} collective-permute-done((bf16[192,640]{1,0:T(8,128)(2,1)S(1)}, bf16[192,640]{1,0:T(8,128)(2,1)S(1)}, u32[]{:S(2)}, u32[]{:S(2)}) %collective-permute-start.14) | collective-permute-done | bytes 245792 | tf_op jit(solution)/shard_map/ppermute | solution.py:357
  82.1 1.2 %finish.1 = (bf16[48,5120]{1,0:T(8,128)(2,1)}, bf16[48,5120]{1,0:T(8,128)(2,1)}) custom-call(bf16[1,5120]{1,0:T(2,128)(2,1)S(1)} %reshape.18.gain, bf16[192,640]{1,0:T(8,128)(2,1)S(1)} %constant_dynamic-update-slice_fusion.4.refs_0_, bf16[192,640]{1,0:T(8,128)(2,1)S(1)} %collective-permute-done.14.refs_1_), custom_call_target="tpu_custom_call" | custom-call | bytes 4000000 | tf_op jit(solution)/shard_map/finish/pallas_call | solution.py:427
  83.3 1.9 %all-to-all-done.part = bf16[16,224,256]{2,1,0:T(8,128)(2,1)S(1)} async-done(((bf16[16,224,256]{2,1,0:T(8,128)(2,1)}), bf16[16,224,256]{2,1,0:T(8,128)(2,1)S(1)}, u32[]{:S(2)}, u32[]{:S(2)}) %all-to-all-start) | async-done | bytes 1835040 | tf_op jit(solution)/shard_map/all_to_all | solution.py:363
  85.1 1.3 %place.3 = bf16[16,2,256,256]{3,2,1,0:T(8,128)(2,1)} custom-call(bf16[16,224,256]{2,1,0:T(8,128)(2,1)S(1)} %all-to-all-done.part, bf16[16,2,256,256]{3,2,1,0:T(8,128)(2,1)} %place.2.refs_0_), custom_call_target="tpu_custom_call", output_to_operand_aliasing={{}: (1, {})} | custom-call | bytes 3670016 | tf_op jit(solution)/shard_map/place/pallas_call | solution.py:320
  (28 shorter events, 0.4 us)
Async XLA Ops:
  3.2 8.7 %copy-start = (bf16[1,1,16,5120]{3,2,1,0:T(8,128)(2,1)S(1)}, bf16[1,1,16,5120]{3,2,1,0:T(8,128)(2,1)}, u32[]{:S(2)}) copy-start(bf16[1,1,16,5120]{3,2,1,0:T(8,128)(2,1)} %param.19) | copy-start | bytes 491524
  3.2 8.7 %copy-start.1 = (bf16[1,1,16,5120]{3,2,1,0:T(8,128)(2,1)S(1)}, bf16[1,1,16,5120]{3,2,1,0:T(8,128)(2,1)}, u32[]{:S(2)}) copy-start(bf16[1,1,16,5120]{3,2,1,0:T(8,128)(2,1)} %param.24) | copy-start | bytes 491524
  3.2 8.7 %copy-start.2 = (bf16[1,1,16,1,256]{4,2,3,1,0:T(8,128)(2,1)S(1)}, bf16[1,1,16,1,256]{4,2,3,1,0:T(8,128)(2,1)}, u32[]{:S(2)}) copy-start(bf16[1,1,16,1,256]{4,2,3,1,0:T(8,128)(2,1)} %param.23) | copy-start | bytes 24580
  3.2 8.7 %copy-start.3 = (bf16[1,1,16,256]{3,2,1,0:T(8,128)(2,1)S(1)}, bf16[1,1,16,256]{3,2,1,0:T(8,128)(2,1)}, u32[]{:S(2)}) copy-start(bf16[1,1,16,256]{3,2,1,0:T(8,128)(2,1)} %param.17) | copy-start | bytes 24580
  3.2 8.7 %copy-start.4 = (bf16[1,1,16,1,256]{4,2,3,1,0:T(8,128)(2,1)S(1)}, bf16[1,1,16,1,256]{4,2,3,1,0:T(8,128)(2,1)}, u32[]{:S(2)}) copy-start(bf16[1,1,16,1,256]{4,2,3,1,0:T(8,128)(2,1)} %param.18) | copy-start | bytes 24580
  3.2 8.7 %copy-start.5 = (bf16[1,1,16,256]{3,2,1,0:T(8,128)(2,1)S(1)}, bf16[1,1,16,256]{3,2,1,0:T(8,128)(2,1)}, u32[]{:S(2)}) copy-start(bf16[1,1,16,256]{3,2,1,0:T(8,128)(2,1)} %param.22) | copy-start | bytes 24580
  3.3 8.7 %copy-start.6 = (s32[1,1,16,1]{2,3,1,0:T(1,128)S(1)}, s32[1,1,16,1]{2,3,1,0:T(1,128)}, u32[]{:S(2)}) copy-start(s32[1,1,16,1]{2,3,1,0:T(1,128)} %param.25) | copy-start | bytes 196
  3.3 8.7 %copy-start.7 = (s32[1,1,16]{2,1,0:T(1,128)S(1)}, s32[1,1,16]{2,1,0:T(1,128)}, u32[]{:S(2)}) copy-start(s32[1,1,16]{2,1,0:T(1,128)} %param.21) | copy-start | bytes 196
  3.3 8.7 %copy-start.8 = (s32[1,1,16]{2,1,0:T(1,128)S(1)}, s32[1,1,16]{2,1,0:T(1,128)}, u32[]{:S(2)}) copy-start(s32[1,1,16]{2,1,0:T(1,128)} %param.16) | copy-start | bytes 196
  3.3 8.7 %copy-start.9 = (s32[1,1,64]{2,1,0:T(1,128)S(1)}, s32[1,1,64]{2,1,0:T(1,128)}, u32[]{:S(2)}) copy-start(s32[1,1,64]{2,1,0:T(1,128)} %param.15) | copy-start | bytes 772
  3.3 46.9 %all-to-all-start.1 = ((bf16[16,288,256]{2,1,0:T(8,128)(2,1)}), bf16[16,288,256]{2,1,0:T(8,128)(2,1)}, u32[]{:S(2)}, u32[]{:S(2)}) async-start(bf16[16,288,256]{2,1,0:T(8,128)(2,1)} %pack.3), calls=%async_computation.1 | async-start | bytes 4718592 | tf_op jit(solution)/shard_map/all_to_all | solution.py:363
  17.1 4.0 %copy-start.10 = (bf16[5120]{0:T(1024)(128)(2,1)S(1)}, bf16[5120]{0:T(1024)(128)(2,1)}, u32[]{:S(2)}) copy-start(bf16[5120]{0:T(1024)(128)(2,1)} %param.27) | copy-start | bytes 30724
  17.1 6.2 %collective-permute-start = (bf16[128,640]{1,0:T(8,128)(2,1)S(1)}, bf16[128,640]{1,0:T(8,128)(2,1)S(1)}, u32[]{:S(2)}, u32[]{:S(2)}) collective-permute-start(bf16[128,640]{1,0:T(8,128)(2,1)S(1)} %get-tuple-element.25), channel_id=1, source_target_pairs={{0,2},{1,3},{2,0},{3,1},{4,6},{5,7},{6,4},{7,5},{8,10},{9,11},{10,... | collective-permute-start | bytes 491528 | tf_op jit(solution)/shard_map/ppermute | solution.py:357
  23.4 8.4 %collective-permute-start.3 = (bf16[32,640]{1,0:T(8,128)(2,1)S(1)}, bf16[32,640]{1,0:T(8,128)(2,1)S(1)}, u32[]{:S(2)}, u32[]{:S(2)}) collective-permute-start(bf16[32,640]{1,0:T(8,128)(2,1)S(1)} %get-tuple-element.50), channel_id=1, source_target_pairs={{0,8},{1,9},{2,10},{3,11},{4,12},{5,13},{6,14},{7,15},{8,0},{9,1},... | collective-permute-start | bytes 122888 | tf_op jit(solution)/shard_map/ppermute | solution.py:357
  30.0 5.2 %collective-permute-start.2 = (bf16[32,640]{1,0:T(8,128)(2,1)S(1)}, bf16[32,640]{1,0:T(8,128)(2,1)S(1)}, u32[]{:S(2)}, u32[]{:S(2)}) collective-permute-start(bf16[32,640]{1,0:T(8,128)(2,1)S(1)} %get-tuple-element.51), channel_id=1, source_target_pairs={{0,12},{1,13},{2,14},{3,15},{4,8},{5,9},{6,10},{7,11},{8,4},{9,5},... | collective-permute-start | bytes 122888 | tf_op jit(solution)/shard_map/ppermute | solution.py:357
  30.0 5.2 %collective-permute-start.1 = (bf16[32,640]{1,0:T(8,128)(2,1)S(1)}, bf16[32,640]{1,0:T(8,128)(2,1)S(1)}, u32[]{:S(2)}, u32[]{:S(2)}) collective-permute-start(bf16[32,640]{1,0:T(8,128)(2,1)S(1)} %get-tuple-element.52), channel_id=1, source_target_pairs={{0,4},{1,5},{2,6},{3,7},{4,0},{5,1},{6,2},{7,3},{8,12},{9,13},{10,... | collective-permute-start | bytes 122888 | tf_op jit(solution)/shard_map/ppermute | solution.py:357
  35.3 7.4 %collective-permute-start.6 = (bf16[16,640]{1,0:T(8,128)(2,1)S(1)}, bf16[16,640]{1,0:T(8,128)(2,1)S(1)}, u32[]{:S(2)}, u32[]{:S(2)}) collective-permute-start(bf16[16,640]{1,0:T(8,128)(2,1)S(1)} %get-tuple-element.32), channel_id=1, source_target_pairs={{0,129},{1,128},{2,131},{3,130},{4,133},{5,132},{6,135},{7,134},{8... | collective-permute-start | bytes 61448 | tf_op jit(solution)/shard_map/ppermute | solution.py:407
  38.0 4.8 %collective-permute-start.5 = (bf16[16,640]{1,0:T(8,128)(2,1)S(1)}, bf16[16,640]{1,0:T(8,128)(2,1)S(1)}, u32[]{:S(2)}, u32[]{:S(2)}) collective-permute-start(bf16[16,640]{1,0:T(8,128)(2,1)S(1)} %get-tuple-element.32), channel_id=1, source_target_pairs={{0,128},{16,144},{32,160},{48,176},{64,192},{80,208},{96,224},{112... | collective-permute-start | bytes 61448 | tf_op jit(solution)/shard_map/ppermute | solution.py:360
  38.3 4.4 %collective-permute-start.4 = (bf16[32,640]{1,0:T(8,128)(2,1)S(1)}, bf16[32,640]{1,0:T(8,128)(2,1)S(1)}, u32[]{:S(2)}, u32[]{:S(2)}) collective-permute-start(bf16[32,640]{1,0:T(8,128)(2,1)S(1)} %get-tuple-element.31), channel_id=1, source_target_pairs={{0,1},{1,0},{2,3},{3,2},{4,5},{5,4},{6,7},{7,6},{8,9},{9,8},{10,11... | collective-permute-start | bytes 122888 | tf_op jit(solution)/shard_map/ppermute | solution.py:357
  42.8 5.5 %collective-permute-start.7 = (bf16[8,640]{1,0:T(8,128)(2,1)S(1)}, bf16[8,640]{1,0:T(8,128)(2,1)S(1)}, u32[]{:S(2)}, u32[]{:S(2)}) collective-permute-start(bf16[8,640]{1,0:T(8,128)(2,1)S(1)} %pad_maximum_fusion.2), channel_id=1, source_target_pairs={{0,32},{16,48},{32,0},{48,16},{64,96},{80,112},{96,64},{112,80},{1... | collective-permute-start | bytes 30728 | tf_op jit(solution)/shard_map/ppermute | solution.py:360
  45.7 4.1 %collective-permute-start.8 = (bf16[8,640]{1,0:T(8,128)(2,1)S(1)}, bf16[8,640]{1,0:T(8,128)(2,1)S(1)}, u32[]{:S(2)}, u32[]{:S(2)}) collective-permute-start(bf16[8,640]{1,0:T(8,128)(2,1)S(1)} %pad_maximum_fusion.3), channel_id=1, source_target_pairs={{0,64},{16,80},{32,96},{48,112},{64,0},{80,16},{96,32},{112,48},{1... | collective-permute-start | bytes 30728 | tf_op jit(solution)/shard_map/ppermute | solution.py:360
  46.4 3.8 %collective-permute-start.9 = (bf16[8,640]{1,0:T(8,128)(2,1)S(1)}, bf16[8,640]{1,0:T(8,128)(2,1)S(1)}, u32[]{:S(2)}, u32[]{:S(2)}) collective-permute-start(bf16[8,640]{1,0:T(8,128)(2,1)S(1)} %pad_maximum_fusion.4), channel_id=1, source_target_pairs={{0,96},{16,112},{32,64},{48,80},{64,32},{80,48},{96,0},{112,16},{1... | collective-permute-start | bytes 30728 | tf_op jit(solution)/shard_map/ppermute | solution.py:360
  50.2 34.9 %all-to-all-start = ((bf16[16,224,256]{2,1,0:T(8,128)(2,1)}), bf16[16,224,256]{2,1,0:T(8,128)(2,1)S(1)}, u32[]{:S(2)}, u32[]{:S(2)}) async-start(bf16[16,224,256]{2,1,0:T(8,128)(2,1)} %pack.2), calls=%async_computation | async-start | bytes 3670016 | tf_op jit(solution)/shard_map/all_to_all | solution.py:363
  59.7 1.3 %collective-permute-start.10 = (bf16[16,640]{1,0:T(8,128)(2,1)S(1)}, bf16[16,640]{1,0:T(8,128)(2,1)S(1)}, u32[]{:S(2)}, u32[]{:S(2)}) collective-permute-start(bf16[16,640]{1,0:T(8,128)(2,1)S(1)} %reshape_squeeze.7), channel_id=1, source_target_pairs={{0,16},{16,0},{32,48},{48,32},{64,80},{80,64},{96,112},{112,96},{1... | collective-permute-start | bytes 61448 | tf_op jit(solution)/shard_map/ppermute | solution.py:360
  61.0 11.3 %collective-permute-start.13 = (bf16[48,640]{1,0:T(8,128)(2,1)S(1)}, bf16[48,640]{1,0:T(8,128)(2,1)S(1)}, u32[]{:S(2)}, u32[]{:S(2)}) collective-permute-start(bf16[48,640]{1,0:T(8,128)(2,1)S(1)} %pad_maximum_fusion), channel_id=1, source_target_pairs={{0,8},{1,9},{2,10},{3,11},{4,12},{5,13},{6,14},{7,15},{8,0},{9,1},... | collective-permute-start | bytes 184328 | tf_op jit(solution)/shard_map/ppermute | solution.py:357
  68.0 5.5 %collective-permute-start.12 = (bf16[48,640]{1,0:T(8,128)(2,1)S(1)}, bf16[48,640]{1,0:T(8,128)(2,1)S(1)}, u32[]{:S(2)}, u32[]{:S(2)}) collective-permute-start(bf16[48,640]{1,0:T(8,128)(2,1)S(1)} %pad_maximum_fusion), channel_id=1, source_target_pairs={{0,12},{1,13},{2,14},{3,15},{4,8},{5,9},{6,10},{7,11},{8,4},{9,5},... | collective-permute-start | bytes 184328 | tf_op jit(solution)/shard_map/ppermute | solution.py:357
  68.0 6.9 %collective-permute-start.11 = (bf16[48,640]{1,0:T(8,128)(2,1)S(1)}, bf16[48,640]{1,0:T(8,128)(2,1)S(1)}, u32[]{:S(2)}, u32[]{:S(2)}) collective-permute-start(bf16[48,640]{1,0:T(8,128)(2,1)S(1)} %pad_maximum_fusion), channel_id=1, source_target_pairs={{0,4},{1,5},{2,6},{3,7},{4,0},{5,1},{6,2},{7,3},{8,12},{9,13},{10,... | collective-permute-start | bytes 184328 | tf_op jit(solution)/shard_map/ppermute | solution.py:357
  74.9 7.1 %collective-permute-start.14 = (bf16[192,640]{1,0:T(8,128)(2,1)S(1)}, bf16[192,640]{1,0:T(8,128)(2,1)S(1)}, u32[]{:S(2)}, u32[]{:S(2)}) collective-permute-start(bf16[192,640]{1,0:T(8,128)(2,1)S(1)} %constant_dynamic-update-slice_fusion.4.refs_0_), channel_id=1, source_target_pairs={{0,2},{1,3},{2,0},{3,1},{4,6},{5,7},{6,4},{7,5},{8,10},{9,11},{10,... | collective-permute-start | bytes 737288 | tf_op jit(solution)/shard_map/ppermute | solution.py:357
